TPU v7x, 32 devices: a whole 2x2x4 slice. The times are simulated.
32 devices in a mesh: stn: 8 (over z, core), seg: 4 (over y, x).
Axes of the slice: x: 2, y: 2, z: 4, core: 2. Of those that a mesh axis runs over, the one named last changes fastest.
Arguments:
- voltages: bfloat16 [128, 32, 8192], P('stn', None, 'seg'), may hold values from -91 to 91
- filter_taps: float32 [8, 32], replicated, may hold values from -0.375 to 0.375
- positions: float32 [2, 128], replicated, may hold values from -8 to 8
- beam_dirs: int32 [128], replicated, may hold values from 0 to 359
- chan_table: int32 [16], replicated, may hold values from 0 to 15, each once
Outputs:
- beam_out: bfloat16 [16, 2, 128, 8192], P('stn', None, None, 'seg')
All inputs are finite; a program needn't handle non-finite values.
Results may differ from a plain program's by a relative error of at most 0.0078.
Values may be sent and summed in bfloat16 or wider, within the bound.
No kernel may reach another device: no remote copies, remote signals or barrier semaphores. Data moves between devices by JAX's collectives and lax.ppermute only.
A program may use at most 64 MiB of HBM per device.

v0:
```python
import math

import jax
import jax.numpy as jnp
from jax import lax
from jax.sharding import PartitionSpec as P

C = 16
TAPS = 8
B = 128
DIRS = 360


loading_level = 0.1
full_turn = 2.0 * math.pi


def passed_along(value, axis, by):
    length = lax.axis_size(axis)
    pairs = [(i, i + by) for i in range(length) if 0 <= i + by < length]
    return lax.ppermute(value, axis, pairs)


def dft_tables(chan_table):
    frame_width = 2 * C
    phase_index = jnp.remainder(
        chan_table[:, None] * jnp.arange(frame_width, dtype=jnp.int32)[None, :], frame_width
    )
    angles = phase_index.astype(jnp.float32) * (full_turn / frame_width)
    return jnp.stack([jnp.cos(angles), -jnp.sin(angles)], axis=1)


def filter_block(station_block, filter_taps):
    snap_count = station_block.shape[2] - (TAPS - 1)
    widened = station_block.astype(jnp.float32)
    summed = jnp.zeros((station_block.shape[0], station_block.shape[1], snap_count), jnp.float32)
    for tap_index in range(TAPS):
        offset = TAPS - 1 - tap_index
        summed = (
            summed
            + filter_taps[tap_index][None, :, None] * widened[:, :, offset : offset + snap_count]
        )
    return summed


def channelize(filtered, dft_table):
    return jnp.einsum("jap,spt->jast", dft_table, filtered, precision=lax.Precision.HIGHEST).astype(
        jnp.bfloat16
    )


def halves(gram_full):
    half_size = gram_full.shape[-1] // 2
    sym_part = gram_full[..., :half_size, :half_size] + gram_full[..., half_size:, half_size:]
    skew_part = gram_full[..., half_size:, :half_size] - gram_full[..., :half_size, half_size:]
    return (sym_part, skew_part)


def assemble(sym_part, skew_part):
    upper_rows = jnp.concatenate([sym_part, -skew_part], axis=-1)
    bottom = jnp.concatenate([skew_part, sym_part], axis=-1)
    return jnp.concatenate([upper_rows, bottom], axis=-2)


def steering(positions, beam_dirs, channel):
    bearing = beam_dirs.astype(jnp.float32) * (full_turn / DIRS)
    frequency = 1.0 + channel.astype(jnp.float32) / C
    path_delay = (
        positions[0][:, None] * jnp.cos(bearing)[None, :]
        + positions[1][:, None] * jnp.sin(bearing)[None, :]
    )
    phases = full_turn * frequency * path_delay
    return jnp.concatenate([jnp.cos(phases), jnp.sin(phases)], axis=0)


def solve_weights(factor, steer):
    whitened = jax.scipy.linalg.solve_triangular(factor, steer, lower=True)
    column_power = jnp.sum(whitened * whitened, axis=0)
    solved = jax.scipy.linalg.solve_triangular(factor, whitened, lower=True, trans=1)
    return (solved / jnp.sqrt(column_power)[None, :]).astype(jnp.bfloat16)


def mixing(weights):
    half_size = weights.shape[0] // 2
    swapped = jnp.concatenate([-weights[half_size:], weights[:half_size]], axis=0)
    return jnp.concatenate([weights.T, swapped.T], axis=0)


def solve_slots(factor, positions, slot_dirs, channels):
    return jax.vmap(
        lambda one_factor, channel: solve_weights(
            one_factor, steering(positions, slot_dirs, channel)
        )
    )(factor, channels)


def on_device(voltages, filter_taps, positions, beam_dirs, chan_table):
    last_frames = voltages[:, :, voltages.shape[2] - (TAPS - 1) :]
    earlier = passed_along(last_frames, "seg", 1)
    extended = jnp.concatenate([earlier, voltages], axis=2)
    filtered = filter_block(extended, filter_taps)
    spectra = channelize(filtered, dft_tables(chan_table))
    turned = lax.all_to_all(spectra, "stn", split_axis=0, concat_axis=2, tiled=True)
    slot_count = turned.shape[0]
    snap_count = turned.shape[3]
    stacked = turned.reshape(slot_count, 2 * turned.shape[2], snap_count)
    gram_full = jnp.einsum("cat,cbt->cab", stacked, stacked, preferred_element_type=jnp.float32)
    sym_part, skew_part = halves(gram_full)
    segments = lax.axis_size("seg")
    snap_total = snap_count * segments
    identity = jnp.eye(stacked.shape[1], dtype=jnp.float32)
    sym_part, skew_part = lax.psum((sym_part, skew_part), "seg")
    covariance = assemble(sym_part, skew_part) / snap_total + loading_level * identity
    factor = jnp.linalg.cholesky(covariance)
    channels = lax.dynamic_slice_in_dim(chan_table, lax.axis_index("stn") * slot_count, slot_count)
    weights = solve_slots(factor, positions, beam_dirs, channels)
    mix_matrix = jax.vmap(mixing)(weights)
    beam_out = jnp.einsum("cbk,ckt->cbt", mix_matrix, stacked, preferred_element_type=jnp.float32)
    return beam_out.astype(jnp.bfloat16).reshape(slot_count, 2, B, snap_count)


def solution(mesh):
    return jax.shard_map(
        on_device,
        mesh=mesh,
        in_specs=(P("stn", None, "seg"), P(), P(), P(), P()),
        out_specs=P("stn", None, None, "seg"),
        check_vma=False,
    )
```

profile of v0, /device:TPU:11, one launch (start us, length us, event | category | flops | bytes accessed | tf_op | source)
XLA Modules:
  0.0 261.6 jit_solution(1455489493558060995)
XLA Ops:
  6.5 1.0 slice.138
  7.5 3.1 %collective-permute-start = (bf16[16,32,7]{2,1,0:T(8,128)(2,1)S(1)}, bf16[16,32,7]{2,1,0:T(8,128)(2,1)S(1)}, u32[]{:S(2)}, u32[]{:S(2)}) collective-permute-start(bf16[16,32,7]{2,1,0:T(8,128)(2,1)S(1)} %slice.138), channel_id=1, source_target_pairs={{0,1},{1,2},{2,3},{4,5},{5,6},{6,7},{8,9},{9,10},{10,11},{12,13},{... | collective-permute-start | bytes 21512 | tf_op jit(solution)/shard_map/ppermute | solution.py:21
  10.7 0.8 fusion.54
  11.5 1.0 slice_bitcast_fusion.15
  12.4 1.4 collective-permute-done
  13.8 2.8 %maximum_convert_fusion = f32[16,32,2055]{2,1,0:T(8,128)S(1)} fusion(bf16[16,32,2048]{2,1,0:T(8,128)(2,1)} %param.5, bf16[16,32,7]{2,1,0:T(8,128)(2,1)S(1)} %collective-permute-done), kind=kLoop, calls=%fused_computation.21 | loop fusion | flops 4208640 | bytes 6312960 | tf_op jit(solution)/shard_map/convert_element_type | solution.py:35
  16.7 11.6 %fusion.16 = bf16[16,2,16,2048]{3,0,2,1:T(8,128)(2,1)S(1)} fusion(f32[16,32,2055]{2,1,0:T(8,128)S(1)} %maximum_convert_fusion, f32[32]{0:T(128)S(1)} %get-tuple-element.38, f32[32]{0:T(128)S(1)} %get-tuple-element.39, f32[32]{0:T(128)S(1)} %get-tuple-element.33, f32[32]{0:T(128)S(1)} %get-tuple-element.34, f32[32]{0:T(128)S(1)} %get-tuple-element.35, ...), kind=kOutput, calls=%fused_computation.19 | convolution fusion | flops 419431424 | bytes 35672064 | tf_op jit(solution)/shard_map/jap,spt->jast/dot_general | solution.py:47
  28.2 0.0 copy-start.4
  28.3 0.0 copy-start.2
  28.3 2.5 copy.31
  30.7 6.5 %all-to-all-start = ((bf16[16,2,16,2048]{3,2,1,0:T(8,128)(2,1)}), bf16[16,2,16,2048]{3,2,1,0:T(8,128)(2,1)S(1)}, u32[]{:S(2)}, u32[]{:S(2)}) async-start(bf16[16,2,16,2048]{3,2,1,0:T(8,128)(2,1)} %copy.31), calls=%async_computation | async-start | bytes 4194304 | tf_op jit(solution)/shard_map/all_to_all | solution.py:103
  37.4 45.3 %all-to-all-done = bf16[16,2,16,2048]{3,2,1,0:T(8,128)(2,1)S(1)} async-done(((bf16[16,2,16,2048]{3,2,1,0:T(8,128)(2,1)}), bf16[16,2,16,2048]{3,2,1,0:T(8,128)(2,1)S(1)}, u32[]{:S(2)}, u32[]{:S(2)}) %all-to-all-start) | async-done | bytes 2097184 | tf_op jit(solution)/shard_map/all_to_all | solution.py:103
  82.8 1.3 copy-done
  84.1 1.7 copy.32
  85.8 0.7 fusion.60
  86.6 0.7 slice_subtract_fusion
  87.3 0.0 all-reduce.4.cloned.1.call-update
  87.3 0.1 add_multiply_fusion
  87.4 0.1 multiply_add_fusion
  87.5 44.1 %all-reduce.4.cloned.1.call-done = (f32[2,128,128]{1,2,0:T(8,128)}, f32[2,128,128]{1,2,0:T(8,128)}) async-done(((f32[2,128,128]{1,2,0:T(8,128)}, f32[2,128,128]{1,2,0:T(8,128)}), (f32[2,128,128]{1,2,0:T(8,128)}, f32[2,128,128]{1,2,0:T(8,128)})) %all-reduce.4.cloned.1.call-update) | async-done | bytes 262160 | tf_op jit(solution)/shard_map/psum | solution.py:112
  131.6 0.9 neg.17
  132.6 1.1 fusion.27
  133.7 0.2 copy.37
  133.9 0.1 fusion.28
  133.9 0.0 copy-start.1
  133.9 0.8 copy-done.1
  134.7 23.5 %custom-call.20 = f32[2,128,128]{2,1,0:T(8,128)S(1)} custom-call(f32[2,128,128]{2,1,0:T(8,128)S(1)} %cholesky.122), custom_call_target="Cholesky" | custom-call | tf_op jit(solution)/shard_map/jit(cholesky)/cholesky | solution.py:114
  158.3 19.7 %custom-call.21 = f32[2,1,128,128]{2,3,1,0:T(8,128)S(1)} custom-call(f32[2,1,128,128]{3,2,1,0:T(8,128)S(1)} %select_bitcast_fusion), custom_call_target="InvertDiagBlocksLowerTriangular" | custom-call | tf_op jit(solution)/shard_map/jit(cholesky)/cholesky | solution.py:114
  178.0 1.2 constant_dynamic-update-slice_fusion.1
  179.1 1.3 convolution_subtract_fusion.2
  180.4 23.5 %custom-call.22 = f32[2,128,128]{2,1,0:T(8,128)S(1)} custom-call(f32[2,128,128]{2,1,0:T(8,128)S(1)} %convolution_subtract_fusion.2), custom_call_target="Cholesky" | custom-call | tf_op jit(solution)/shard_map/jit(cholesky)/cholesky | solution.py:114
  203.9 0.2 compare_reduce_fusion
  204.1 0.1 select_select_fusion
  204.3 0.1 triangular_solve.72
  204.3 5.3 %while.1 = (s32[]{:T(128)}, f32[2,256,256]{2,1,0:T(8,128)S(1)}, s32[2,2]{1,0:T(2,128)S(1)}, f32[2,2,128,128]{3,2,0,1:T(8,128)}, s32[]{:T(128)}) while((s32[]{:T(128)}, f32[2,256,256]{2,1,0:T(8,128)S(1)}, s32[2,2]{1,0:T(2,128)S(1)}, f32[2,2,128,128]{3,2,0,1:T(8,128)}, s32[]{:T(128)}) %tuple.35), condition=%wide.while_cond, body=%wide.while_body.sunk | while | flops 2 | bytes 263777 | solution.py:79
  204.3 0.6 fusion.72
  204.9 2.0 bitcast_dynamic-update-slice_fusion.2
  207.0 0.6 fusion.72
  207.6 2.1 bitcast_dynamic-update-slice_fusion.2
  209.6 40.1 %custom-call.23 = f32[2,2,128,128]{2,3,1,0:T(8,128)S(1)} custom-call(f32[2,2,128,128]{3,2,1,0:T(8,128)} %bitcast.86), custom_call_target="InvertDiagBlocksLowerTriangular" | custom-call | tf_op jit(solution)/shard_map/vmap(jit(_solve_triangular))/triangular_solve | solution.py:79
  249.8 0.8 fusion.35
  250.6 0.6 convolution_subtract_fusion.1
  251.1 0.4 fusion.41
  251.5 0.1 fusion.30
  251.6 0.3 fusion.40
  251.9 0.4 convolution_subtract_fusion
  252.3 0.3 fusion.39
  252.6 2.1 convolution_convert_fusion
  (25 shorter events, 0.3 us)
Async XLA Ops:
  7.5 6.3 %collective-permute-start = (bf16[16,32,7]{2,1,0:T(8,128)(2,1)S(1)}, bf16[16,32,7]{2,1,0:T(8,128)(2,1)S(1)}, u32[]{:S(2)}, u32[]{:S(2)}) collective-permute-start(bf16[16,32,7]{2,1,0:T(8,128)(2,1)S(1)} %slice.138), channel_id=1, source_target_pairs={{0,1},{1,2},{2,3},{4,5},{5,6},{6,7},{8,9},{9,10},{10,11},{12,13},{... | collective-permute-start | bytes 21512 | tf_op jit(solution)/shard_map/ppermute | solution.py:21
  28.2 9.1 %copy-start.4 = (s32[128]{0:T(128)S(1)}, s32[128]{0:T(128)}, u32[]{:S(2)}) copy-start(s32[128]{0:T(128)} %param.8) | copy-start | bytes 1540
  28.3 9.1 %copy-start.2 = (f32[2,128]{1,0:T(2,128)S(1)}, f32[2,128]{1,0:T(2,128)}, u32[]{:S(2)}) copy-start(f32[2,128]{1,0:T(2,128)} %param.7) | copy-start | bytes 3076
  30.7 52.0 %all-to-all-start = ((bf16[16,2,16,2048]{3,2,1,0:T(8,128)(2,1)}), bf16[16,2,16,2048]{3,2,1,0:T(8,128)(2,1)S(1)}, u32[]{:S(2)}, u32[]{:S(2)}) async-start(bf16[16,2,16,2048]{3,2,1,0:T(8,128)(2,1)} %copy.31), calls=%async_computation | async-start | bytes 4194304 | tf_op jit(solution)/shard_map/all_to_all | solution.py:103
  37.2 94.4 %all-reduce.4.cloned.1.call-start = ((), (), s32[]{:S(2)}) async-start(), calls=%async_computation.1 | async-start | bytes 524288 | tf_op jit(solution)/shard_map/psum | solution.py:112
  82.8 1.3 copy-start
  84.1 3.2 %copy-start.3 = (s32[16]{0:T(128)S(1)}, s32[16]{0:T(128)}, u32[]{:S(2)}) copy-start(s32[16]{0:T(128)} %param.9) | copy-start | bytes 196
  133.9 0.8 copy-start.1
Sparse Core Ops, SparseCore 0:
  87.4 44.1 all-reduce.3
where the time goes:
time: 264 us; the launch traced here: 262 us
  other arithmetic  114 us (43%)
  waiting for transfers between devices  90.8 us (34%)
  matrix products  19.6 us (7%)
  local copies, waits for them, and re-layouts  13.9 us (5%)
  between operations  13.7 us (5%)
  starting transfers between devices  9.62 us (4%)
    another operation x9, other arithmetic, on_device(): factor = jnp.linalg.cholesky(covariance)  66.8 us
    all_to_all x1, waiting for transfers between devices, on_device(): lax.all_to_all(spectra, 'stn', split_axis=0, concat_axis=2, tiled=True)  45.3 us
    psum x1, waiting for transfers between devices, on_device(): sym_part, skew_part = lax.psum((sym_part, skew_part), 'seg')  44.1 us
    another operation x4, other arithmetic, solve_weights(): jax.scipy.linalg.solve_triangular(factor, whitened, lower=True, trans=1)  40.3 us
    dot_general x1, matrix products, channelize(): jnp.einsum('jap,spt->jast', dft_table, filtered, precision=lax.Precision....  11.6 us
    all_to_all x1, starting transfers between devices, on_device(): lax.all_to_all(spectra, 'stn', split_axis=0, concat_axis=2, tiled=True)  6.5 us
    another operation x6, local copies, waits for them, and re-layouts  5.28 us
  transfers between devices with their start and end apart: 3, of which 3 were waited for; matrix products, arithmetic and copies ran while one was open for 1% of the time, Pallas kernels for 0%

commit v1 on v0

v1 whole, which is shorter than its diff:
```python
import functools
import math

import jax
import jax.numpy as jnp
import numpy as np
from jax import lax
from jax.experimental import pallas as pl
from jax.experimental.pallas import tpu as pltpu
from jax.sharding import PartitionSpec as P

DIRS = 360
LANES = 128
GROUP = 8
PIVOTS = 16

loading_level = 0.1
full_turn = 2.0 * math.pi
NT = (((1,), (1,)), ((), ()))
TN = (((0,), (0,)), ((), ()))
f32, bf16 = jnp.float32, jnp.bfloat16


def split_in_two(value):
    high = value.astype(bf16)
    return high, (value - high.astype(f32)).astype(bf16)


def block_tables(channels):
    width = 2 * channels
    phase = (np.arange(channels)[:, None] * np.arange(width)[None, :]) % width
    angles = phase * (full_turn / width)
    parts = np.stack([np.cos(angles), -np.sin(angles)], axis=1).astype(np.float32)
    blocks = np.einsum("kap,st->kastp", parts, np.eye(GROUP, dtype=np.float32))
    blocks = blocks.reshape(channels, 2 * GROUP, GROUP * width)
    high = blocks.astype(bf16)
    return high, (blocks - high.astype(np.float32)).astype(bf16)


def merged_rows(pieces):
    if all(piece.shape[0] % 16 == 0 for piece in pieces):
        return jnp.concatenate(pieces, axis=0)
    return jnp.concatenate([piece.astype(f32) for piece in pieces], axis=0).astype(bf16)


def channelize_kernel(slot, slots, owners, chans, volts, halo, taps, table_high, table_low, *refs):
    outs, (dft, before, high, low) = refs[:owners], refs[owners:]
    stations, width, chunk = volts.shape
    rows = 2 * GROUP

    @pl.when(pl.program_id(0) == 0)
    def _():
        before[...] = halo[...]
        for index in range(owners):
            channel = chans[index, slot]
            dft[pl.ds(index * rows, rows), :] = table_high[channel]
            dft[pl.ds((owners + index) * rows, rows), :] = table_low[channel]

    tap = [jnp.broadcast_to(taps[:, m : m + 1], (width, LANES)) for m in range(8)]
    tap = [jnp.concatenate([one] * (chunk // LANES + 1), axis=1) for one in tap]
    groups = []
    for group in range(stations // GROUP):
        for member in range(GROUP):
            station = group * GROUP + member
            now = jnp.concatenate([before[station], volts[station]], axis=1).astype(f32)
            shifted = [now] + [pltpu.roll(now, m, axis=1) for m in (1, 2, 3)]
            near = sum(tap[m] * shifted[m] for m in range(4))
            far = sum(tap[4 + m] * shifted[m] for m in range(4))
            filtered = (near + pltpu.roll(far, 4, axis=1))[:, LANES:]
            top, rest = split_in_two(filtered)
            high[pl.ds(member * width, width), :] = top
            low[pl.ds(member * width, width), :] = rest
            before[station] = volts[station, :, chunk - LANES :]
        both = jnp.dot(dft[...], high[...], preferred_element_type=f32)
        cross = jnp.dot(dft[: owners * rows], low[...], preferred_element_type=f32)
        groups.append(both[: owners * rows] + (both[owners * rows :] + cross))
    for index in range(owners):
        for part in range(2):
            first = index * rows + part * GROUP
            piece = [one[first : first + GROUP] for one in groups]
            outs[index][part] = jnp.concatenate(piece, axis=0).astype(bf16)


def channelize(slot, slots, chans, volts, halo, taps, tables):
    stations, width, snaps = volts.shape
    owners = chans.shape[0]
    chunk = min(snaps, 512)
    kernel = functools.partial(channelize_kernel, slot, slots, owners)
    whole = lambda shape: pl.BlockSpec(shape, lambda t, c: (0,) * len(shape))
    out = jax.ShapeDtypeStruct((2, stations, snaps), bf16)
    return pl.pallas_call(
        kernel,
        grid_spec=pltpu.PrefetchScalarGridSpec(
            num_scalar_prefetch=1,
            grid=(snaps // chunk,),
            in_specs=[
                pl.BlockSpec((stations, width, chunk), lambda t, c: (0, 0, t)),
                whole(halo.shape),
                whole(taps.shape),
                whole(tables[0].shape),
                whole(tables[1].shape),
            ],
            out_specs=[pl.BlockSpec((2, stations, chunk), lambda t, c: (0, 0, t))] * owners,
            scratch_shapes=[
                pltpu.VMEM((2 * owners * 2 * GROUP, GROUP * width), bf16),
                pltpu.VMEM((stations, width, LANES), bf16),
                pltpu.VMEM((GROUP * width, chunk), bf16),
                pltpu.VMEM((GROUP * width, chunk), bf16),
            ],
        ),
        out_shape=[out] * owners,
        compiler_params=pltpu.CompilerParams(vmem_limit_bytes=32 << 20),
        cost_estimate=pl.CostEstimate(flops=2 * 10**9, bytes_accessed=4 << 20, transcendentals=0),
        name="channelize",
    )(chans, volts, halo, taps, *tables)


def gram_kernel(owners, *refs):
    blocks, out, total = refs[:owners], refs[owners], refs[owners + 1]
    half = owners * blocks[0].shape[1]
    stacked = merged_rows([one[part] for part in range(2) for one in blocks])
    gram = lax.dot_general(stacked, stacked, NT, preferred_element_type=f32)

    @pl.when(pl.program_id(0) == 0)
    def _():
        total[...] = gram

    @pl.when(pl.program_id(0) > 0)
    def _():
        total[...] += gram

    @pl.when(pl.program_id(0) == pl.num_programs(0) - 1)
    def _():
        sym_part = total[:half, :half] + total[half:, half:]
        skew_part = total[half:, :half] - total[:half, half:]
        row = lax.broadcasted_iota(jnp.int32, (half, half), 0)
        column = lax.broadcasted_iota(jnp.int32, (half, half), 1)
        out[...] = jnp.where(row >= column, sym_part, skew_part)


def packed_gram(blocks):
    _, stations, snaps = blocks[0].shape
    half = len(blocks) * stations
    chunk = min(snaps, 1024)
    return pl.pallas_call(
        functools.partial(gram_kernel, len(blocks)),
        grid=(snaps // chunk,),
        in_specs=[pl.BlockSpec((2, stations, chunk), lambda t: (0, 0, t))] * len(blocks),
        out_specs=pl.BlockSpec((half, half), lambda t: (0, 0)),
        out_shape=jax.ShapeDtypeStruct((half, half), f32),
        scratch_shapes=[pltpu.VMEM((2 * half, 2 * half), f32)],
        compiler_params=pltpu.CompilerParams(vmem_limit_bytes=32 << 20),
        cost_estimate=pl.CostEstimate(flops=3 * 10**8, bytes_accessed=1 << 20, transcendentals=0),
        name="gram",
    )(*blocks)


def dot(a, b, dims=(((1,), (0,)), ((), ()))):
    return lax.dot_general(a, b, dims, precision=lax.Precision.HIGHEST, preferred_element_type=f32)


def eliminate(real, imag, pivots):
    half = real.shape[0]
    for first in range(0, half, pivots):
        row_r, row_i = real[first : first + pivots], imag[first : first + pivots]
        side = jnp.concatenate(
            [
                jnp.concatenate([row_r[:, :half], -row_i[:, :half]], axis=1),
                jnp.concatenate([row_i[:, :half], row_r[:, :half]], axis=1),
            ],
            axis=0,
        )
        tile = first // LANES * LANES
        index = lax.broadcasted_iota(jnp.int32, row_r.shape, 0)
        lane = lax.broadcasted_iota(jnp.int32, row_r.shape, 1) - first
        inside = (lane >= 0) & (lane < pivots)
        row_r = jnp.concatenate([row_r[:, tile : tile + LANES], jnp.where(inside, jnp.where(lane == index, -1.0, 0.0), row_r)], axis=1)
        row_i = jnp.concatenate([row_i[:, tile : tile + LANES], jnp.where(inside, 0.0, row_i)], axis=1)
        index = lax.broadcasted_iota(jnp.int32, row_r.shape, 0)
        for step in range(pivots):
            lane = first - tile + step
            col_r = jnp.broadcast_to(row_r[:, lane : lane + 1], row_r.shape)
            col_i = jnp.broadcast_to(row_i[:, lane : lane + 1], row_i.shape)
            scale = 1.0 / jnp.broadcast_to(col_r[step : step + 1], row_r.shape)
            pick_r = jnp.broadcast_to(row_r[step : step + 1], row_r.shape) * scale
            pick_i = jnp.broadcast_to(row_i[step : step + 1], row_i.shape) * scale
            here = index == step
            row_r, row_i = (
                jnp.where(here, pick_r, row_r - (col_r * pick_r - col_i * pick_i)),
                jnp.where(here, pick_i, row_i - (col_r * pick_i + col_i * pick_r)),
            )
        row_r, row_i = row_r[:, LANES:], row_i[:, LANES:]
        update = dot(side, jnp.concatenate([row_r, row_i], axis=0), TN)
        rank = lax.broadcasted_iota(jnp.int32, real.shape, 0) - first
        own = (rank >= 0) & (rank < pivots)
        lane = lax.broadcasted_iota(jnp.int32, real.shape, 1) - first
        gone = (lane >= 0) & (lane < pivots)
        spread = lambda piece: jnp.concatenate([piece] * (half // pivots), axis=0)
        real = jnp.where(own, spread(row_r), jnp.where(gone, 0.0, real) - update[:half])
        imag = jnp.where(own, spread(row_i), jnp.where(gone, 0.0, imag) - update[half:])
    return real, imag


def beams_kernel(owners, segments, snap_total, has_earlier, *refs):
    grams, steer, blocks = refs[:segments], refs[segments], refs[segments + 1 : segments + 1 + owners]
    out, mix = refs[-2], refs[-1]
    half = grams[0].shape[0]

    @pl.when(pl.program_id(0) == 0)
    def _():
        packed = sum(one[...] for one in grams) * (1.0 / snap_total)
        row = lax.broadcasted_iota(jnp.int32, (half, half), 0)
        column = lax.broadcasted_iota(jnp.int32, (half, half), 1)
        turned = packed.T
        real = jnp.where(row >= column, packed, turned)
        real = jnp.where(row == column, real + loading_level, real)
        imag = jnp.where(row < column, packed, jnp.where(row > column, -turned, 0.0))
        steer_r, steer_i = steer[:half], steer[half:]
        real, imag = eliminate(
            jnp.concatenate([real, steer_r], axis=1),
            jnp.concatenate([imag, steer_i], axis=1),
            PIVOTS,
        )
        solved_r, solved_i = real[:, half:], imag[:, half:]
        power = jnp.sum(steer_r * solved_r + steer_i * solved_i, axis=0, keepdims=True)
        scale = 1.0 / jnp.sqrt(power)
        weight_r, weight_i = solved_r * scale, solved_i * scale
        upper = jnp.concatenate([weight_r.T, weight_i.T], axis=1)
        lower = jnp.concatenate([-weight_i.T, weight_r.T], axis=1)
        mix[...] = jnp.concatenate([upper, lower], axis=0).astype(bf16)

    stacked = merged_rows([one[part] for part in range(2) for one in blocks])
    beams = jnp.dot(mix[...], stacked, preferred_element_type=f32).astype(bf16)
    count = mix.shape[0] // 2
    out[0, 0] = beams[:count]
    out[0, 1] = beams[count:]


def beams(slot, slots, snap_total, grams, steer, blocks, earlier):
    _, stations, snaps = blocks[0].shape
    half = len(blocks) * stations
    count = steer.shape[1]
    chunk = min(snaps, 1024)
    whole = lambda shape: pl.BlockSpec(shape, lambda t: (0,) * len(shape))
    kernel = functools.partial(beams_kernel, len(blocks), len(grams), snap_total, earlier is not None)
    operands = [*grams, steer, *blocks]
    specs = [whole((half, half))] * len(grams) + [whole(steer.shape)]
    specs += [pl.BlockSpec((2, stations, chunk), lambda t: (0, 0, t))] * len(blocks)
    aliases = {}
    if earlier is not None:
        aliases = {len(operands): 0}
        operands.append(earlier)
        specs.append(pl.BlockSpec(memory_space=pl.ANY))
    return pl.pallas_call(
        kernel,
        grid=(snaps // chunk,),
        in_specs=specs,
        out_specs=pl.BlockSpec((1, 2, count, chunk), lambda t: (slot, 0, 0, t)),
        out_shape=jax.ShapeDtypeStruct((slots, 2, count, snaps), bf16),
        scratch_shapes=[pltpu.VMEM((2 * count, 2 * half), bf16)],
        input_output_aliases=aliases,
        compiler_params=pltpu.CompilerParams(vmem_limit_bytes=48 << 20),
        cost_estimate=pl.CostEstimate(flops=10**10, bytes_accessed=3 << 20, transcendentals=0),
        name="beams",
    )(*operands)


def partners(value, axis, distance):
    length = lax.axis_size(axis)
    return lax.ppermute(value, axis, [(i, i ^ distance) for i in range(length)])


def segment_sums(packed):
    length = lax.axis_size("seg")
    if length <= 4:
        return [packed] + [partners(packed, "seg", d) for d in range(1, length)]
    distance = 1
    while distance < length:
        packed = packed + partners(packed, "seg", distance)
        distance *= 2
    return [packed]


def steering(positions, beam_dirs, channel, channels):
    bearing = beam_dirs.astype(f32) * (full_turn / DIRS)
    frequency = 1.0 + channel.astype(f32) / channels
    path_delay = (
        positions[0][:, None] * jnp.cos(bearing)[None, :]
        + positions[1][:, None] * jnp.sin(bearing)[None, :]
    )
    phases = full_turn * frequency * path_delay
    return jnp.concatenate([jnp.cos(phases), jnp.sin(phases)], axis=0)


def on_device(voltages, filter_taps, positions, beam_dirs, chan_table):
    stations, width, snaps = voltages.shape
    channels = chan_table.shape[0]
    owners = lax.axis_size("stn")
    segments = lax.axis_size("seg")
    slots = channels // owners
    snap_total = snaps * segments
    halo = lax.ppermute(
        voltages[:, :, snaps - LANES :], "seg", [(i, i + 1) for i in range(segments - 1)]
    )
    order = lax.axis_index("stn") ^ jnp.arange(owners, dtype=jnp.int32)
    chans = chan_table.reshape(owners, slots)[order]
    places = positions.reshape(2, owners, stations)[:, order].reshape(2, owners * stations)
    steer = [steering(places, beam_dirs, chans[0, slot], channels) for slot in range(slots)]
    tables = block_tables(channels)
    taps = filter_taps.T
    result = None
    distances = sorted(range(1, owners), key=lambda d: (d < owners // 2, d))
    spectra = [channelize(s, slots, chans, voltages, halo, taps, tables) for s in range(slots)]
    for slot in range(slots):
        mine = spectra[slot]
        arrived = {d: partners(mine[d], "stn", d) for d in distances}
        blocks = [mine[0]] + [arrived[d] for d in range(1, owners)]
        grams = segment_sums(packed_gram(blocks))
        result = beams(slot, slots, snap_total, grams, steer[slot], blocks, result)
    return result


def solution(mesh):
    return jax.shard_map(
        on_device,
        mesh=mesh,
        in_specs=(P("stn", None, "seg"), P(), P(), P(), P()),
        out_specs=P("stn", None, None, "seg"),
        check_vma=False,
    )
```

time: 264 us -> 121 us (0.46)
  other arithmetic: 114 us -> 0.64 us
  waiting for transfers between devices: 90.8 us -> 19.8 us
  Pallas kernels: 0 us -> 63.8 us
  matrix products: 19.6 us -> 0 us
  starting transfers between devices: 9.62 us -> 25.9 us
  between operations: 13.7 us -> 1.48 us
  local copies, waits for them, and re-layouts: 13.9 us -> 8.55 us
    another operation x13 -> x0, other arithmetic: 107 us -> none  [the longest x9 66.8 us: on_device(): factor = jnp.linalg.cholesky(covariance)]
    pallas_call x0 -> x6, Pallas kernels: none -> 63.8 us  [the longest x2 43 us: beams(): pl.pallas_call(kernel, grid=(snaps // chunk,), in_specs=specs, out_specs=...]
    all_to_all x1 -> x0, waiting for transfers between devices: 45.3 us -> none  [on_device(): lax.all_to_all(spectra, 'stn', split_axis=0, concat_axis=2, tiled=True)]
    psum x1 -> x0, waiting for transfers between devices: 44.1 us -> none  [on_device(): sym_part, skew_part = lax.psum((sym_part, skew_part), 'seg')]
    ppermute x1 -> x21, starting transfers between devices: 3.12 us -> 25.9 us  [the longest x20 22.7 us: partners(): return lax.ppermute(value, axis, [(i, i ^ distance) for i in range(length)])]
    ppermute x1 -> x21, waiting for transfers between devices: 1.36 us -> 19.8 us  [the longest x20 19.8 us: partners(): return lax.ppermute(value, axis, [(i, i ^ distance) for i in range(length)])]
    dot_general x3 -> x0, matrix products: 14.4 us -> none  [the longest x1 11.6 us: channelize(): jnp.einsum('jap,spt->jast', dft_table, filtered, precision=lax.Precision....]
    all_to_all x1 -> x0, starting transfers between devices: 6.5 us -> none  [on_device(): lax.all_to_all(spectra, 'stn', split_axis=0, concat_axis=2, tiled=True)]
  transfers between devices with their start and end apart: 3 -> 21, of which waited for: 3 -> 6; matrix products, arithmetic and copies ran while one was open for 1% -> 4% of each run, Pallas kernels for 0% -> 27%
where the time goes in v1:
time: 121 us; the launch traced here: 120 us
  Pallas kernels  63.8 us (53%)
  starting transfers between devices  25.9 us (21%)
  waiting for transfers between devices  19.8 us (16%)
  local copies, waits for them, and re-layouts  8.55 us (7%)
  between operations  1.48 us (1%)
    pallas_call x2, Pallas kernels, beams(): pl.pallas_call(kernel, grid=(snaps // chunk,), in_specs=specs, out_specs=...  43 us
    ppermute x20, starting transfers between devices, partners(): return lax.ppermute(value, axis, [(i, i ^ distance) for i in range(length)])  22.7 us
    ppermute x20, waiting for transfers between devices, partners(): return lax.ppermute(value, axis, [(i, i ^ distance) for i in range(length)])  19.8 us
    pallas_call x2, Pallas kernels, channelize(): pl.pallas_call(kernel, grid_spec=pltpu.PrefetchScalarGridSpec(num_scalar_...  19.1 us
    unnamed x11, local copies, waits for them, and re-layouts  4.17 us
    ppermute x1, starting transfers between devices, on_device(): lax.ppermute(voltages[:, :, snaps - LANES:], 'seg', [(i, i + 1) for i in...  3.12 us
  transfers between devices with their start and end apart: 21, of which 6 were waited for; matrix products, arithmetic and copies ran while one was open for 4% of the time, Pallas kernels for 27%

profile of v1, /device:TPU:11, one launch (start us, length us, event | category | flops | bytes accessed | tf_op | source)
XLA Modules:
  0.0 120.1 jit_solution(11483359015753609275)
XLA Ops:
  0.0 0.9 slice.19
  0.9 3.1 %collective-permute-start = (bf16[16,32,128]{2,1,0:T(8,128)(2,1)S(1)}, bf16[16,32,128]{2,1,0:T(8,128)(2,1)S(1)}, u32[]{:S(2)}, u32[]{:S(2)}) collective-permute-start(bf16[16,32,128]{2,1,0:T(8,128)(2,1)S(1)} %slice.19), channel_id=1, source_target_pairs={{0,1},{1,2},{2,3},{4,5},{5,6},{6,7},{8,9},{9,10},{10,11},{12,13},{... | collective-permute-start | bytes 393224 | tf_op jit(solution)/shard_map/ppermute | solution.py:302
  4.1 0.7 reshape.45
  4.8 0.6 gather_fusion
  5.4 0.6 fusion.9
  7.3 0.8 reshape.46
  8.1 0.6 gather_fusion.1
  8.7 0.1 mul.75
  8.8 0.1 mul.80
  8.9 0.8 copy.11
  9.7 1.6 %copy-done = bf16[16,32,2048]{2,1,0:T(8,128)(2,1)S(1)} copy-done((bf16[16,32,2048]{2,1,0:T(8,128)(2,1)S(1)}, bf16[16,32,2048]{2,1,0:T(8,128)(2,1)}, u32[]{:S(2)}) %copy-start) | copy-done | bytes 2097176
  11.2 0.9 copy-done.1
  12.2 0.9 copy-done.2
  13.1 9.5 %channelize.3 = (bf16[2,16,2048]{2,1,0:T(8,128)(2,1)S(1)}, bf16[2,16,2048]{2,1,0:T(8,128)(2,1)S(1)}, bf16[2,16,2048]{2,1,0:T(8,128)(2,1)S(1)}, bf16[2,16,2048]{2...) custom-call(s32[8,2]{1,0:T(8,128)S(1)} %gather_fusion, ...), custom_call_target="tpu_custom_call" | custom-call | flops 2000000000 | bytes 4194304 | tf_op jit(solution)/shard_map/channelize/pallas_call | solution.py:91
  22.6 1.0 collective-permute-start.11
  23.6 0.2 collective-permute-start.12
  23.9 1.6 %collective-permute-start.13 = (bf16[2,16,2048]{2,1,0:T(8,128)(2,1)S(1)}, bf16[2,16,2048]{2,1,0:T(8,128)(2,1)S(1)}, u32[]{:S(2)}, u32[]{:S(2)}) collective-permute-start(bf16[2,16,2048]{2,1,0:T(8,128)(2,1)S(1)} %get-tuple-element.32), channel_id=1, source_target_pairs={{0,12},{4,8},{8,4},{12,0},{16,28},{20,24},{24,20},{28,16},{1,13},{... | collective-permute-start | bytes 393224 | tf_op jit(solution)/shard_map/ppermute | solution.py:270
  25.5 2.3 %collective-permute-start.14 = (bf16[2,16,2048]{2,1,0:T(8,128)(2,1)S(1)}, bf16[2,16,2048]{2,1,0:T(8,128)(2,1)S(1)}, u32[]{:S(2)}, u32[]{:S(2)}) collective-permute-start(bf16[2,16,2048]{2,1,0:T(8,128)(2,1)S(1)} %get-tuple-element.33), channel_id=1, source_target_pairs={{0,16},{4,20},{8,24},{12,28},{16,0},{20,4},{24,8},{28,12},{1,17},{... | collective-permute-start | bytes 393224 | tf_op jit(solution)/shard_map/ppermute | solution.py:270
  27.8 0.4 collective-permute-start.15
  28.2 1.3 %collective-permute-start.16 = (bf16[2,16,2048]{2,1,0:T(8,128)(2,1)S(1)}, bf16[2,16,2048]{2,1,0:T(8,128)(2,1)S(1)}, u32[]{:S(2)}, u32[]{:S(2)}) collective-permute-start(bf16[2,16,2048]{2,1,0:T(8,128)(2,1)S(1)} %get-tuple-element.35), channel_id=1, source_target_pairs={{0,24},{4,28},{8,16},{12,20},{16,8},{20,12},{24,0},{28,4},{1,25},{... | collective-permute-start | bytes 393224 | tf_op jit(solution)/shard_map/ppermute | solution.py:270
  29.5 3.0 %collective-permute-start.17 = (bf16[2,16,2048]{2,1,0:T(8,128)(2,1)S(1)}, bf16[2,16,2048]{2,1,0:T(8,128)(2,1)S(1)}, u32[]{:S(2)}, u32[]{:S(2)}) collective-permute-start(bf16[2,16,2048]{2,1,0:T(8,128)(2,1)S(1)} %get-tuple-element.36), channel_id=1, source_target_pairs={{0,28},{4,24},{8,20},{12,16},{16,12},{20,8},{24,4},{28,0},{1,29},{... | collective-permute-start | bytes 393224 | tf_op jit(solution)/shard_map/ppermute | solution.py:270
  32.5 9.5 %channelize.2 = (bf16[2,16,2048]{2,1,0:T(8,128)(2,1)S(1)}, bf16[2,16,2048]{2,1,0:T(8,128)(2,1)S(1)}, bf16[2,16,2048]{2,1,0:T(8,128)(2,1)S(1)}, bf16[2,16,2048]{2...) custom-call(s32[8,2]{1,0:T(8,128)S(1)} %gather_fusion, ...), custom_call_target="tpu_custom_call" | custom-call | flops 2000000000 | bytes 4194304 | tf_op jit(solution)/shard_map/channelize/pallas_call | solution.py:91
  42.1 0.1 collective-permute-start.1
  42.1 0.0 collective-permute-done.14.refs_4_.refs_9_
  42.1 3.7 %collective-permute-start.2 = (bf16[2,16,2048]{2,1,0:T(8,128)(2,1)S(1)}, bf16[2,16,2048]{2,1,0:T(8,128)(2,1)S(1)}, u32[]{:S(2)}, u32[]{:S(2)}) collective-permute-start(bf16[2,16,2048]{2,1,0:T(8,128)(2,1)S(1)} %get-tuple-element.23), channel_id=1, source_target_pairs={{0,8},{4,12},{8,0},{12,4},{16,24},{20,28},{24,16},{28,20},{1,9},{5... | collective-permute-start | bytes 393224 | tf_op jit(solution)/shard_map/ppermute | solution.py:270
  45.9 0.0 collective-permute-done.15.refs_5_.refs_10_
  45.9 0.4 collective-permute-start.3
  46.3 1.3 %collective-permute-done.16.refs_6_.refs_11_ = bf16[2,16,2048]{2,1,0:T(8,128)(2,1)S(1)} collective-permute-done((bf16[2,16,2048]{2,1,0:T(8,128)(2,1)S(1)}, bf16[2,16,2048]{2,1,0:T(8,128)(2,1)S(1)}, u32[]{:S(2)}, u32[]{:S(2)}) %collective-permute-start.16) | collective-permute-done | bytes 131104 | tf_op jit(solution)/shard_map/ppermute | solution.py:270
  47.6 1.3 %collective-permute-start.4 = (bf16[2,16,2048]{2,1,0:T(8,128)(2,1)S(1)}, bf16[2,16,2048]{2,1,0:T(8,128)(2,1)S(1)}, u32[]{:S(2)}, u32[]{:S(2)}) collective-permute-start(bf16[2,16,2048]{2,1,0:T(8,128)(2,1)S(1)} %get-tuple-element.25), channel_id=1, source_target_pairs={{0,16},{4,20},{8,24},{12,28},{16,0},{20,4},{24,8},{28,12},{1,17},{... | collective-permute-start | bytes 393224 | tf_op jit(solution)/shard_map/ppermute | solution.py:270
  48.9 1.6 %collective-permute-done.17.refs_7_.refs_12_ = bf16[2,16,2048]{2,1,0:T(8,128)(2,1)S(1)} collective-permute-done((bf16[2,16,2048]{2,1,0:T(8,128)(2,1)S(1)}, bf16[2,16,2048]{2,1,0:T(8,128)(2,1)S(1)}, u32[]{:S(2)}, u32[]{:S(2)}) %collective-permute-start.17) | collective-permute-done | bytes 131104 | tf_op jit(solution)/shard_map/ppermute | solution.py:270
  50.6 0.9 collective-permute-start.5
  51.5 0.6 fusion.5
  52.0 0.0 collective-permute-done.1.refs_1_.refs_6_
  52.1 2.3 %collective-permute-start.6 = (bf16[2,16,2048]{2,1,0:T(8,128)(2,1)S(1)}, bf16[2,16,2048]{2,1,0:T(8,128)(2,1)S(1)}, u32[]{:S(2)}, u32[]{:S(2)}) collective-permute-start(bf16[2,16,2048]{2,1,0:T(8,128)(2,1)S(1)} %get-tuple-element.27), channel_id=1, source_target_pairs={{0,24},{4,28},{8,16},{12,20},{16,8},{20,12},{24,0},{28,4},{1,25},{... | collective-permute-start | bytes 393224 | tf_op jit(solution)/shard_map/ppermute | solution.py:270
  54.3 0.0 collective-permute-start.7
  54.3 0.9 gram.3.refs_0_
  55.2 1.3 %collective-permute-start.20 = (f32[128,128]{1,0:T(8,128)S(1)}, f32[128,128]{1,0:T(8,128)S(1)}, u32[]{:S(2)}, u32[]{:S(2)}) collective-permute-start(f32[128,128]{1,0:T(8,128)S(1)} %gram.3.refs_0_), channel_id=1, source_target_pairs={{0,3},{1,2},{2,1},{3,0},{4,7},{5,6},{6,5},{7,4},{8,11},{9,10},{10,... | collective-permute-start | bytes 196616 | tf_op jit(solution)/shard_map/ppermute | solution.py:270
  56.5 7.8 %collective-permute-done.4.refs_4_.refs_9_ = bf16[2,16,2048]{2,1,0:T(8,128)(2,1)S(1)} collective-permute-done((bf16[2,16,2048]{2,1,0:T(8,128)(2,1)S(1)}, bf16[2,16,2048]{2,1,0:T(8,128)(2,1)S(1)}, u32[]{:S(2)}, u32[]{:S(2)}) %collective-permute-start.4) | collective-permute-done | bytes 131104 | tf_op jit(solution)/shard_map/ppermute | solution.py:270
  64.3 2.8 %collective-permute-done.5.refs_5_.refs_10_ = bf16[2,16,2048]{2,1,0:T(8,128)(2,1)S(1)} collective-permute-done((bf16[2,16,2048]{2,1,0:T(8,128)(2,1)S(1)}, bf16[2,16,2048]{2,1,0:T(8,128)(2,1)S(1)}, u32[]{:S(2)}, u32[]{:S(2)}) %collective-permute-start.5) | collective-permute-done | bytes 131104 | tf_op jit(solution)/shard_map/ppermute | solution.py:270
  67.1 0.3 collective-permute-start.18
  67.4 3.4 %collective-permute-done.6.refs_6_.refs_11_ = bf16[2,16,2048]{2,1,0:T(8,128)(2,1)S(1)} collective-permute-done((bf16[2,16,2048]{2,1,0:T(8,128)(2,1)S(1)}, bf16[2,16,2048]{2,1,0:T(8,128)(2,1)S(1)}, u32[]{:S(2)}, u32[]{:S(2)}) %collective-permute-start.6) | collective-permute-done | bytes 131104 | tf_op jit(solution)/shard_map/ppermute | solution.py:270
  70.7 2.8 %collective-permute-done.7.refs_7_.refs_12_ = bf16[2,16,2048]{2,1,0:T(8,128)(2,1)S(1)} collective-permute-done((bf16[2,16,2048]{2,1,0:T(8,128)(2,1)S(1)}, bf16[2,16,2048]{2,1,0:T(8,128)(2,1)S(1)}, u32[]{:S(2)}, u32[]{:S(2)}) %collective-permute-start.7) | collective-permute-done | bytes 131104 | tf_op jit(solution)/shard_map/ppermute | solution.py:270
  73.5 0.9 gram.2.refs_0_
  74.4 1.3 %collective-permute-start.10 = (f32[128,128]{1,0:T(8,128)S(1)}, f32[128,128]{1,0:T(8,128)S(1)}, u32[]{:S(2)}, u32[]{:S(2)}) collective-permute-start(f32[128,128]{1,0:T(8,128)S(1)} %gram.2.refs_0_), channel_id=1, source_target_pairs={{0,3},{1,2},{2,1},{3,0},{4,7},{5,6},{6,5},{7,4},{8,11},{9,10},{10,... | collective-permute-start | bytes 196616 | tf_op jit(solution)/shard_map/ppermute | solution.py:270
  75.7 0.2 collective-permute-start.9
  75.9 1.2 collective-permute-start.8
  77.1 21.4 %beams.2.refs_13_ = bf16[2,2,128,2048]{3,2,1,0:T(8,128)(2,1)} custom-call(f32[128,128]{1,0:T(8,128)S(1)} %gram.3.refs_0_, f32[128,128]{1,0:T(8,128)S(1)} %collective-permute-done.18.refs_1_, f32[128,128]{1,0:T(8,128)S(1)} %collective-permute-done.19.refs_2_, f32[128,128]{1,0:T(8,128)S(1)} %collective-permute-done.20.refs_3_, ...), custom_call_target="tpu_custom_call" | custom-call | flops 10000000000 | bytes 3145728 | tf_op jit(solution)/shard_map/beams/pallas_call | solution.py:254
  98.5 21.6 %beams.3 = bf16[2,2,128,2048]{3,2,1,0:T(8,128)(2,1)} custom-call(f32[128,128]{1,0:T(8,128)S(1)} %gram.2.refs_0_, f32[128,128]{1,0:T(8,128)S(1)} %collective-permute-done.8.refs_1_, f32[128,128]{1,0:T(8,128)S(1)} %collective-permute-done.9.refs_2_, f32[128,128]{1,0:T(8,128)S(1)} %collective-permute-done.10.refs_3_, ...), custom_call_target="tpu_custom_call", output_to_operand_aliasing={{}: (13, {})} | custom-call | flops 10000000000 | bytes 3145728 | tf_op jit(solution)/shard_map/beams/pallas_call | solution.py:254
  (26 shorter events, 0.2 us)
Async XLA Ops:
  0.9 8.7 %collective-permute-start = (bf16[16,32,128]{2,1,0:T(8,128)(2,1)S(1)}, bf16[16,32,128]{2,1,0:T(8,128)(2,1)S(1)}, u32[]{:S(2)}, u32[]{:S(2)}) collective-permute-start(bf16[16,32,128]{2,1,0:T(8,128)(2,1)S(1)} %slice.19), channel_id=1, source_target_pairs={{0,1},{1,2},{2,3},{4,5},{5,6},{6,7},{8,9},{9,10},{10,11},{12,13},{... | collective-permute-start | bytes 393224 | tf_op jit(solution)/shard_map/ppermute | solution.py:302
  9.7 1.6 %copy-start = (bf16[16,32,2048]{2,1,0:T(8,128)(2,1)S(1)}, bf16[16,32,2048]{2,1,0:T(8,128)(2,1)}, u32[]{:S(2)}) copy-start(bf16[16,32,2048]{2,1,0:T(8,128)(2,1)} %volts.3) | copy-start | bytes 6291460
  11.2 0.9 copy-start.1
  12.2 0.9 copy-start.2
  13.1 10.8 %copy-start.4 = (s32[128]{0:T(128)S(1)}, s32[128]{0:T(128)}, u32[]{:S(2)}) copy-start(s32[128]{0:T(128)} %param.10) | copy-start | bytes 1540
  13.1 19.4 %copy-start.3 = (bf16[16,16,256]{2,1,0:T(8,128)(2,1)S(1)}, bf16[16,16,256]{2,1,0:T(8,128)(2,1)}, u32[]{:S(2)}) copy-start(bf16[16,16,256]{2,1,0:T(8,128)(2,1)} %constant.30.clone.table_high) | copy-start | bytes 393220
  22.6 5.5 %collective-permute-start.11 = (bf16[2,16,2048]{2,1,0:T(8,128)(2,1)S(1)}, bf16[2,16,2048]{2,1,0:T(8,128)(2,1)S(1)}, u32[]{:S(2)}, u32[]{:S(2)}) collective-permute-start(bf16[2,16,2048]{2,1,0:T(8,128)(2,1)S(1)} %get-tuple-element.30), channel_id=1, source_target_pairs={{0,4},{4,0},{8,12},{12,8},{16,20},{20,16},{24,28},{28,24},{1,5},{5... | collective-permute-start | bytes 393224 | tf_op jit(solution)/shard_map/ppermute | solution.py:270
  23.6 5.8 %collective-permute-start.12 = (bf16[2,16,2048]{2,1,0:T(8,128)(2,1)S(1)}, bf16[2,16,2048]{2,1,0:T(8,128)(2,1)S(1)}, u32[]{:S(2)}, u32[]{:S(2)}) collective-permute-start(bf16[2,16,2048]{2,1,0:T(8,128)(2,1)S(1)} %get-tuple-element.31), channel_id=1, source_target_pairs={{0,8},{4,12},{8,0},{12,4},{16,24},{20,28},{24,16},{28,20},{1,9},{5... | collective-permute-start | bytes 393224 | tf_op jit(solution)/shard_map/ppermute | solution.py:270
  23.9 18.2 %collective-permute-start.13 = (bf16[2,16,2048]{2,1,0:T(8,128)(2,1)S(1)}, bf16[2,16,2048]{2,1,0:T(8,128)(2,1)S(1)}, u32[]{:S(2)}, u32[]{:S(2)}) collective-permute-start(bf16[2,16,2048]{2,1,0:T(8,128)(2,1)S(1)} %get-tuple-element.32), channel_id=1, source_target_pairs={{0,12},{4,8},{8,4},{12,0},{16,28},{20,24},{24,20},{28,16},{1,13},{... | collective-permute-start | bytes 393224 | tf_op jit(solution)/shard_map/ppermute | solution.py:270
  25.5 16.7 %collective-permute-start.14 = (bf16[2,16,2048]{2,1,0:T(8,128)(2,1)S(1)}, bf16[2,16,2048]{2,1,0:T(8,128)(2,1)S(1)}, u32[]{:S(2)}, u32[]{:S(2)}) collective-permute-start(bf16[2,16,2048]{2,1,0:T(8,128)(2,1)S(1)} %get-tuple-element.33), channel_id=1, source_target_pairs={{0,16},{4,20},{8,24},{12,28},{16,0},{20,4},{24,8},{28,12},{1,17},{... | collective-permute-start | bytes 393224 | tf_op jit(solution)/shard_map/ppermute | solution.py:270
  27.8 18.1 %collective-permute-start.15 = (bf16[2,16,2048]{2,1,0:T(8,128)(2,1)S(1)}, bf16[2,16,2048]{2,1,0:T(8,128)(2,1)S(1)}, u32[]{:S(2)}, u32[]{:S(2)}) collective-permute-start(bf16[2,16,2048]{2,1,0:T(8,128)(2,1)S(1)} %get-tuple-element.34), channel_id=1, source_target_pairs={{0,20},{4,16},{8,28},{12,24},{16,4},{20,0},{24,12},{28,8},{1,21},{... | collective-permute-start | bytes 393224 | tf_op jit(solution)/shard_map/ppermute | solution.py:270
  28.2 19.4 %collective-permute-start.16 = (bf16[2,16,2048]{2,1,0:T(8,128)(2,1)S(1)}, bf16[2,16,2048]{2,1,0:T(8,128)(2,1)S(1)}, u32[]{:S(2)}, u32[]{:S(2)}) collective-permute-start(bf16[2,16,2048]{2,1,0:T(8,128)(2,1)S(1)} %get-tuple-element.35), channel_id=1, source_target_pairs={{0,24},{4,28},{8,16},{12,20},{16,8},{20,12},{24,0},{28,4},{1,25},{... | collective-permute-start | bytes 393224 | tf_op jit(solution)/shard_map/ppermute | solution.py:270
  29.5 21.1 %collective-permute-start.17 = (bf16[2,16,2048]{2,1,0:T(8,128)(2,1)S(1)}, bf16[2,16,2048]{2,1,0:T(8,128)(2,1)S(1)}, u32[]{:S(2)}, u32[]{:S(2)}) collective-permute-start(bf16[2,16,2048]{2,1,0:T(8,128)(2,1)S(1)} %get-tuple-element.36), channel_id=1, source_target_pairs={{0,28},{4,24},{8,20},{12,16},{16,12},{20,8},{24,4},{28,0},{1,29},{... | collective-permute-start | bytes 393224 | tf_op jit(solution)/shard_map/ppermute | solution.py:270
  42.1 10.0 %collective-permute-start.1 = (bf16[2,16,2048]{2,1,0:T(8,128)(2,1)S(1)}, bf16[2,16,2048]{2,1,0:T(8,128)(2,1)S(1)}, u32[]{:S(2)}, u32[]{:S(2)}) collective-permute-start(bf16[2,16,2048]{2,1,0:T(8,128)(2,1)S(1)} %get-tuple-element.22), channel_id=1, source_target_pairs={{0,4},{4,0},{8,12},{12,8},{16,20},{20,16},{24,28},{28,24},{1,5},{5... | collective-permute-start | bytes 393224 | tf_op jit(solution)/shard_map/ppermute | solution.py:270
  42.1 12.2 %collective-permute-start.2 = (bf16[2,16,2048]{2,1,0:T(8,128)(2,1)S(1)}, bf16[2,16,2048]{2,1,0:T(8,128)(2,1)S(1)}, u32[]{:S(2)}, u32[]{:S(2)}) collective-permute-start(bf16[2,16,2048]{2,1,0:T(8,128)(2,1)S(1)} %get-tuple-element.23), channel_id=1, source_target_pairs={{0,8},{4,12},{8,0},{12,4},{16,24},{20,28},{24,16},{28,20},{1,9},{5... | collective-permute-start | bytes 393224 | tf_op jit(solution)/shard_map/ppermute | solution.py:270
  45.9 9.3 %collective-permute-start.3 = (bf16[2,16,2048]{2,1,0:T(8,128)(2,1)S(1)}, bf16[2,16,2048]{2,1,0:T(8,128)(2,1)S(1)}, u32[]{:S(2)}, u32[]{:S(2)}) collective-permute-start(bf16[2,16,2048]{2,1,0:T(8,128)(2,1)S(1)} %get-tuple-element.24), channel_id=1, source_target_pairs={{0,12},{4,8},{8,4},{12,0},{16,28},{20,24},{24,20},{28,16},{1,13},{... | collective-permute-start | bytes 393224 | tf_op jit(solution)/shard_map/ppermute | solution.py:270
  47.6 16.7 %collective-permute-start.4 = (bf16[2,16,2048]{2,1,0:T(8,128)(2,1)S(1)}, bf16[2,16,2048]{2,1,0:T(8,128)(2,1)S(1)}, u32[]{:S(2)}, u32[]{:S(2)}) collective-permute-start(bf16[2,16,2048]{2,1,0:T(8,128)(2,1)S(1)} %get-tuple-element.25), channel_id=1, source_target_pairs={{0,16},{4,20},{8,24},{12,28},{16,0},{20,4},{24,8},{28,12},{1,17},{... | collective-permute-start | bytes 393224 | tf_op jit(solution)/shard_map/ppermute | solution.py:270
  50.6 16.5 %collective-permute-start.5 = (bf16[2,16,2048]{2,1,0:T(8,128)(2,1)S(1)}, bf16[2,16,2048]{2,1,0:T(8,128)(2,1)S(1)}, u32[]{:S(2)}, u32[]{:S(2)}) collective-permute-start(bf16[2,16,2048]{2,1,0:T(8,128)(2,1)S(1)} %get-tuple-element.26), channel_id=1, source_target_pairs={{0,20},{4,16},{8,28},{12,24},{16,4},{20,0},{24,12},{28,8},{1,21},{... | collective-permute-start | bytes 393224 | tf_op jit(solution)/shard_map/ppermute | solution.py:270
  52.1 18.7 %collective-permute-start.6 = (bf16[2,16,2048]{2,1,0:T(8,128)(2,1)S(1)}, bf16[2,16,2048]{2,1,0:T(8,128)(2,1)S(1)}, u32[]{:S(2)}, u32[]{:S(2)}) collective-permute-start(bf16[2,16,2048]{2,1,0:T(8,128)(2,1)S(1)} %get-tuple-element.27), channel_id=1, source_target_pairs={{0,24},{4,28},{8,16},{12,20},{16,8},{20,12},{24,0},{28,4},{1,25},{... | collective-permute-start | bytes 393224 | tf_op jit(solution)/shard_map/ppermute | solution.py:270
  54.3 19.2 %collective-permute-start.7 = (bf16[2,16,2048]{2,1,0:T(8,128)(2,1)S(1)}, bf16[2,16,2048]{2,1,0:T(8,128)(2,1)S(1)}, u32[]{:S(2)}, u32[]{:S(2)}) collective-permute-start(bf16[2,16,2048]{2,1,0:T(8,128)(2,1)S(1)} %get-tuple-element.28), channel_id=1, source_target_pairs={{0,28},{4,24},{8,20},{12,16},{16,12},{20,8},{24,4},{28,0},{1,29},{... | collective-permute-start | bytes 393224 | tf_op jit(solution)/shard_map/ppermute | solution.py:270
  55.2 20.7 %collective-permute-start.20 = (f32[128,128]{1,0:T(8,128)S(1)}, f32[128,128]{1,0:T(8,128)S(1)}, u32[]{:S(2)}, u32[]{:S(2)}) collective-permute-start(f32[128,128]{1,0:T(8,128)S(1)} %gram.3.refs_0_), channel_id=1, source_target_pairs={{0,3},{1,2},{2,1},{3,0},{4,7},{5,6},{6,5},{7,4},{8,11},{9,10},{10,... | collective-permute-start | bytes 196616 | tf_op jit(solution)/shard_map/ppermute | solution.py:270
  64.3 12.9 %collective-permute-start.19 = (f32[128,128]{1,0:T(8,128)S(1)}, f32[128,128]{1,0:T(8,128)S(1)}, u32[]{:S(2)}, u32[]{:S(2)}) collective-permute-start(f32[128,128]{1,0:T(8,128)S(1)} %gram.3.refs_0_), channel_id=1, source_target_pairs={{0,2},{1,3},{2,0},{3,1},{4,6},{5,7},{6,4},{7,5},{8,10},{9,11},{10,... | collective-permute-start | bytes 196616 | tf_op jit(solution)/shard_map/ppermute | solution.py:270
  67.1 10.1 %collective-permute-start.18 = (f32[128,128]{1,0:T(8,128)S(1)}, f32[128,128]{1,0:T(8,128)S(1)}, u32[]{:S(2)}, u32[]{:S(2)}) collective-permute-start(f32[128,128]{1,0:T(8,128)S(1)} %gram.3.refs_0_), channel_id=1, source_target_pairs={{0,1},{1,0},{2,3},{3,2},{4,5},{5,4},{6,7},{7,6},{8,9},{9,8},{10,11... | collective-permute-start | bytes 196616 | tf_op jit(solution)/shard_map/ppermute | solution.py:270
  74.4 24.1 %collective-permute-start.10 = (f32[128,128]{1,0:T(8,128)S(1)}, f32[128,128]{1,0:T(8,128)S(1)}, u32[]{:S(2)}, u32[]{:S(2)}) collective-permute-start(f32[128,128]{1,0:T(8,128)S(1)} %gram.2.refs_0_), channel_id=1, source_target_pairs={{0,3},{1,2},{2,1},{3,0},{4,7},{5,6},{6,5},{7,4},{8,11},{9,10},{10,... | collective-permute-start | bytes 196616 | tf_op jit(solution)/shard_map/ppermute | solution.py:270
  75.7 22.8 %collective-permute-start.9 = (f32[128,128]{1,0:T(8,128)S(1)}, f32[128,128]{1,0:T(8,128)S(1)}, u32[]{:S(2)}, u32[]{:S(2)}) collective-permute-start(f32[128,128]{1,0:T(8,128)S(1)} %gram.2.refs_0_), channel_id=1, source_target_pairs={{0,2},{1,3},{2,0},{3,1},{4,6},{5,7},{6,4},{7,5},{8,10},{9,11},{10,... | collective-permute-start | bytes 196616 | tf_op jit(solution)/shard_map/ppermute | solution.py:270
  75.9 22.6 %collective-permute-start.8 = (f32[128,128]{1,0:T(8,128)S(1)}, f32[128,128]{1,0:T(8,128)S(1)}, u32[]{:S(2)}, u32[]{:S(2)}) collective-permute-start(f32[128,128]{1,0:T(8,128)S(1)} %gram.2.refs_0_), channel_id=1, source_target_pairs={{0,1},{1,0},{2,3},{3,2},{4,5},{5,4},{6,7},{7,6},{8,9},{9,8},{10,11... | collective-permute-start | bytes 196616 | tf_op jit(solution)/shard_map/ppermute | solution.py:270

commit v2 on v0

v2 whole, which is shorter than its diff:
```python
import functools
import math

import jax
import jax.numpy as jnp
from jax import lax
from jax.experimental import pallas as pl
from jax.experimental.pallas import tpu as pltpu
from jax.sharding import PartitionSpec as P

DIRS = 360
LANES = 128
GROUP = 8
PIVOTS = 16
AT_ONCE = 8
VMEM_BYTES = 16 << 20
GRAM_VMEM = 8 << 20
BEAMS_VMEM = 12 << 20

loading_level = 0.1
full_turn = 2.0 * math.pi
NT = (((1,), (1,)), ((), ()))
TN = (((0,), (0,)), ((), ()))
f32, bf16 = jnp.float32, jnp.bfloat16


def split_in_two(value):
    high = value.astype(bf16)
    return high, (value - high.astype(f32)).astype(bf16)


def merged_rows(pieces):
    if all(piece.shape[0] % 16 == 0 for piece in pieces):
        return jnp.concatenate(pieces, axis=0)
    return jnp.concatenate([piece.astype(f32) for piece in pieces], axis=0).astype(bf16)


def dft_rows(channels, width):
    shape = (2 * len(channels), GROUP * width)
    row = lax.broadcasted_iota(jnp.int32, shape, 0)
    lane = lax.broadcasted_iota(jnp.int32, shape, 1)
    channel = jnp.zeros(shape, jnp.int32)
    for index, one in enumerate(channels):
        channel = jnp.where(row // 2 == index, one, channel)
    angle = lax.rem(channel * lax.rem(lane, width), width).astype(f32) * (full_turn / width)
    values = jnp.where(row % 2 == 0, jnp.cos(angle), -jnp.sin(angle))
    shape = (GROUP, GROUP * width)
    own = lax.broadcasted_iota(jnp.int32, shape, 1) // width == lax.broadcasted_iota(jnp.int32, shape, 0)
    spread = [jnp.where(own, jnp.broadcast_to(values[i : i + 1], shape), 0.0) for i in range(2 * len(channels))]
    return jnp.concatenate(spread, axis=0)


def channelize_kernel(owners, first_slot, slots, part, joined, *refs):
    count = owners * slots
    has_halo = part != "second"
    chans_in, volts, taps_in = refs[:3]
    others = refs[3 + has_halo : 3 + has_halo + joined]
    outs = refs[3 + has_halo + joined : len(refs) - 10]
    dft, held, high, low, chans, taps, sems, chans_sem, taps_sem, halo_sem = refs[-10:]
    stations, width, snaps = volts.shape
    chunk = held.shape[2] - LANES
    tap_count = taps.shape[0]
    step = tap_count // 2
    rows = 2 * GROUP
    half = count * rows
    pieces = sems.shape[0]
    piece = stations // pieces
    small = [pltpu.make_async_copy(chans_in, chans, chans_sem), pltpu.make_async_copy(taps_in, taps, taps_sem)]
    if has_halo:
        small.append(pltpu.make_async_copy(refs[3], held.at[:, :, :LANES], halo_sem))
    copies = []
    for index in range(pieces):
        members = pl.ds(index * piece, piece)
        if has_halo:
            source, target = volts.at[members, :, :chunk], held.at[members, :, LANES:]
        else:
            source, target = volts.at[members, :, snaps - chunk - LANES :], held.at[members]
        copies.append(pltpu.make_async_copy(source, target, sems.at[index]))
    for copy in small + copies:
        copy.start()
    for copy in small:
        copy.wait()

    me = lax.axis_index("stn")
    every = chans.shape[0] // owners
    table = dft_rows([chans[(me ^ d) * every + first_slot + slot] for slot in range(slots) for d in range(owners)], width)
    dft[:half], dft[half:] = split_in_two(table)
    columns = taps[...].T
    tap = [jnp.broadcast_to(columns[:, m : m + 1], (width, chunk + LANES)) for m in range(tap_count)]
    results = []
    for station in range(stations):
        if station % piece == 0:
            copies[station // piece].wait()
        now = held[station]
        shifted = [(pltpu.roll(now, m, axis=1) if m else now).astype(f32) for m in range(step)]
        near = sum(tap[m] * shifted[m] for m in range(step))
        far = sum(tap[step + m] * shifted[m] for m in range(step))
        filtered = (near + pltpu.roll(far, step, axis=1))[:, LANES:]
        member = station % GROUP
        high[pl.ds(member * width, width), :], low[pl.ds(member * width, width), :] = split_in_two(filtered)
        if member == GROUP - 1:
            both = jnp.dot(dft[...], high[...], preferred_element_type=f32)
            cross = jnp.dot(dft[:half], low[...], preferred_element_type=f32)
            results.append(both[:half] + (both[half:] + cross))
    for index in range(count):
        for real in range(2):
            first = index * rows + real * GROUP
            outs[index][real, :, :chunk] = jnp.concatenate([one[first : first + GROUP] for one in results], axis=0).astype(bf16)
        if index < joined:
            outs[index][:, :, chunk:] = others[index][...]


def channelize(owners, first_slot, slots, part, chans, volts, taps, halo=None, joined=()):
    stations, width, snaps = volts.shape
    count = owners * slots
    chunk = snaps if part == "whole" else snaps // 2
    pieces = max(stations // 4, 1)
    out_shape = [jax.ShapeDtypeStruct((2, stations, snaps if i < len(joined) else chunk), bf16) for i in range(count)]
    operands = [pltpu.with_memory_space_constraint(one, pltpu.HBM) for one in (chans, volts, taps)]
    operands += ([] if halo is None else [halo]) + list(joined)
    return pl.pallas_call(
        functools.partial(channelize_kernel, owners, first_slot, slots, part, len(joined)),
        in_specs=[pl.BlockSpec(memory_space=pltpu.HBM)] * 3
        + [pl.BlockSpec(memory_space=pl.ANY)] * (halo is not None)
        + [pl.BlockSpec(memory_space=pltpu.VMEM)] * len(joined),
        out_specs=[pl.BlockSpec(memory_space=pltpu.VMEM)] * len(out_shape),
        out_shape=out_shape,
        scratch_shapes=[
            pltpu.VMEM((4 * count * GROUP, GROUP * width), bf16),
            pltpu.VMEM((stations, width, chunk + LANES), bf16),
            pltpu.VMEM((GROUP * width, chunk), bf16),
            pltpu.VMEM((GROUP * width, chunk), bf16),
            pltpu.SMEM(chans.shape, jnp.int32),
            pltpu.VMEM(taps.shape, f32),
            pltpu.SemaphoreType.DMA((pieces,)),
            pltpu.SemaphoreType.DMA(()),
            pltpu.SemaphoreType.DMA(()),
            pltpu.SemaphoreType.DMA(()),
        ],
        compiler_params=pltpu.CompilerParams(vmem_limit_bytes=VMEM_BYTES),
        cost_estimate=pl.CostEstimate(flops=4 * 10**9, bytes_accessed=3 << 20, transcendentals=0),
        name="channelize_" + part,
    )(*operands)


def stacked_rows(counts, refs):
    rows = []
    for part in range(2):
        at = 0
        for count in counts:
            rows.append(jnp.concatenate([one[part] for one in refs[at : at + count]], axis=1))
            at += count
    return merged_rows(rows)


def gram_kernel(counts, *refs):
    out = refs[-1]
    half = out.shape[0]
    stacked = stacked_rows(counts, refs[:-1])
    gram = lax.dot_general(stacked, stacked, NT, preferred_element_type=f32)
    sym_part = gram[:half, :half] + gram[half:, half:]
    skew_part = gram[half:, :half] - gram[:half, half:]
    row = lax.broadcasted_iota(jnp.int32, (half, half), 0)
    column = lax.broadcasted_iota(jnp.int32, (half, half), 1)
    out[...] = jnp.where(row >= column, sym_part, skew_part)


def packed_gram(blocks):
    half = len(blocks) * blocks[0][0].shape[1]
    operands = [one for block in blocks for one in block]
    return pl.pallas_call(
        functools.partial(gram_kernel, [len(block) for block in blocks]),
        in_specs=[pl.BlockSpec(memory_space=pltpu.VMEM)] * len(operands),
        out_specs=pl.BlockSpec(memory_space=pltpu.VMEM),
        out_shape=jax.ShapeDtypeStruct((half, half), f32),
        compiler_params=pltpu.CompilerParams(vmem_limit_bytes=GRAM_VMEM),
        cost_estimate=pl.CostEstimate(flops=3 * 10**8, bytes_accessed=1 << 20, transcendentals=0),
        name="gram",
    )(*operands)


def split_in_three(value):
    high, rest = value.astype(bf16), value
    rest = rest - high.astype(f32)
    middle = rest.astype(bf16)
    return high, middle, (rest - middle.astype(f32)).astype(bf16)


def deep_dot(left, right):
    a, b = split_in_three(left), split_in_three(right)
    left = jnp.concatenate([a[0], a[0], a[1], a[1], a[0], a[2]], axis=0)
    right = jnp.concatenate([b[0], b[1], b[0], b[1], b[2], b[0]], axis=0)
    return lax.dot_general(left, right, TN, preferred_element_type=f32)


def sweep_rows(row_r, row_i, lanes, at_once):
    count, width = row_r.shape
    narrow = (count, LANES)
    tiles = width // LANES
    index, index_wide = (lax.broadcasted_iota(jnp.int32, shape, 0) for shape in (narrow, (count, width)))
    repeated = lambda value: jnp.concatenate([value] * tiles, axis=1)
    for start in range(0, count, at_once):
        fetched = lanes[start : start + at_once]
        col_r = [jnp.broadcast_to(row_r[:, lane : lane + 1], narrow) for lane in fetched]
        col_i = [jnp.broadcast_to(row_i[:, lane : lane + 1], narrow) for lane in fetched]
        for j in range(len(fetched)):
            step = start + j
            spread = lambda value: jnp.broadcast_to(value[step : step + 1], value.shape)
            a, b = col_r[j], col_i[j]
            scale = 1.0 / spread(a)

            def swept(real, imag, here, a, b, scale):
                pick_r, pick_i = spread(real) * scale, spread(imag) * scale
                return (
                    jnp.where(here, pick_r, real - (a * pick_r - b * pick_i)),
                    jnp.where(here, pick_i, imag - (a * pick_i + b * pick_r)),
                )

            for later in range(j + 1, len(fetched)):
                col_r[later], col_i[later] = swept(col_r[later], col_i[later], index == step, a, b, scale)
            row_r, row_i = swept(row_r, row_i, index_wide == step, repeated(a), repeated(b), repeated(scale))
    return row_r, row_i


def eliminate(real, imag, pivots, at_once):
    half = real.shape[0]
    rank = lax.broadcasted_iota(jnp.int32, real.shape, 0)
    lane = lax.broadcasted_iota(jnp.int32, real.shape, 1)
    for first in range(0, half, pivots):
        last = first + pivots
        row_r, row_i = real[first:last], imag[first:last]
        side = jnp.concatenate(
            [
                jnp.concatenate([row_r[:, :half], -row_i[:, :half]], axis=1),
                jnp.concatenate([row_i[:, :half], row_r[:, :half]], axis=1),
            ],
            axis=0,
        )
        tile = first // LANES * LANES
        inside = (lane[first:last] >= first) & (lane[first:last] < last)
        minus_one = jnp.where(rank[first:last] == lane[first:last], -1.0, 0.0)
        row_r, row_i = sweep_rows(
            jnp.concatenate([row_r[:, tile : tile + LANES], jnp.where(inside, minus_one, row_r)], axis=1),
            jnp.concatenate([row_i[:, tile : tile + LANES], jnp.where(inside, 0.0, row_i)], axis=1),
            range(first - tile, last - tile),
            at_once,
        )
        row_r, row_i = row_r[:, LANES:], row_i[:, LANES:]
        update = deep_dot(side, jnp.concatenate([row_r, row_i], axis=0))
        own = (rank >= first) & (rank < last)
        gone = (lane >= first) & (lane < last)
        spread = lambda piece: jnp.concatenate([piece] * (half // pivots), axis=0)
        real = jnp.where(own, spread(row_r), jnp.where(gone, 0.0, real) - update[:half])
        imag = jnp.where(own, spread(row_i), jnp.where(gone, 0.0, imag) - update[half:])
    return real, imag


def beams_kernel(segments, snap_total, counts, *refs):
    grams, steer, blocks = refs[:segments], refs[segments], refs[segments + 1 : segments + 1 + sum(counts)]
    out = refs[-1]
    half = grams[0].shape[0]
    packed = sum(one[...] for one in grams) * (1.0 / snap_total)
    row = lax.broadcasted_iota(jnp.int32, (half, half), 0)
    column = lax.broadcasted_iota(jnp.int32, (half, half), 1)
    turned = packed.T
    real = jnp.where(row >= column, packed, turned)
    real = jnp.where(row == column, real + loading_level, real)
    imag = jnp.where(row < column, packed, jnp.where(row > column, -turned, 0.0))
    steer_r, steer_i = steer[:half], steer[half:]
    real, imag = eliminate(
        jnp.concatenate([real, steer_r], axis=1),
        jnp.concatenate([imag, steer_i], axis=1),
        PIVOTS,
        AT_ONCE,
    )
    solved_r, solved_i = real[:, half:], imag[:, half:]
    power = jnp.sum(steer_r * solved_r + steer_i * solved_i, axis=0, keepdims=True)
    scale = 1.0 / jnp.sqrt(power)
    weight_r, weight_i = (solved_r * scale).T, (solved_i * scale).T
    upper = jnp.concatenate([weight_r, weight_i], axis=1)
    lower = jnp.concatenate([-weight_i, weight_r], axis=1)
    mix = jnp.concatenate([upper, lower], axis=0).astype(bf16)
    count = steer.shape[1]
    mixed = jnp.dot(mix, stacked_rows(counts, blocks), preferred_element_type=f32).astype(bf16)
    out[0, 0] = mixed[:count]
    out[0, 1] = mixed[count:]


def beams(slot, slots, snap_total, grams, steer, blocks, earlier):
    snaps = sum(one.shape[2] for one in blocks[0])
    count = steer.shape[1]
    operands = [*grams, steer] + [one for block in blocks for one in block]
    specs = [pl.BlockSpec(memory_space=pltpu.VMEM)] * len(operands)
    aliases = {}
    if earlier is not None:
        aliases = {len(operands): 0}
        operands.append(earlier)
        specs.append(pl.BlockSpec(memory_space=pl.ANY))
    return pl.pallas_call(
        functools.partial(beams_kernel, len(grams), snap_total, [len(block) for block in blocks]),
        grid=(1,),
        in_specs=specs,
        out_specs=pl.BlockSpec((1, 2, count, snaps), lambda i: (slot, 0, 0, 0)),
        out_shape=jax.ShapeDtypeStruct((slots, 2, count, snaps), bf16),
        input_output_aliases=aliases,
        compiler_params=pltpu.CompilerParams(vmem_limit_bytes=BEAMS_VMEM),
        cost_estimate=pl.CostEstimate(flops=10**10, bytes_accessed=3 << 20, transcendentals=0),
        name="beams",
    )(*operands)


def partners(value, axis, distance):
    length = lax.axis_size(axis)
    return lax.ppermute(value, axis, [(i, i ^ distance) for i in range(length)])


def segment_sums(packed, hurried):
    length = lax.axis_size("seg")
    if hurried and length <= 4:
        return [packed] + [partners(packed, "seg", d) for d in range(1, length)]
    distance = 1
    while distance < length:
        packed = packed + partners(packed, "seg", distance)
        distance *= 2
    return [packed]


def steering(positions, beam_dirs, channel, channels):
    bearing = beam_dirs.astype(f32) * (full_turn / DIRS)
    frequency = 1.0 + channel.astype(f32) / channels
    path_delay = (
        positions[0][:, None] * jnp.cos(bearing)[None, :]
        + positions[1][:, None] * jnp.sin(bearing)[None, :]
    )
    phases = full_turn * frequency * path_delay
    return jnp.concatenate([jnp.cos(phases), jnp.sin(phases)], axis=0)


def after(value, earlier):
    return lax.optimization_barrier((value, earlier))


def on_device(voltages, filter_taps, positions, beam_dirs, chan_table):
    stations, width, snaps = voltages.shape
    channels = chan_table.shape[0]
    owners = lax.axis_size("stn")
    segments = lax.axis_size("seg")
    slots = channels // owners
    snap_total = snaps * segments
    near, far = list(range(1, owners // 2)), list(range(owners // 2, owners))
    halo = lax.ppermute(voltages[:, :, snaps - LANES :], "seg", [(i, i + 1) for i in range(segments - 1)])
    second = channelize(owners, 0, 1, "second", chan_table, voltages, filter_taps)
    late = {d: partners(second[d], "stn", d) for d in far}
    first = channelize(owners, 0, 1, "first", chan_table, voltages, filter_taps, halo, second[: owners // 2])
    early = {d: partners(first[d], "stn", d) for d in far}
    own, whole = first[0], {}
    for index, d in enumerate(near):
        value, late[far[index]] = after(first[d], late[far[index]])
        whole[d] = partners(value, "stn", d)
    blocks = [[own]] + [[whole[d]] for d in near] + [[early[d], late[d]] for d in far]
    result = None
    if slots > 1:
        halo, blocks[0][0] = after(halo, blocks[0][0])
        rest = channelize(owners, 1, slots - 1, "whole", chan_table, voltages, filter_taps, halo)
    if near:
        (positions, beam_dirs, chan_table), blocks[near[-1]][0] = after(
            (positions, beam_dirs, chan_table), blocks[near[-1]][0]
        )
    order = lax.axis_index("stn") ^ jnp.arange(owners, dtype=jnp.int32)
    places = positions.reshape(2, owners, stations)[:, order].reshape(2, owners * stations)
    chans = lax.dynamic_slice_in_dim(chan_table, lax.axis_index("stn") * slots, slots)
    for slot in range(slots):
        steer = steering(places, beam_dirs, chans[slot], channels)
        following = [None] * owners
        if slot + 1 < slots:
            sent = rest[slot * owners : (slot + 1) * owners]
            following[0] = [sent[0]]
            gates = [near[-1]] + far if near else far
            for index, d in enumerate(far):
                gate = blocks[gates[index]]
                value, gate[0] = after(sent[d], gate[0])
                following[d] = [partners(value, "stn", d)]
        grams = segment_sums(packed_gram(blocks), slot + 1 == slots)
        if slot + 1 < slots:
            for d in near:
                value, grams[0] = after(sent[d], grams[0])
                following[d] = [partners(value, "stn", d)]
        result = beams(slot, slots, snap_total, grams, steer, blocks, result)
        if slot + 1 < slots:
            blocks, result = after(following, result)
    return result


def solution(mesh):
    return jax.shard_map(
        on_device,
        mesh=mesh,
        in_specs=(P("stn", None, "seg"), P(), P(), P(), P()),
        out_specs=P("stn", None, None, "seg"),
        check_vma=False,
    )
```

time: 264 us -> 83.6 us (0.32)
  the two profiles are of different devices: /device:TPU:11 before, /device:TPU:0 now
where the time goes in v2:
time: 83.6 us; the launch traced here: 83.4 us
  starting transfers between devices  37.1 us (44%)
  Pallas kernels  31 us (37%)
  waiting for transfers between devices  10.7 us (13%)
  local copies, waits for them, and re-layouts  2.44 us (3%)
  between operations  1.53 us (2%)
    ppermute x23, starting transfers between devices, partners(): return lax.ppermute(value, axis, [(i, i ^ distance) for i in range(length)])  32.3 us
    pallas_call x3, Pallas kernels, channelize(): pl.pallas_call(functools.partial(channelize_kernel, owners, first_slot, s...  15.7 us
    pallas_call x2, Pallas kernels, beams(): pl.pallas_call(functools.partial(beams_kernel, len(grams), snap_total, [l...  14.4 us
    ppermute x23, waiting for transfers between devices, partners(): return lax.ppermute(value, axis, [(i, i ^ distance) for i in range(length)])  10.7 us
    ppermute x1, starting transfers between devices, on_device(): lax.ppermute(voltages[:, :, snaps - LANES:], 'seg', [(i, i + 1) for i in...  4.85 us
  transfers between devices with their start and end apart: 24, of which 8 were waited for; matrix products, arithmetic and copies ran while one was open for 3% of the time, Pallas kernels for 28%

profile of v2, /device:TPU:0, one launch (start us, length us, event | category | flops | bytes accessed | tf_op | source)
XLA Modules:
  0.0 83.4 jit_solution(879015401875986073)
XLA Ops:
  0.0 0.9 %slice.19 = bf16[16,32,128]{2,1,0:T(8,128)(2,1)S(1)} slice(bf16[16,32,2048]{2,1,0:T(8,128)(2,1)} %refs_1_.5), slice={[0:16], [0:32], [1920:2048]} | slice | bytes 262144 | tf_op jit(solution)/shard_map/slice | solution.py:351
  0.9 4.8 %collective-permute-start = (bf16[16,32,128]{2,1,0:T(8,128)(2,1)S(1)}, bf16[16,32,128]{2,1,0:T(8,128)(2,1)S(1)}, u32[]{:S(2)}, u32[]{:S(2)}) collective-permute-start(bf16[16,32,128]{2,1,0:T(8,128)(2,1)S(1)} %slice.19), channel_id=1, source_target_pairs={{0,1},{1,2},{2,3},{4,5},{5,6},{6,7},{8,9},{9,10},{10,11},{12,13},{... | collective-permute-start | bytes 393224 | tf_op jit(solution)/shard_map/ppermute | solution.py:351
  5.8 4.5 %channelize_second.1 = (bf16[2,16,1024]{2,1,0:T(8,128)(2,1)S(1)}, bf16[2,16,1024]{2,1,0:T(8,128)(2,1)S(1)}, bf16[2,16,1024]{2,1,0:T(8,128)(2,1)S(1)}, bf16[2,16,...) custom-call(s32[16]{0:T(128)} %refs_0_.5, ...), custom_call_target="tpu_custom_call" | custom-call | flops 4000000000 | bytes 3145728 | tf_op jit(solution)/shard_map/channelize_second/pallas_call | solution.py:121
  10.3 2.7 %collective-permute-start.1 = (bf16[2,16,1024]{2,1,0:T(8,128)(2,1)S(1)}, bf16[2,16,1024]{2,1,0:T(8,128)(2,1)S(1)}, u32[]{:S(2)}, u32[]{:S(2)}) collective-permute-start(bf16[2,16,1024]{2,1,0:T(8,128)(2,1)S(1)} %get-tuple-element.74), channel_id=1, source_target_pairs={{0,16},{4,20},{8,24},{12,28},{16,0},{20,4},{24,8},{28,12},{1,17},{... | collective-permute-start | bytes 196616 | tf_op jit(solution)/shard_map/ppermute | solution.py:314
  12.9 0.0 collective-permute-start.3
  12.9 2.8 %collective-permute-start.5 = (bf16[2,16,1024]{2,1,0:T(8,128)(2,1)S(1)}, bf16[2,16,1024]{2,1,0:T(8,128)(2,1)S(1)}, u32[]{:S(2)}, u32[]{:S(2)}) collective-permute-start(bf16[2,16,1024]{2,1,0:T(8,128)(2,1)S(1)} %get-tuple-element.81), channel_id=1, source_target_pairs={{0,24},{4,28},{8,16},{12,20},{16,8},{20,12},{24,0},{28,4},{1,25},{... | collective-permute-start | bytes 196616 | tf_op jit(solution)/shard_map/ppermute | solution.py:314
  15.8 0.0 collective-permute-done.refs_3_
  15.8 4.3 %channelize_first.1 = (bf16[2,16,2048]{2,1,0:T(8,128)(2,1)S(1)}, bf16[2,16,2048]{2,1,0:T(8,128)(2,1)S(1)}, bf16[2,16,2048]{2,1,0:T(8,128)(2,1)S(1)}, bf16[2,16,2...) custom-call(s32[16]{0:T(128)} %refs_0_.5, ...), custom_call_target="tpu_custom_call" | custom-call | flops 4000000000 | bytes 3145728 | tf_op jit(solution)/shard_map/channelize_first/pallas_call | solution.py:121
  20.1 4.3 %collective-permute-start.7 = (bf16[2,16,1024]{2,1,0:T(8,128)(2,1)S(1)}, bf16[2,16,1024]{2,1,0:T(8,128)(2,1)S(1)}, u32[]{:S(2)}, u32[]{:S(2)}) collective-permute-start(bf16[2,16,1024]{2,1,0:T(8,128)(2,1)S(1)} %get-tuple-element.86), channel_id=1, source_target_pairs={{0,16},{4,20},{8,24},{12,28},{16,0},{20,4},{24,8},{28,12},{1,17},{... | collective-permute-start | bytes 196616 | tf_op jit(solution)/shard_map/ppermute | solution.py:314
  24.4 0.5 collective-permute-start.9
  24.9 0.0 collective-permute-done.1.refs_5_.refs_7_
  24.9 2.4 %collective-permute-start.6 = (bf16[2,16,2048]{2,1,0:T(8,128)(2,1)S(1)}, bf16[2,16,2048]{2,1,0:T(8,128)(2,1)S(1)}, u32[]{:S(2)}, u32[]{:S(2)}) collective-permute-start(bf16[2,16,2048]{2,1,0:T(8,128)(2,1)S(1)} %get-tuple-element.82), channel_id=1, source_target_pairs={{0,12},{4,8},{8,4},{12,0},{16,28},{20,24},{24,20},{28,16},{1,13},{... | collective-permute-start | bytes 393224 | tf_op jit(solution)/shard_map/ppermute | solution.py:314
  27.4 6.9 %channelize_whole.1 = (bf16[2,16,2048]{2,1,0:T(8,128)(2,1)S(1)}, bf16[2,16,2048]{2,1,0:T(8,128)(2,1)S(1)}, bf16[2,16,2048]{2,1,0:T(8,128)(2,1)S(1)}, bf16[2,16,2...) custom-call(s32[16]{0:T(128)} %refs_0_.5, ...), custom_call_target="tpu_custom_call" | custom-call | flops 4000000000 | bytes 3145728 | tf_op jit(solution)/shard_map/channelize_whole/pallas_call | solution.py:121
  34.2 0.0 collective-permute-done.3.refs_7_.refs_9_
  34.2 0.4 collective-permute-start.11
  34.7 0.0 collective-permute-done.7.refs_4_.refs_6_
  34.7 3.2 %collective-permute-start.10 = (bf16[2,16,1024]{2,1,0:T(8,128)(2,1)S(1)}, bf16[2,16,1024]{2,1,0:T(8,128)(2,1)S(1)}, u32[]{:S(2)}, u32[]{:S(2)}) collective-permute-start(bf16[2,16,1024]{2,1,0:T(8,128)(2,1)S(1)} %get-tuple-element.97), channel_id=1, source_target_pairs={{0,28},{4,24},{8,20},{12,16},{16,12},{20,8},{24,4},{28,0},{1,29},{... | collective-permute-start | bytes 196616 | tf_op jit(solution)/shard_map/ppermute | solution.py:314
  37.8 0.1 collective-permute-start.2
  37.9 1.4 %collective-permute-start.20 = (bf16[2,16,2048]{2,1,0:T(8,128)(2,1)S(1)}, bf16[2,16,2048]{2,1,0:T(8,128)(2,1)S(1)}, u32[]{:S(2)}, u32[]{:S(2)}) collective-permute-start(bf16[2,16,2048]{2,1,0:T(8,128)(2,1)S(1)} %get-tuple-element.109), channel_id=1, source_target_pairs={{0,28},{4,24},{8,20},{12,16},{16,12},{20,8},{24,4},{28,0},{1,29},{... | collective-permute-start | bytes 393224 | tf_op jit(solution)/shard_map/ppermute | solution.py:314
  39.4 0.1 dynamic_slice.3
  39.4 0.6 fusion.9
  41.4 0.1 reshape.42
  41.5 0.6 gather_fusion
  42.1 0.1 mul.79
  42.2 0.1 mul.84
  42.3 2.6 %collective-permute-start.19 = (bf16[2,16,2048]{2,1,0:T(8,128)(2,1)S(1)}, bf16[2,16,2048]{2,1,0:T(8,128)(2,1)S(1)}, u32[]{:S(2)}, u32[]{:S(2)}) collective-permute-start(bf16[2,16,2048]{2,1,0:T(8,128)(2,1)S(1)} %get-tuple-element.108), channel_id=1, source_target_pairs={{0,24},{4,28},{8,16},{12,20},{16,8},{20,12},{24,0},{28,4},{1,25},{... | collective-permute-start | bytes 393224 | tf_op jit(solution)/shard_map/ppermute | solution.py:314
  44.9 0.1 collective-permute-done.4.refs_2_.refs_4_
  45.0 0.5 gram.2
  45.5 1.6 %collective-permute-start.12 = (f32[128,128]{1,0:T(8,128)S(1)}, f32[128,128]{1,0:T(8,128)S(1)}, u32[]{:S(2)}, u32[]{:S(2)}) collective-permute-start(f32[128,128]{1,0:T(8,128)S(1)} %gram.2), channel_id=1, source_target_pairs={{0,1},{1,0},{2,3},{3,2},{4,5},{5,4},{6,7},{7,6},{8,9},{9,8},{10,11... | collective-permute-start | bytes 196616 | tf_op jit(solution)/shard_map/ppermute | solution.py:314
  47.0 2.2 %collective-permute-start.17 = (bf16[2,16,2048]{2,1,0:T(8,128)(2,1)S(1)}, bf16[2,16,2048]{2,1,0:T(8,128)(2,1)S(1)}, u32[]{:S(2)}, u32[]{:S(2)}) collective-permute-start(bf16[2,16,2048]{2,1,0:T(8,128)(2,1)S(1)} %get-tuple-element.106), channel_id=1, source_target_pairs={{0,16},{4,20},{8,24},{12,28},{16,0},{20,4},{24,8},{28,12},{1,17},{... | collective-permute-start | bytes 393224 | tf_op jit(solution)/shard_map/ppermute | solution.py:314
  49.2 0.6 fusion.5
  49.8 1.5 %collective-permute-start.13 = (f32[128,128]{1,0:T(8,128)S(1)}, f32[128,128]{1,0:T(8,128)S(1)}, u32[]{:S(2)}, u32[]{:S(2)}) collective-permute-start(f32[128,128]{1,0:T(8,128)S(1)} %add.31), channel_id=1, source_target_pairs={{0,2},{1,3},{2,0},{3,1},{4,6},{5,7},{6,4},{7,5},{8,10},{9,11},{10,... | collective-permute-start | bytes 196616 | tf_op jit(solution)/shard_map/ppermute | solution.py:314
  51.4 2.8 %collective-permute-done.13 = f32[128,128]{1,0:T(8,128)S(1)} collective-permute-done((f32[128,128]{1,0:T(8,128)S(1)}, f32[128,128]{1,0:T(8,128)S(1)}, u32[]{:S(2)}, u32[]{:S(2)}) %collective-permute-start.13) | collective-permute-done | bytes 65568 | tf_op jit(solution)/shard_map/ppermute | solution.py:314
  54.2 0.2 collective-permute-start.16
  54.4 2.6 %collective-permute-start.15 = (bf16[2,16,2048]{2,1,0:T(8,128)(2,1)S(1)}, bf16[2,16,2048]{2,1,0:T(8,128)(2,1)S(1)}, u32[]{:S(2)}, u32[]{:S(2)}) collective-permute-start(bf16[2,16,2048]{2,1,0:T(8,128)(2,1)S(1)} %get-tuple-element.102), channel_id=1, source_target_pairs={{0,8},{4,12},{8,0},{12,4},{16,24},{20,28},{24,16},{28,20},{1,9},{5... | collective-permute-start | bytes 393224 | tf_op jit(solution)/shard_map/ppermute | solution.py:314
  57.0 0.2 collective-permute-start.14
  57.2 7.2 %beams.2.refs_13_ = bf16[2,2,128,2048]{3,2,1,0:T(8,128)(2,1)} custom-call(f32[128,128]{1,0:T(8,128)S(1)} %add.32.refs_0_, f32[256,128]{1,0:T(8,128)S(1)} %pad_maximum_fusion.refs_1_, bf16[2,16,2048]{2,1,0:T(8,128)(2,1)S(1)} %get-tuple-element.72.refs_0_.refs_2_, bf16[2,16,2048]{2,1,0:T(8,128)(2,1)S(1)} %collective-permute-done.2.refs_1_.refs_3_, ...), custom_call_target="tpu_custom_call" | custom-call | flops 10000000000 | bytes 3145728 | tf_op jit(solution)/shard_map/beams/pallas_call | solution.py:299
  64.4 0.9 %collective-permute-done.17.refs_4_.refs_9_ = bf16[2,16,2048]{2,1,0:T(8,128)(2,1)S(1)} collective-permute-done((bf16[2,16,2048]{2,1,0:T(8,128)(2,1)S(1)}, bf16[2,16,2048]{2,1,0:T(8,128)(2,1)S(1)}, u32[]{:S(2)}, u32[]{:S(2)}) %collective-permute-start.17) | collective-permute-done | bytes 131104 | tf_op jit(solution)/shard_map/ppermute | solution.py:314
  65.3 0.3 collective-permute-done.16.refs_3_.refs_8_
  65.6 2.9 %collective-permute-done.15.refs_2_.refs_7_ = bf16[2,16,2048]{2,1,0:T(8,128)(2,1)S(1)} collective-permute-done((bf16[2,16,2048]{2,1,0:T(8,128)(2,1)S(1)}, bf16[2,16,2048]{2,1,0:T(8,128)(2,1)S(1)}, u32[]{:S(2)}, u32[]{:S(2)}) %collective-permute-start.15) | collective-permute-done | bytes 131104 | tf_op jit(solution)/shard_map/ppermute | solution.py:314
  68.5 0.5 gram.3.refs_0_
  69.0 1.1 %collective-permute-start.23 = (f32[128,128]{1,0:T(8,128)S(1)}, f32[128,128]{1,0:T(8,128)S(1)}, u32[]{:S(2)}, u32[]{:S(2)}) collective-permute-start(f32[128,128]{1,0:T(8,128)S(1)} %gram.3.refs_0_), channel_id=1, source_target_pairs={{0,3},{1,2},{2,1},{3,0},{4,7},{5,6},{6,5},{7,4},{8,11},{9,10},{10,... | collective-permute-start | bytes 196616 | tf_op jit(solution)/shard_map/ppermute | solution.py:314
  70.1 1.9 %collective-permute-start.22 = (f32[128,128]{1,0:T(8,128)S(1)}, f32[128,128]{1,0:T(8,128)S(1)}, u32[]{:S(2)}, u32[]{:S(2)}) collective-permute-start(f32[128,128]{1,0:T(8,128)S(1)} %gram.3.refs_0_), channel_id=1, source_target_pairs={{0,2},{1,3},{2,0},{3,1},{4,6},{5,7},{6,4},{7,5},{8,10},{9,11},{10,... | collective-permute-start | bytes 196616 | tf_op jit(solution)/shard_map/ppermute | solution.py:314
  71.9 0.6 collective-permute-start.21
  72.5 2.2 %collective-permute-done.23.refs_3_ = f32[128,128]{1,0:T(8,128)S(1)} collective-permute-done((f32[128,128]{1,0:T(8,128)S(1)}, f32[128,128]{1,0:T(8,128)S(1)}, u32[]{:S(2)}, u32[]{:S(2)}) %collective-permute-start.23) | collective-permute-done | bytes 65568 | tf_op jit(solution)/shard_map/ppermute | solution.py:314
  74.7 0.6 collective-permute-done.22.refs_2_
  75.3 0.9 %collective-permute-done.21.refs_1_ = f32[128,128]{1,0:T(8,128)S(1)} collective-permute-done((f32[128,128]{1,0:T(8,128)S(1)}, f32[128,128]{1,0:T(8,128)S(1)}, u32[]{:S(2)}, u32[]{:S(2)}) %collective-permute-start.21) | collective-permute-done | bytes 65568 | tf_op jit(solution)/shard_map/ppermute | solution.py:314
  76.2 7.2 %beams.3 = bf16[2,2,128,2048]{3,2,1,0:T(8,128)(2,1)} custom-call(f32[128,128]{1,0:T(8,128)S(1)} %gram.3.refs_0_, f32[128,128]{1,0:T(8,128)S(1)} %collective-permute-done.21.refs_1_, f32[128,128]{1,0:T(8,128)S(1)} %collective-permute-done.22.refs_2_, f32[128,128]{1,0:T(8,128)S(1)} %collective-permute-done.23.refs_3_, ...), custom_call_target="tpu_custom_call", output_to_operand_aliasing={{}: (13, {})} | custom-call | flops 10000000000 | bytes 3145728 | tf_op jit(solution)/shard_map/beams/pallas_call | solution.py:299
  (30 shorter events, 0.2 us)
Async XLA Ops:
  0.9 14.9 %collective-permute-start = (bf16[16,32,128]{2,1,0:T(8,128)(2,1)S(1)}, bf16[16,32,128]{2,1,0:T(8,128)(2,1)S(1)}, u32[]{:S(2)}, u32[]{:S(2)}) collective-permute-start(bf16[16,32,128]{2,1,0:T(8,128)(2,1)S(1)} %slice.19), channel_id=1, source_target_pairs={{0,1},{1,2},{2,3},{4,5},{5,6},{6,7},{8,9},{9,10},{10,11},{12,13},{... | collective-permute-start | bytes 393224 | tf_op jit(solution)/shard_map/ppermute | solution.py:351
  10.3 14.7 %collective-permute-start.1 = (bf16[2,16,1024]{2,1,0:T(8,128)(2,1)S(1)}, bf16[2,16,1024]{2,1,0:T(8,128)(2,1)S(1)}, u32[]{:S(2)}, u32[]{:S(2)}) collective-permute-start(bf16[2,16,1024]{2,1,0:T(8,128)(2,1)S(1)} %get-tuple-element.74), channel_id=1, source_target_pairs={{0,16},{4,20},{8,24},{12,28},{16,0},{20,4},{24,8},{28,12},{1,17},{... | collective-permute-start | bytes 196616 | tf_op jit(solution)/shard_map/ppermute | solution.py:314
  12.9 21.3 %collective-permute-start.3 = (bf16[2,16,1024]{2,1,0:T(8,128)(2,1)S(1)}, bf16[2,16,1024]{2,1,0:T(8,128)(2,1)S(1)}, u32[]{:S(2)}, u32[]{:S(2)}) collective-permute-start(bf16[2,16,1024]{2,1,0:T(8,128)(2,1)S(1)} %get-tuple-element.77), channel_id=1, source_target_pairs={{0,20},{4,16},{8,28},{12,24},{16,4},{20,0},{24,12},{28,8},{1,21},{... | collective-permute-start | bytes 196616 | tf_op jit(solution)/shard_map/ppermute | solution.py:314
  12.9 7.2 %collective-permute-start.5 = (bf16[2,16,1024]{2,1,0:T(8,128)(2,1)S(1)}, bf16[2,16,1024]{2,1,0:T(8,128)(2,1)S(1)}, u32[]{:S(2)}, u32[]{:S(2)}) collective-permute-start(bf16[2,16,1024]{2,1,0:T(8,128)(2,1)S(1)} %get-tuple-element.81), channel_id=1, source_target_pairs={{0,24},{4,28},{8,16},{12,20},{16,8},{20,12},{24,0},{28,4},{1,25},{... | collective-permute-start | bytes 196616 | tf_op jit(solution)/shard_map/ppermute | solution.py:314
  20.1 14.5 %collective-permute-start.7 = (bf16[2,16,1024]{2,1,0:T(8,128)(2,1)S(1)}, bf16[2,16,1024]{2,1,0:T(8,128)(2,1)S(1)}, u32[]{:S(2)}, u32[]{:S(2)}) collective-permute-start(bf16[2,16,1024]{2,1,0:T(8,128)(2,1)S(1)} %get-tuple-element.86), channel_id=1, source_target_pairs={{0,16},{4,20},{8,24},{12,28},{16,0},{20,4},{24,8},{28,12},{1,17},{... | collective-permute-start | bytes 196616 | tf_op jit(solution)/shard_map/ppermute | solution.py:314
  24.4 13.4 %collective-permute-start.8 = (bf16[2,16,1024]{2,1,0:T(8,128)(2,1)S(1)}, bf16[2,16,1024]{2,1,0:T(8,128)(2,1)S(1)}, u32[]{:S(2)}, u32[]{:S(2)}) collective-permute-start(bf16[2,16,1024]{2,1,0:T(8,128)(2,1)S(1)} %get-tuple-element.90), channel_id=1, source_target_pairs={{0,20},{4,16},{8,28},{12,24},{16,4},{20,0},{24,12},{28,8},{1,21},{... | collective-permute-start | bytes 196616 | tf_op jit(solution)/shard_map/ppermute | solution.py:314
  24.4 14.9 %copy-start.1 = (s32[128]{0:T(128)S(1)}, s32[128]{0:T(128)}, u32[]{:S(2)}) copy-start(s32[128]{0:T(128)} %param.8) | copy-start | bytes 1540
  24.4 14.9 %copy-start.2 = (s32[16]{0:T(128)S(1)}, s32[16]{0:T(128)}, u32[]{:S(2)}) copy-start(s32[16]{0:T(128)} %refs_0_.5) | copy-start | bytes 196
  24.4 17.0 %copy-start = (f32[2,128]{1,0:T(2,128)S(1)}, f32[2,128]{1,0:T(2,128)}, u32[]{:S(2)}) copy-start(f32[2,128]{1,0:T(2,128)} %param.7) | copy-start | bytes 3076
  24.4 13.4 %collective-permute-start.9 = (bf16[2,16,1024]{2,1,0:T(8,128)(2,1)S(1)}, bf16[2,16,1024]{2,1,0:T(8,128)(2,1)S(1)}, u32[]{:S(2)}, u32[]{:S(2)}) collective-permute-start(bf16[2,16,1024]{2,1,0:T(8,128)(2,1)S(1)} %get-tuple-element.94), channel_id=1, source_target_pairs={{0,24},{4,28},{8,16},{12,20},{16,8},{20,12},{24,0},{28,4},{1,25},{... | collective-permute-start | bytes 196616 | tf_op jit(solution)/shard_map/ppermute | solution.py:314
  24.9 13.0 %collective-permute-start.6 = (bf16[2,16,2048]{2,1,0:T(8,128)(2,1)S(1)}, bf16[2,16,2048]{2,1,0:T(8,128)(2,1)S(1)}, u32[]{:S(2)}, u32[]{:S(2)}) collective-permute-start(bf16[2,16,2048]{2,1,0:T(8,128)(2,1)S(1)} %get-tuple-element.82), channel_id=1, source_target_pairs={{0,12},{4,8},{8,4},{12,0},{16,28},{20,24},{24,20},{28,16},{1,13},{... | collective-permute-start | bytes 393224 | tf_op jit(solution)/shard_map/ppermute | solution.py:314
  34.2 8.0 %collective-permute-start.11 = (bf16[2,16,1024]{2,1,0:T(8,128)(2,1)S(1)}, bf16[2,16,1024]{2,1,0:T(8,128)(2,1)S(1)}, u32[]{:S(2)}, u32[]{:S(2)}) collective-permute-start(bf16[2,16,1024]{2,1,0:T(8,128)(2,1)S(1)} %get-tuple-element.98), channel_id=1, source_target_pairs={{0,28},{4,24},{8,20},{12,16},{16,12},{20,8},{24,4},{28,0},{1,29},{... | collective-permute-start | bytes 196616 | tf_op jit(solution)/shard_map/ppermute | solution.py:314
  34.7 10.2 %collective-permute-start.10 = (bf16[2,16,1024]{2,1,0:T(8,128)(2,1)S(1)}, bf16[2,16,1024]{2,1,0:T(8,128)(2,1)S(1)}, u32[]{:S(2)}, u32[]{:S(2)}) collective-permute-start(bf16[2,16,1024]{2,1,0:T(8,128)(2,1)S(1)} %get-tuple-element.97), channel_id=1, source_target_pairs={{0,28},{4,24},{8,20},{12,16},{16,12},{20,8},{24,4},{28,0},{1,29},{... | collective-permute-start | bytes 196616 | tf_op jit(solution)/shard_map/ppermute | solution.py:314
  37.8 7.1 %collective-permute-start.4 = (bf16[2,16,2048]{2,1,0:T(8,128)(2,1)S(1)}, bf16[2,16,2048]{2,1,0:T(8,128)(2,1)S(1)}, u32[]{:S(2)}, u32[]{:S(2)}) collective-permute-start(bf16[2,16,2048]{2,1,0:T(8,128)(2,1)S(1)} %get-tuple-element.78), channel_id=1, source_target_pairs={{0,8},{4,12},{8,0},{12,4},{16,24},{20,28},{24,16},{28,20},{1,9},{5... | collective-permute-start | bytes 393224 | tf_op jit(solution)/shard_map/ppermute | solution.py:314
  37.8 7.1 %collective-permute-start.2 = (bf16[2,16,2048]{2,1,0:T(8,128)(2,1)S(1)}, bf16[2,16,2048]{2,1,0:T(8,128)(2,1)S(1)}, u32[]{:S(2)}, u32[]{:S(2)}) collective-permute-start(bf16[2,16,2048]{2,1,0:T(8,128)(2,1)S(1)} %get-tuple-element.75), channel_id=1, source_target_pairs={{0,4},{4,0},{8,12},{12,8},{16,20},{20,16},{24,28},{28,24},{1,5},{5... | collective-permute-start | bytes 393224 | tf_op jit(solution)/shard_map/ppermute | solution.py:314
  37.9 16.5 %collective-permute-start.20 = (bf16[2,16,2048]{2,1,0:T(8,128)(2,1)S(1)}, bf16[2,16,2048]{2,1,0:T(8,128)(2,1)S(1)}, u32[]{:S(2)}, u32[]{:S(2)}) collective-permute-start(bf16[2,16,2048]{2,1,0:T(8,128)(2,1)S(1)} %get-tuple-element.109), channel_id=1, source_target_pairs={{0,28},{4,24},{8,20},{12,16},{16,12},{20,8},{24,4},{28,0},{1,29},{... | collective-permute-start | bytes 393224 | tf_op jit(solution)/shard_map/ppermute | solution.py:314
  42.3 14.7 %collective-permute-start.19 = (bf16[2,16,2048]{2,1,0:T(8,128)(2,1)S(1)}, bf16[2,16,2048]{2,1,0:T(8,128)(2,1)S(1)}, u32[]{:S(2)}, u32[]{:S(2)}) collective-permute-start(bf16[2,16,2048]{2,1,0:T(8,128)(2,1)S(1)} %get-tuple-element.108), channel_id=1, source_target_pairs={{0,24},{4,28},{8,16},{12,20},{16,8},{20,12},{24,0},{28,4},{1,25},{... | collective-permute-start | bytes 393224 | tf_op jit(solution)/shard_map/ppermute | solution.py:314
  44.9 19.5 %collective-permute-start.18 = (bf16[2,16,2048]{2,1,0:T(8,128)(2,1)S(1)}, bf16[2,16,2048]{2,1,0:T(8,128)(2,1)S(1)}, u32[]{:S(2)}, u32[]{:S(2)}) collective-permute-start(bf16[2,16,2048]{2,1,0:T(8,128)(2,1)S(1)} %get-tuple-element.107), channel_id=1, source_target_pairs={{0,20},{4,16},{8,28},{12,24},{16,4},{20,0},{24,12},{28,8},{1,21},{... | collective-permute-start | bytes 393224 | tf_op jit(solution)/shard_map/ppermute | solution.py:314
  45.5 4.4 %collective-permute-start.12 = (f32[128,128]{1,0:T(8,128)S(1)}, f32[128,128]{1,0:T(8,128)S(1)}, u32[]{:S(2)}, u32[]{:S(2)}) collective-permute-start(f32[128,128]{1,0:T(8,128)S(1)} %gram.2), channel_id=1, source_target_pairs={{0,1},{1,0},{2,3},{3,2},{4,5},{5,4},{6,7},{7,6},{8,9},{9,8},{10,11... | collective-permute-start | bytes 196616 | tf_op jit(solution)/shard_map/ppermute | solution.py:314
  47.0 18.3 %collective-permute-start.17 = (bf16[2,16,2048]{2,1,0:T(8,128)(2,1)S(1)}, bf16[2,16,2048]{2,1,0:T(8,128)(2,1)S(1)}, u32[]{:S(2)}, u32[]{:S(2)}) collective-permute-start(bf16[2,16,2048]{2,1,0:T(8,128)(2,1)S(1)} %get-tuple-element.106), channel_id=1, source_target_pairs={{0,16},{4,20},{8,24},{12,28},{16,0},{20,4},{24,8},{28,12},{1,17},{... | collective-permute-start | bytes 393224 | tf_op jit(solution)/shard_map/ppermute | solution.py:314
  49.8 4.3 %collective-permute-start.13 = (f32[128,128]{1,0:T(8,128)S(1)}, f32[128,128]{1,0:T(8,128)S(1)}, u32[]{:S(2)}, u32[]{:S(2)}) collective-permute-start(f32[128,128]{1,0:T(8,128)S(1)} %add.31), channel_id=1, source_target_pairs={{0,2},{1,3},{2,0},{3,1},{4,6},{5,7},{6,4},{7,5},{8,10},{9,11},{10,... | collective-permute-start | bytes 196616 | tf_op jit(solution)/shard_map/ppermute | solution.py:314
  54.2 11.4 %collective-permute-start.16 = (bf16[2,16,2048]{2,1,0:T(8,128)(2,1)S(1)}, bf16[2,16,2048]{2,1,0:T(8,128)(2,1)S(1)}, u32[]{:S(2)}, u32[]{:S(2)}) collective-permute-start(bf16[2,16,2048]{2,1,0:T(8,128)(2,1)S(1)} %get-tuple-element.105), channel_id=1, source_target_pairs={{0,12},{4,8},{8,4},{12,0},{16,28},{20,24},{24,20},{28,16},{1,13},{... | collective-permute-start | bytes 393224 | tf_op jit(solution)/shard_map/ppermute | solution.py:314
  54.4 14.1 %collective-permute-start.15 = (bf16[2,16,2048]{2,1,0:T(8,128)(2,1)S(1)}, bf16[2,16,2048]{2,1,0:T(8,128)(2,1)S(1)}, u32[]{:S(2)}, u32[]{:S(2)}) collective-permute-start(bf16[2,16,2048]{2,1,0:T(8,128)(2,1)S(1)} %get-tuple-element.102), channel_id=1, source_target_pairs={{0,8},{4,12},{8,0},{12,4},{16,24},{20,28},{24,16},{28,20},{1,9},{5... | collective-permute-start | bytes 393224 | tf_op jit(solution)/shard_map/ppermute | solution.py:314
  57.0 11.5 %collective-permute-start.14 = (bf16[2,16,2048]{2,1,0:T(8,128)(2,1)S(1)}, bf16[2,16,2048]{2,1,0:T(8,128)(2,1)S(1)}, u32[]{:S(2)}, u32[]{:S(2)}) collective-permute-start(bf16[2,16,2048]{2,1,0:T(8,128)(2,1)S(1)} %get-tuple-element.99), channel_id=1, source_target_pairs={{0,4},{4,0},{8,12},{12,8},{16,20},{20,16},{24,28},{28,24},{1,5},{5... | collective-permute-start | bytes 393224 | tf_op jit(solution)/shard_map/ppermute | solution.py:314
  69.0 5.7 %collective-permute-start.23 = (f32[128,128]{1,0:T(8,128)S(1)}, f32[128,128]{1,0:T(8,128)S(1)}, u32[]{:S(2)}, u32[]{:S(2)}) collective-permute-start(f32[128,128]{1,0:T(8,128)S(1)} %gram.3.refs_0_), channel_id=1, source_target_pairs={{0,3},{1,2},{2,1},{3,0},{4,7},{5,6},{6,5},{7,4},{8,11},{9,10},{10,... | collective-permute-start | bytes 196616 | tf_op jit(solution)/shard_map/ppermute | solution.py:314
  70.1 5.2 %collective-permute-start.22 = (f32[128,128]{1,0:T(8,128)S(1)}, f32[128,128]{1,0:T(8,128)S(1)}, u32[]{:S(2)}, u32[]{:S(2)}) collective-permute-start(f32[128,128]{1,0:T(8,128)S(1)} %gram.3.refs_0_), channel_id=1, source_target_pairs={{0,2},{1,3},{2,0},{3,1},{4,6},{5,7},{6,4},{7,5},{8,10},{9,11},{10,... | collective-permute-start | bytes 196616 | tf_op jit(solution)/shard_map/ppermute | solution.py:314
  71.9 4.3 %collective-permute-start.21 = (f32[128,128]{1,0:T(8,128)S(1)}, f32[128,128]{1,0:T(8,128)S(1)}, u32[]{:S(2)}, u32[]{:S(2)}) collective-permute-start(f32[128,128]{1,0:T(8,128)S(1)} %gram.3.refs_0_), channel_id=1, source_target_pairs={{0,1},{1,0},{2,3},{3,2},{4,5},{5,4},{6,7},{7,6},{8,9},{9,8},{10,11... | collective-permute-start | bytes 196616 | tf_op jit(solution)/shard_map/ppermute | solution.py:314

commit v3 on v2

v3 whole, which is shorter than its diff:
```python
import functools
import math

import jax
import jax.numpy as jnp
from jax import lax
from jax.experimental import pallas as pl
from jax.experimental.pallas import tpu as pltpu
from jax.sharding import PartitionSpec as P

DIRS = 360
LANES = 128
GROUP = 8
PIVOTS = 16
QUICK = pl.CostEstimate(flops=1000, bytes_accessed=1000, transcendentals=0)
AT_ONCE = 4
VMEM_BYTES = 16 << 20
GRAM_VMEM = 8 << 20
BEAMS_VMEM = 12 << 20

loading_level = 0.1
full_turn = 2.0 * math.pi
NN = (((1,), (0,)), ((), ()))
NT = (((1,), (1,)), ((), ()))
TN = (((0,), (0,)), ((), ()))
f32, bf16 = jnp.float32, jnp.bfloat16


def split_in_two(value):
    high = value.astype(bf16)
    return high, (value - high.astype(f32)).astype(bf16)


def merged_rows(pieces):
    if all(piece.shape[0] % 16 == 0 for piece in pieces):
        return jnp.concatenate(pieces, axis=0)
    return jnp.concatenate([piece.astype(f32) for piece in pieces], axis=0).astype(bf16)


def dft_rows(channels, width):
    shape = (2 * len(channels), GROUP * width)
    row = lax.broadcasted_iota(jnp.int32, shape, 0)
    lane = lax.broadcasted_iota(jnp.int32, shape, 1)
    channel = jnp.zeros(shape, jnp.int32)
    for index, one in enumerate(channels):
        channel = jnp.where(row // 2 == index, one, channel)
    angle = lax.rem(channel * lax.rem(lane, width), width).astype(f32) * (full_turn / width)
    values = jnp.where(row % 2 == 0, jnp.cos(angle), -jnp.sin(angle))
    shape = (GROUP, GROUP * width)
    own = lax.broadcasted_iota(jnp.int32, shape, 1) // width == lax.broadcasted_iota(jnp.int32, shape, 0)
    spread = [jnp.where(own, jnp.broadcast_to(values[i : i + 1], shape), 0.0) for i in range(2 * len(channels))]
    return jnp.concatenate(spread, axis=0)


def steering(me, order, positions, beam_dirs, channel, channels):
    owners = len(order)
    stations = positions.shape[1] // owners
    columns = jnp.concatenate([positions, jnp.zeros((6, positions.shape[1]), f32)], axis=0).T
    span = 1
    while span < owners:
        parts = [columns[i * stations : (i + 1) * stations] for i in range(owners)]
        turned = jnp.concatenate([parts[i ^ span] for i in range(owners)], axis=0)
        columns = jnp.where((me & span) != 0, turned, columns)
        span *= 2
    columns = jnp.concatenate([columns[d * stations : (d + 1) * stations] for d in order], axis=0)
    bearing = beam_dirs.astype(f32) * (full_turn / DIRS)
    frequency = 1.0 + channel.astype(f32) / channels
    path_delay = columns[:, 0:1] * jnp.cos(bearing) + columns[:, 1:2] * jnp.sin(bearing)
    turns = frequency * path_delay
    phases = full_turn * (turns - jnp.round(turns))
    return jnp.concatenate([jnp.cos(phases), jnp.sin(phases)], axis=0)


def channelize_kernel(owners, slots, part, order, places, joined, other_count, *refs):
    count = owners * slots
    has_halo = part != "second"
    chans_in, volts, taps_in = refs[:3]
    others = refs[3 + 3 * has_halo : 3 + 3 * has_halo + other_count]
    outs = refs[3 + 3 * has_halo + other_count : len(refs) - 10]
    dft, held, high, low, chans, taps, sems, chans_sem, taps_sem, halo_sem = refs[-10:]
    stations, width, snaps = volts.shape
    chunk = held.shape[2] - LANES
    tap_count = taps.shape[0]
    step = tap_count // 2
    rows = 2 * GROUP
    half = count * rows
    pieces = sems.shape[0]
    piece = stations // pieces
    small = [pltpu.make_async_copy(chans_in, chans, chans_sem), pltpu.make_async_copy(taps_in, taps, taps_sem)]
    if has_halo:
        small.append(pltpu.make_async_copy(refs[3], held.at[:, :, :LANES], halo_sem))
    copies = []
    for index in range(pieces):
        members = pl.ds(index * piece, piece)
        if has_halo:
            source, target = volts.at[members, :, :chunk], held.at[members, :, LANES:]
        else:
            source, target = volts.at[members, :, snaps - chunk - LANES :], held.at[members]
        copies.append(pltpu.make_async_copy(source, target, sems.at[index]))
    for copy in small + copies:
        copy.start()
    for copy in small:
        copy.wait()

    me = lax.axis_index("stn")
    table = dft_rows([chans[(me ^ d) * slots + slot] for slot in range(slots) for d in range(owners)], width)
    dft[:half], dft[half:] = split_in_two(table)
    columns = taps[...].T
    tap = [jnp.broadcast_to(columns[:, m : m + 1], (width, chunk + LANES)) for m in range(tap_count)]
    results = []
    for station in range(stations):
        if station % piece == 0:
            copies[station // piece].wait()
        now = held[station]
        shifted = [(pltpu.roll(now, m, axis=1) if m else now).astype(f32) for m in range(step)]
        near = sum(tap[m] * shifted[m] for m in range(step))
        far = sum(tap[step + m] * shifted[m] for m in range(step))
        filtered = (near + pltpu.roll(far, step, axis=1))[:, LANES:]
        member = station % GROUP
        high[pl.ds(member * width, width), :], low[pl.ds(member * width, width), :] = split_in_two(filtered)
        if member == GROUP - 1:
            both = jnp.dot(dft[...], high[...], preferred_element_type=f32)
            cross = jnp.dot(dft[:half], low[...], preferred_element_type=f32)
            results.append(both[:half] + (both[half:] + cross))
    for index in range(count):
        slot, d = divmod(index, owners)
        number, entry = places[slot, d]
        target = outs[number].at[entry]
        for real in range(2):
            first = index * rows + real * GROUP
            merged = jnp.concatenate([one[first : first + GROUP] for one in results], axis=0)
            target[real, :, :chunk] = merged.astype(bf16)
        if (slot, d) in joined:
            at, inside = joined[slot, d]
            target[:, :, chunk:] = others[at][inside]
    if not has_halo:
        outs[-1][...] = held[:, :, chunk:]
    else:
        for slot in range(slots):
            channel = chans[me * slots + slot]
            outs[-1][slot] = steering(me, order, refs[4][...], refs[5][...], channel, owners * slots)


def channelize(slots, part, order, layout, chans, volts, taps, halo=None, positions=None, beam_dirs=None, joined=None):
    stations, width, snaps = volts.shape
    owners = len(order)
    count = owners * slots
    chunk = snaps // 2
    pieces = max(stations // 4, 1)
    joined = joined or {}
    others = []
    for array, _ in joined.values():
        if not any(array is one for one in others):
            others.append(array)
    number_of = lambda array: next(i for i, one in enumerate(others) if one is array)
    joined = {key: (number_of(array), entry) for key, (array, entry) in joined.items()}
    places, out_shape = {}, []
    for number, keys in enumerate(layout):
        for entry, key in enumerate(keys):
            places[key] = (number, entry)
        length = snaps if keys[0] in joined else chunk
        out_shape.append(jax.ShapeDtypeStruct((len(keys), 2, stations, length), bf16))
    if halo is None:
        out_shape.append(jax.ShapeDtypeStruct((stations, width, LANES), bf16))
    else:
        out_shape.append(jax.ShapeDtypeStruct((slots, 2 * owners * stations, beam_dirs.shape[0]), f32))
    operands = [pltpu.with_memory_space_constraint(one, pltpu.HBM) for one in (chans, volts, taps)]
    operands += ([] if halo is None else [halo, positions, beam_dirs[None, :]]) + others
    return pl.pallas_call(
        functools.partial(channelize_kernel, owners, slots, part, order, places, joined, len(others)),
        in_specs=[pl.BlockSpec(memory_space=pltpu.HBM)] * 3
        + [pl.BlockSpec(memory_space=pl.ANY)] * (halo is not None)
        + [pl.BlockSpec(memory_space=pltpu.VMEM)] * (len(operands) - 3 - (halo is not None)),
        out_specs=[pl.BlockSpec(memory_space=pltpu.VMEM)] * len(out_shape),
        out_shape=out_shape,
        scratch_shapes=[
            pltpu.VMEM((4 * count * GROUP, GROUP * width), bf16),
            pltpu.VMEM((stations, width, chunk + LANES), bf16),
            pltpu.VMEM((GROUP * width, chunk), bf16),
            pltpu.VMEM((GROUP * width, chunk), bf16),
            pltpu.SMEM(chans.shape, jnp.int32),
            pltpu.VMEM(taps.shape, f32),
            pltpu.SemaphoreType.DMA((pieces,)),
            pltpu.SemaphoreType.DMA(()),
            pltpu.SemaphoreType.DMA(()),
            pltpu.SemaphoreType.DMA(()),
        ],
        compiler_params=pltpu.CompilerParams(vmem_limit_bytes=VMEM_BYTES),
        cost_estimate=QUICK,
        name="channelize_" + part,
    )(*operands)


def flattened(blocks):
    arrays, numbered = [], []
    for block in blocks:
        numbered.append([])
        for array, entry in block:
            found = [i for i, one in enumerate(arrays) if one is array]
            if not found:
                found = [len(arrays)]
                arrays.append(array)
            numbered[-1].append((found[0], entry))
    return arrays, numbered


def stacked_rows(blocks, refs):
    rows = []
    for part in range(2):
        for block in blocks:
            rows.append(jnp.concatenate([refs[at][entry, part] for at, entry in block], axis=1))
    return merged_rows(rows)


def first_gram_kernel(blocks, *refs):
    out = refs[-1]
    slots, half, wide = out.shape
    row = lax.broadcasted_iota(jnp.int32, (half, half), 0)
    column = lax.broadcasted_iota(jnp.int32, (half, half), 1)
    for slot in range(slots):
        stacked = stacked_rows(blocks[slot], refs[:-1])
        gram = lax.dot_general(stacked, stacked, NT, preferred_element_type=f32)
        sym_part = gram[:half, :half] + gram[half:, half:]
        skew_part = gram[half:, :half] - gram[:half, half:]
        packed = jnp.where(row >= column, sym_part, skew_part)
        out[slot] = jnp.concatenate([packed, jnp.zeros((half, wide - half), f32)], axis=1)


def last_gram_kernel(blocks, count, *refs):
    out = refs[-1]
    slots, double, half = out.shape
    rows = double // 2
    for slot in range(slots):
        stacked = stacked_rows(blocks[slot], refs[:-1])
        ours = stacked_rows(blocks[slot][-count:], refs[:-1])
        gram = lax.dot_general(ours, stacked, NT, preferred_element_type=f32)
        out[slot, :rows] = gram[:rows, :half] + gram[rows:, half:]
        out[slot, rows:] = gram[rows:, :half] - gram[:rows, half:]


def gram_call(kernel, blocks, shape, name):
    operands, numbered = flattened([block for one in blocks for block in one])
    per_slot = len(blocks[0])
    numbered = [numbered[i * per_slot : (i + 1) * per_slot] for i in range(len(blocks))]
    return pl.pallas_call(
        functools.partial(kernel, numbered),
        in_specs=[pl.BlockSpec(memory_space=pltpu.VMEM)] * len(operands),
        out_specs=pl.BlockSpec(memory_space=pltpu.VMEM),
        out_shape=jax.ShapeDtypeStruct((len(blocks), *shape), f32),
        compiler_params=pltpu.CompilerParams(vmem_limit_bytes=GRAM_VMEM),
        cost_estimate=QUICK,
        name=name,
    )(*operands)


def first_gram(blocks, stations, half):
    return gram_call(first_gram_kernel, blocks, (stations, half), "first_gram")


def last_gram(blocks, count, stations, half):
    kernel = lambda numbered, *refs: last_gram_kernel(numbered, count, *refs)
    return gram_call(kernel, blocks, (2 * stations, half), "last_gram")


def dot(left, right, dims=NN):
    return lax.dot_general(left, right, dims, precision=lax.Precision.HIGHEST, preferred_element_type=f32)


def split_in_three(value):
    high, rest = value.astype(bf16), value
    rest = rest - high.astype(f32)
    middle = rest.astype(bf16)
    return high, middle, (rest - middle.astype(f32)).astype(bf16)


def deep_dot(left, right):
    a, b = split_in_three(left), split_in_three(right)
    left = jnp.concatenate([a[0], a[0], a[1], a[1], a[0], a[2]], axis=0)
    right = jnp.concatenate([b[0], b[1], b[0], b[1], b[2], b[0]], axis=0)
    return lax.dot_general(left, right, TN, preferred_element_type=f32)


def sweep_rows(systems, lanes, at_once):
    count, width = systems[0][0].shape
    narrow = (count, LANES)
    index, index_wide = (lax.broadcasted_iota(jnp.int32, shape, 0) for shape in (narrow, (count, width)))
    repeated = lambda value: jnp.concatenate([value] * (width // LANES), axis=1)
    rows = list(systems)
    for start in range(0, count, at_once):
        fetched = lanes[start : start + at_once]
        columns = [
            [tuple(jnp.broadcast_to(part[:, lane : lane + 1], narrow) for part in row) for lane in fetched] for row in rows
        ]
        for j in range(len(fetched)):
            step = start + j
            spread = lambda value: jnp.broadcast_to(value[step : step + 1], value.shape)

            def swept(value, here, a, b, scale):
                real, imag = value
                pick_r, pick_i = spread(real) * scale, spread(imag) * scale
                return (
                    jnp.where(here, pick_r, real - (a * pick_r - b * pick_i)),
                    jnp.where(here, pick_i, imag - (a * pick_i + b * pick_r)),
                )

            scales = [1.0 / spread(column[j][0]) for column in columns]
            for later in range(j + 1, len(fetched)):
                for column, scale in zip(columns, scales):
                    column[later] = swept(column[later], index == step, *column[j], scale)
            for number, (column, scale) in enumerate(zip(columns, scales)):
                a, b = column[j]
                rows[number] = swept(rows[number], index_wide == step, repeated(a), repeated(b), repeated(scale))
    return rows


def eliminate(systems, start, stop, pivots, at_once):
    half = systems[0][0].shape[0]
    shape = systems[0][0].shape
    rank = lax.broadcasted_iota(jnp.int32, shape, 0)
    lane = lax.broadcasted_iota(jnp.int32, shape, 1)
    for first in range(start, stop, pivots):
        last = first + pivots
        tile = first // LANES * LANES
        inside = (lane[first:last] >= first) & (lane[first:last] < last)
        minus_one = jnp.where(rank[first:last] == lane[first:last], -1.0, 0.0)
        sides, rows = [], []
        for real, imag in systems:
            row_r, row_i = real[first:last], imag[first:last]
            upper = jnp.concatenate([row_r[:, :half], -row_i[:, :half]], axis=1)
            lower = jnp.concatenate([row_i[:, :half], row_r[:, :half]], axis=1)
            sides.append(jnp.concatenate([upper, lower], axis=0))
            rows.append((
                jnp.concatenate([row_r[:, tile : tile + LANES], jnp.where(inside, minus_one, row_r)], axis=1),
                jnp.concatenate([row_i[:, tile : tile + LANES], jnp.where(inside, 0.0, row_i)], axis=1),
            ))
        rows = sweep_rows(rows, range(first - tile, last - tile), at_once)
        own = (rank >= first) & (rank < last)
        gone = (lane >= first) & (lane < last)
        spread = lambda piece: jnp.concatenate([piece] * (half // pivots), axis=0)
        results = []
        for (real, imag), side, (row_r, row_i) in zip(systems, sides, rows):
            row_r, row_i = row_r[:, LANES:], row_i[:, LANES:]
            update = deep_dot(side, jnp.concatenate([row_r, row_i], axis=0))
            results.append((
                jnp.where(own, spread(row_r), jnp.where(gone, 0.0, real) - update[:half]),
                jnp.where(own, spread(row_i), jnp.where(gone, 0.0, imag) - update[half:]),
            ))
        systems = results
    return systems


def first_solve_kernel(segments, snap_total, *refs):
    grams, steer, out = refs[:segments], refs[segments], refs[-1]
    slots, stations, half = grams[0].shape
    row = lax.broadcasted_iota(jnp.int32, (half, half), 0)
    column = lax.broadcasted_iota(jnp.int32, (half, half), 1)
    systems = []
    for slot in range(slots):
        packed = sum(one[slot] for one in grams) * (1.0 / snap_total)
        if stations < half:
            packed = jnp.concatenate([packed, jnp.zeros((half - stations, half), f32)], axis=0)
        turned = packed.T
        real = jnp.where(row >= column, packed, turned)
        real = jnp.where((row == column) & (row < stations), real + loading_level, real)
        imag = jnp.where(row < column, packed, jnp.where(row > column, -turned, 0.0))
        known = row < stations
        systems.append((
            jnp.concatenate([real, jnp.where(known, steer[slot, :half], 0.0)], axis=1),
            jnp.concatenate([imag, jnp.where(known, steer[slot, half:], 0.0)], axis=1),
        ))
    for slot, (real, imag) in enumerate(eliminate(systems, 0, stations, math.gcd(stations, PIVOTS), AT_ONCE)):
        out[slot, 0] = jnp.concatenate([real, systems[slot][0][:, :half]], axis=1)
        out[slot, 1] = jnp.concatenate([imag, systems[slot][1][:, :half]], axis=1)


def first_solve(snap_total, grams, steer):
    slots, _, count = steer.shape
    half = grams[0].shape[2]
    return pl.pallas_call(
        functools.partial(first_solve_kernel, len(grams), snap_total),
        in_specs=[pl.BlockSpec(memory_space=pltpu.VMEM)] * (len(grams) + 1),
        out_specs=pl.BlockSpec(memory_space=pltpu.VMEM),
        out_shape=jax.ShapeDtypeStruct((slots, 2, half, 2 * half + count), f32),
        compiler_params=pltpu.CompilerParams(vmem_limit_bytes=BEAMS_VMEM),
        cost_estimate=QUICK,
        name="first_solve",
    )(*grams, steer)


def complex_rows(real, imag):
    upper = jnp.concatenate([real, -imag], axis=1)
    return jnp.concatenate([upper, jnp.concatenate([imag, real], axis=1)], axis=0)


def joined_system(swept_r, swept_i, rows_r, rows_i, steer_r, steer_i, known):
    count, half = rows_r.shape
    end = half + steer_r.shape[1]
    lane = lax.broadcasted_iota(jnp.int32, rows_r.shape, 1)
    cross_r, cross_i = jnp.where(lane < known, rows_r, 0.0), jnp.where(lane < known, rows_i, 0.0)
    stacked = lambda first, last: jnp.concatenate([swept_r[:, first:last], swept_i[:, first:last]], axis=0)
    inverse, matrix = stacked(0, half), stacked(end, end + half)
    guess = -dot(complex_rows(cross_r, cross_i), inverse)
    rest = jnp.concatenate([cross_r, cross_i], axis=0) - dot(complex_rows(guess[:count], guess[count:]), matrix)
    guess = guess - dot(complex_rows(rest[:count], rest[count:]), inverse)
    turn_r, turn_i = guess[:count], guess[count:]
    ahead = lax.broadcasted_iota(jnp.int32, steer_r.shape, 0) < known
    first_steer = jnp.concatenate([jnp.where(ahead, steer_r, 0.0), jnp.where(ahead, steer_i, 0.0)], axis=0)
    taken = dot(complex_rows(turn_r, turn_i), first_steer)
    back_r, back_i = steer_r[known:] - taken[:count], steer_i[known:] - taken[count:]
    left = jnp.concatenate(
        [jnp.concatenate([turn_r, turn_i], axis=1), jnp.concatenate([turn_i, -turn_r], axis=1)], axis=0
    )
    right = jnp.concatenate([jnp.zeros((known, 2 * half), f32), jnp.concatenate([cross_r, cross_i], axis=1)], axis=0)
    inner = dot(left, right, NT)
    rows_r = jnp.where(lane < known, turn_r, rows_r - inner[:count])
    rows_i = jnp.where(lane < known, turn_i, rows_i - inner[count:])
    real = jnp.concatenate([swept_r[:known, :end], jnp.concatenate([rows_r, back_r], axis=1)], axis=0)
    imag = jnp.concatenate([swept_i[:known, :end], jnp.concatenate([rows_i, back_i], axis=1)], axis=0)
    return real, imag


def beams_kernel(segments, snap_total, blocks, *refs):
    grams, swept, steer = refs[:segments], refs[segments], refs[segments + 1]
    arrays, out, mix = refs[segments + 2 : -2], refs[-2], refs[-1]
    slots, double, half = grams[0].shape
    known = half - double // 2
    count = steer.shape[2]

    @pl.when(pl.program_id(0) == 0)
    def _():
        systems = []
        shape = (double // 2, half)
        diagonal = lax.broadcasted_iota(jnp.int32, shape, 0) + known == lax.broadcasted_iota(jnp.int32, shape, 1)
        for slot in range(slots):
            rows = sum(one[slot] for one in grams) * (1.0 / snap_total)
            rows_r, rows_i = rows[: double // 2], rows[double // 2 :]
            rows_r = jnp.where(diagonal, rows_r + loading_level, rows_r)
            steer_r, steer_i = steer[slot, :half], steer[slot, half:]
            systems.append(joined_system(swept[slot, 0], swept[slot, 1], rows_r, rows_i, steer_r, steer_i, known))
        for slot, (real, imag) in enumerate(eliminate(systems, known, half, math.gcd(known, PIVOTS), AT_ONCE)):
            solved_r, solved_i = real[:, half:], imag[:, half:]
            power = jnp.sum(steer[slot, :half] * solved_r + steer[slot, half:] * solved_i, axis=0, keepdims=True)
            scale = 1.0 / jnp.sqrt(power)
            weight_r, weight_i = (solved_r * scale).T, (solved_i * scale).T
            mix[slot, :count] = jnp.concatenate([weight_r, weight_i], axis=1).astype(bf16)
            mix[slot, count:] = jnp.concatenate([-weight_i, weight_r], axis=1).astype(bf16)

    for slot in range(slots):

        @pl.when(pl.program_id(0) == slot)
        def _():
            mixed = jnp.dot(mix[slot], stacked_rows(blocks[slot], arrays), preferred_element_type=f32).astype(bf16)
            out[0, 0] = mixed[:count]
            out[0, 1] = mixed[count:]


def beams(snap_total, grams, swept, steer, blocks):
    slots, double, count = steer.shape
    arrays, numbered = flattened([block for one in blocks for block in one])
    per_slot = len(blocks[0])
    numbered = [numbered[i * per_slot : (i + 1) * per_slot] for i in range(slots)]
    snaps = sum(array.shape[-1] for array, _ in blocks[0][0])
    operands = [*grams, swept, steer, *arrays]
    return pl.pallas_call(
        functools.partial(beams_kernel, len(grams), snap_total, numbered),
        grid=(slots,),
        in_specs=[pl.BlockSpec(memory_space=pltpu.VMEM)] * len(operands),
        out_specs=pl.BlockSpec((1, 2, count, snaps), lambda i: (i, 0, 0, 0)),
        out_shape=jax.ShapeDtypeStruct((slots, 2, count, snaps), bf16),
        scratch_shapes=[pltpu.VMEM((slots, 2 * count, double), bf16)],
        compiler_params=pltpu.CompilerParams(vmem_limit_bytes=BEAMS_VMEM),
        cost_estimate=QUICK,
        name="beams",
    )(*operands)


def partners(value, axis, distance):
    length = lax.axis_size(axis)
    return lax.ppermute(value, axis, [(i, i ^ distance) for i in range(length)])


def segment_sums(packed):
    length = lax.axis_size("seg")
    if length <= 4:
        return [packed] + [partners(packed, "seg", d) for d in range(1, length)]
    distance = 1
    while distance < length:
        packed = packed + partners(packed, "seg", distance)
        distance *= 2
    return [packed]


def after(value, *earlier):
    return lax.optimization_barrier((value, *earlier))


def on_device(voltages, filter_taps, positions, beam_dirs, chan_table):
    stations, width, snaps = voltages.shape
    channels = chan_table.shape[0]
    owners = lax.axis_size("stn")
    segments = lax.axis_size("seg")
    slots = channels // owners
    half = owners * stations
    snap_total = snaps * segments
    near, far = list(range(1, owners // 2)), list(range(owners // 2, owners))
    split, unsplit = far[: len(far) // 2], far[len(far) // 2 :]
    late_ones = near[-1:] + unsplit if len(near) > 1 else unsplit
    order = [d for d in range(owners) if d not in late_ones] + late_ones
    known = (owners - len(late_ones)) * stations
    together = lambda d: [[(slot, d) for slot in range(slots)]]
    apart = lambda d: [[(slot, d)] for slot in range(slots)]
    middle = [d for d in near if d not in late_ones and d > 1]
    sent = [keys for d in split for keys in together(d)] + [keys for d in middle for keys in apart(d)] + together(1)
    outer = [keys for d in late_ones for keys in together(d)]
    layout = sent + outer + together(0)
    *second, last = channelize(slots, "second", order, layout, chan_table, voltages, filter_taps)
    late = [partners(one, "stn", d) for d, one in zip(split, second)]
    halo = lax.ppermute(last, "seg", [(i, i + 1) for i in range(segments - 1)])
    joined = {key: (one, i) for keys, one in zip(layout[len(split) :], second[len(split) :]) for i, key in enumerate(keys)}
    *first, steer = channelize(
        slots, "first", order, layout, chan_table, voltages, filter_taps, halo, positions, beam_dirs, joined
    )
    first, steer, late = after(first, steer, late)
    early = [partners(one, "stn", keys[0][1]) for one, keys in zip(first, sent)]
    following, early[: len(split)] = after(first[len(sent) : -1], early[: len(split)])
    following = [partners(one, "stn", keys[0][1]) for one, keys in zip(following, outer)]
    held = {}
    for keys, one in zip(layout, early + following + first[-1:]):
        held.update({key: [(one, i)] for i, key in enumerate(keys)})
    for keys, one in zip(layout, late):
        for i, key in enumerate(keys):
            held[key].append((one, i))
    blocks = lambda ds: [[held[slot, d] for d in ds] for slot in range(slots)]
    grams = segment_sums(first_gram(blocks([d for d in order if d not in late_ones]), known, half))
    swept = first_solve(snap_total, grams, steer)
    following, swept = after(following, swept)
    for keys, one in zip(outer, following):
        held.update({key: [(one, i)] for i, key in enumerate(keys)})
    grams = segment_sums(last_gram(blocks(order), len(late_ones), half - known, half))
    return beams(snap_total, grams, swept, steer, blocks(order))


def solution(mesh):
    return jax.shard_map(
        on_device,
        mesh=mesh,
        in_specs=(P("stn", None, "seg"), P(), P(), P(), P()),
        out_specs=P("stn", None, None, "seg"),
        check_vma=False,
    )
```

time: 83.6 us -> 77.6 us (0.928)
  the two profiles are of different devices: /device:TPU:0 before, /device:TPU:11 now
where the time goes in v3:
time: 77.6 us; the launch traced here: 77.4 us
  waiting for transfers between devices  32.6 us (42%)
  Pallas kernels  23.1 us (30%)
  starting transfers between devices  21.6 us (28%)
    ppermute x16, waiting for transfers between devices, partners(): return lax.ppermute(value, axis, [(i, i ^ distance) for i in range(length)])  32.6 us
    ppermute x16, starting transfers between devices, partners(): return lax.ppermute(value, axis, [(i, i ^ distance) for i in range(length)])  18.3 us
    pallas_call x2, Pallas kernels, channelize(): pl.pallas_call(functools.partial(channelize_kernel, owners, slots, part,...  9.97 us
    pallas_call x1, Pallas kernels, beams(): pl.pallas_call(functools.partial(beams_kernel, len(grams), snap_total, nu...  6.72 us
    pallas_call x1, Pallas kernels, first_solve(): pl.pallas_call(functools.partial(first_solve_kernel, len(grams), snap_tot...  5.01 us
    ppermute x1, starting transfers between devices, on_device(): halo = lax.ppermute(last, 'seg', [(i, i + 1) for i in range(segments - 1)])  3.3 us
  transfers between devices with their start and end apart: 17, of which 10 were waited for; matrix products, arithmetic and copies ran while one was open for 0% of the time, Pallas kernels for 14%

profile of v3, /device:TPU:11, one launch (start us, length us, event | category | flops | bytes accessed | tf_op | source)
XLA Modules:
  0.0 77.4 jit_solution(14507205063080231014)
XLA Ops:
  0.0 0.0 copy-start.1
  0.0 0.0 copy-start
  0.0 4.9 %channelize_second.1 = (bf16[2,2,16,1024]{3,2,1,0:T(8,128)(2,1)S(1)}, bf16[2,2,16,1024]{3,2,1,0:T(8,128)(2,1)S(1)}, bf16[1,2,16,1024]{3,2,1,0:T(8,128)(2,1)S(1)}...) custom-call(s32[16]{0:T(128)} %refs_0_.3, ...), custom_call_target="tpu_custom_call" | custom-call | flops 1000 | bytes 1000 | tf_op jit(solution)/shard_map/channelize_second/pallas_call | solution.py:169
  4.9 3.3 %collective-permute-start = (bf16[16,32,128]{2,1,0:T(8,128)(2,1)S(1)}, bf16[16,32,128]{2,1,0:T(8,128)(2,1)S(1)}, u32[]{:S(2)}, u32[]{:S(2)}) collective-permute-start(bf16[16,32,128]{2,1,0:T(8,128)(2,1)S(1)} %get-tuple-element.46), channel_id=1, source_target_pairs={{0,1},{1,2},{2,3},{4,5},{5,6},{6,7},{8,9},{9,10},{10,11},{12,13},{... | collective-permute-start | bytes 393224 | tf_op jit(solution)/shard_map/ppermute | solution.py:518
  8.2 2.4 %collective-permute-start.1 = (bf16[2,2,16,1024]{3,2,1,0:T(8,128)(2,1)S(1)}, bf16[2,2,16,1024]{3,2,1,0:T(8,128)(2,1)S(1)}, u32[]{:S(2)}, u32[]{:S(2)}) collective-permute-start(bf16[2,2,16,1024]{3,2,1,0:T(8,128)(2,1)S(1)} %get-tuple-element.64), channel_id=1, source_target_pairs={{0,16},{4,20},{8,24},{12,28},{16,0},{20,4},{24,8},{28,12},{1,17},{... | collective-permute-start | bytes 393224 | tf_op jit(solution)/shard_map/ppermute | solution.py:479
  10.6 1.2 %collective-permute-start.2 = (bf16[2,2,16,1024]{3,2,1,0:T(8,128)(2,1)S(1)}, bf16[2,2,16,1024]{3,2,1,0:T(8,128)(2,1)S(1)}, u32[]{:S(2)}, u32[]{:S(2)}) collective-permute-start(bf16[2,2,16,1024]{3,2,1,0:T(8,128)(2,1)S(1)} %get-tuple-element.65), channel_id=1, source_target_pairs={{0,20},{4,16},{8,28},{12,24},{16,4},{20,0},{24,12},{28,8},{1,21},{... | collective-permute-start | bytes 393224 | tf_op jit(solution)/shard_map/ppermute | solution.py:479
  11.8 0.0 collective-permute-done.refs_3_
  11.8 0.0 copy-done.1
  11.8 0.0 copy-done
  11.8 5.1 %channelize_first.1 = (bf16[2,2,16,1024]{3,2,1,0:T(8,128)(2,1)S(1)}, bf16[2,2,16,1024]{3,2,1,0:T(8,128)(2,1)S(1)}, bf16[1,2,16,2048]{3,2,1,0:T(8,128)(2,1)S(1)},...) custom-call(s32[16]{0:T(128)} %refs_0_.3, ...), custom_call_target="tpu_custom_call" | custom-call | flops 1000 | bytes 1000 | tf_op jit(solution)/shard_map/channelize_first/pallas_call | solution.py:169
  16.9 2.4 %collective-permute-done.1.refs_4_.refs_10_ = bf16[2,2,16,1024]{3,2,1,0:T(8,128)(2,1)S(1)} collective-permute-done((bf16[2,2,16,1024]{3,2,1,0:T(8,128)(2,1)S(1)}, bf16[2,2,16,1024]{3,2,1,0:T(8,128)(2,1)S(1)}, u32[]{:S(2)}, u32[]{:S(2)}) %collective-permute-start.1) | collective-permute-done | bytes 131104 | tf_op jit(solution)/shard_map/ppermute | solution.py:479
  19.3 2.8 %collective-permute-done.2.refs_6_.refs_12_ = bf16[2,2,16,1024]{3,2,1,0:T(8,128)(2,1)S(1)} collective-permute-done((bf16[2,2,16,1024]{3,2,1,0:T(8,128)(2,1)S(1)}, bf16[2,2,16,1024]{3,2,1,0:T(8,128)(2,1)S(1)}, u32[]{:S(2)}, u32[]{:S(2)}) %collective-permute-start.2) | collective-permute-done | bytes 131104 | tf_op jit(solution)/shard_map/ppermute | solution.py:479
  22.1 0.5 collective-permute-start.3
  22.6 3.0 %collective-permute-start.5 = (bf16[2,2,16,1024]{3,2,1,0:T(8,128)(2,1)S(1)}, bf16[2,2,16,1024]{3,2,1,0:T(8,128)(2,1)S(1)}, u32[]{:S(2)}, u32[]{:S(2)}) collective-permute-start(bf16[2,2,16,1024]{3,2,1,0:T(8,128)(2,1)S(1)} %get-tuple-element.72), channel_id=1, source_target_pairs={{0,16},{4,20},{8,24},{12,28},{16,0},{20,4},{24,8},{28,12},{1,17},{... | collective-permute-start | bytes 393224 | tf_op jit(solution)/shard_map/ppermute | solution.py:479
  25.6 0.1 collective-permute-start.6
  25.7 0.4 collective-permute-start.4
  26.0 1.1 %collective-permute-start.10 = (bf16[1,2,16,2048]{3,2,1,0:T(8,128)(2,1)S(1)}, bf16[1,2,16,2048]{3,2,1,0:T(8,128)(2,1)S(1)}, u32[]{:S(2)}, u32[]{:S(2)}) collective-permute-start(bf16[1,2,16,2048]{3,2,1,0:T(8,128)(2,1)S(1)} %get-tuple-element.81), channel_id=1, source_target_pairs={{0,8},{4,12},{8,0},{12,4},{16,24},{20,28},{24,16},{28,20},{1,9},{5... | collective-permute-start | bytes 393224 | tf_op jit(solution)/shard_map/ppermute | solution.py:479
  27.1 4.5 %collective-permute-done.5.refs_3_.refs_9_ = bf16[2,2,16,1024]{3,2,1,0:T(8,128)(2,1)S(1)} collective-permute-done((bf16[2,2,16,1024]{3,2,1,0:T(8,128)(2,1)S(1)}, bf16[2,2,16,1024]{3,2,1,0:T(8,128)(2,1)S(1)}, u32[]{:S(2)}, u32[]{:S(2)}) %collective-permute-start.5) | collective-permute-done | bytes 131104 | tf_op jit(solution)/shard_map/ppermute | solution.py:479
  31.6 2.8 %collective-permute-done.6.refs_5_.refs_11_ = bf16[2,2,16,1024]{3,2,1,0:T(8,128)(2,1)S(1)} collective-permute-done((bf16[2,2,16,1024]{3,2,1,0:T(8,128)(2,1)S(1)}, bf16[2,2,16,1024]{3,2,1,0:T(8,128)(2,1)S(1)}, u32[]{:S(2)}, u32[]{:S(2)}) %collective-permute-start.6) | collective-permute-done | bytes 131104 | tf_op jit(solution)/shard_map/ppermute | solution.py:479
  34.4 2.8 %collective-permute-start.7 = (bf16[2,2,16,2048]{3,2,1,0:T(8,128)(2,1)S(1)}, bf16[2,2,16,2048]{3,2,1,0:T(8,128)(2,1)S(1)}, u32[]{:S(2)}, u32[]{:S(2)}) collective-permute-start(bf16[2,2,16,2048]{3,2,1,0:T(8,128)(2,1)S(1)} %get-tuple-element.78), channel_id=1, source_target_pairs={{0,12},{4,8},{8,4},{12,0},{16,28},{20,24},{24,20},{28,16},{1,13},{... | collective-permute-start | bytes 786440 | tf_op jit(solution)/shard_map/ppermute | solution.py:479
  37.3 0.9 %collective-permute-start.8 = (bf16[2,2,16,2048]{3,2,1,0:T(8,128)(2,1)S(1)}, bf16[2,2,16,2048]{3,2,1,0:T(8,128)(2,1)S(1)}, u32[]{:S(2)}, u32[]{:S(2)}) collective-permute-start(bf16[2,2,16,2048]{3,2,1,0:T(8,128)(2,1)S(1)} %get-tuple-element.79), channel_id=1, source_target_pairs={{0,24},{4,28},{8,16},{12,20},{16,8},{20,12},{24,0},{28,4},{1,25},{... | collective-permute-start | bytes 786440 | tf_op jit(solution)/shard_map/ppermute | solution.py:479
  38.2 0.0 collective-permute-done.4.refs_2_.refs_8_
  38.2 1.5 %collective-permute-start.9 = (bf16[2,2,16,2048]{3,2,1,0:T(8,128)(2,1)S(1)}, bf16[2,2,16,2048]{3,2,1,0:T(8,128)(2,1)S(1)}, u32[]{:S(2)}, u32[]{:S(2)}) collective-permute-start(bf16[2,2,16,2048]{3,2,1,0:T(8,128)(2,1)S(1)} %get-tuple-element.80), channel_id=1, source_target_pairs={{0,28},{4,24},{8,20},{12,16},{16,12},{20,8},{24,4},{28,0},{1,29},{... | collective-permute-start | bytes 786440 | tf_op jit(solution)/shard_map/ppermute | solution.py:479
  39.7 0.0 collective-permute-done.10.refs_7_.refs_10_.refs_16_
  39.7 0.0 collective-permute-done.3.refs_1_.refs_7_
  39.7 0.6 first_gram.1.refs_0_
  40.3 1.3 %collective-permute-start.13 = (f32[2,80,128]{2,1,0:T(8,128)S(1)}, f32[2,80,128]{2,1,0:T(8,128)S(1)}, u32[]{:S(2)}, u32[]{:S(2)}) collective-permute-start(f32[2,80,128]{2,1,0:T(8,128)S(1)} %first_gram.1.refs_0_), channel_id=1, source_target_pairs={{0,3},{1,2},{2,1},{3,0},{4,7},{5,6},{6,5},{7,4},{8,11},{9,10},{10,... | collective-permute-start | bytes 245768 | tf_op jit(solution)/shard_map/ppermute | solution.py:479
  41.6 0.2 collective-permute-start.12
  41.8 3.7 %collective-permute-done.13.refs_3_ = f32[2,80,128]{2,1,0:T(8,128)S(1)} collective-permute-done((f32[2,80,128]{2,1,0:T(8,128)S(1)}, f32[2,80,128]{2,1,0:T(8,128)S(1)}, u32[]{:S(2)}, u32[]{:S(2)}) %collective-permute-start.13) | collective-permute-done | bytes 81952 | tf_op jit(solution)/shard_map/ppermute | solution.py:479
  45.5 0.3 collective-permute-start.11
  45.8 1.6 %collective-permute-done.12.refs_2_ = f32[2,80,128]{2,1,0:T(8,128)S(1)} collective-permute-done((f32[2,80,128]{2,1,0:T(8,128)S(1)}, f32[2,80,128]{2,1,0:T(8,128)S(1)}, u32[]{:S(2)}, u32[]{:S(2)}) %collective-permute-start.12) | collective-permute-done | bytes 81952 | tf_op jit(solution)/shard_map/ppermute | solution.py:479
  47.4 1.7 %collective-permute-done.11.refs_1_ = f32[2,80,128]{2,1,0:T(8,128)S(1)} collective-permute-done((f32[2,80,128]{2,1,0:T(8,128)S(1)}, f32[2,80,128]{2,1,0:T(8,128)S(1)}, u32[]{:S(2)}, u32[]{:S(2)}) %collective-permute-start.11) | collective-permute-done | bytes 81952 | tf_op jit(solution)/shard_map/ppermute | solution.py:479
  49.1 5.0 %first_solve.1.refs_4_ = f32[2,2,128,384]{3,2,1,0:T(8,128)S(1)} custom-call(f32[2,80,128]{2,1,0:T(8,128)S(1)} %first_gram.1.refs_0_, f32[2,80,128]{2,1,0:T(8,128)S(1)} %collective-permute-done.11.refs_1_, f32[2,80,128]{2,1,0:T(8,128)S(1)} %collective-permute-done.12.refs_2_, f32[2,80,128]{2,1,0:T(8,128)S(1)} %collective-permute-done.13.refs_3_, ...), custom_call_target="tpu_custom_call" | custom-call | flops 1000 | bytes 1000 | tf_op jit(solution)/shard_map/first_solve/pallas_call | solution.py:379
  54.1 0.0 collective-permute-done.7.refs_7_.refs_13_
  54.2 0.0 collective-permute-done.8.refs_8_.refs_14_
  54.2 8.0 %collective-permute-done.9.refs_9_.refs_15_ = bf16[2,2,16,2048]{3,2,1,0:T(8,128)(2,1)S(1)} collective-permute-done((bf16[2,2,16,2048]{3,2,1,0:T(8,128)(2,1)S(1)}, bf16[2,2,16,2048]{3,2,1,0:T(8,128)(2,1)S(1)}, u32[]{:S(2)}, u32[]{:S(2)}) %collective-permute-start.9) | collective-permute-done | bytes 262176 | tf_op jit(solution)/shard_map/ppermute | solution.py:479
  62.1 0.8 %last_gram.1.refs_0_ = f32[2,96,128]{2,1,0:T(8,128)S(1)} custom-call(bf16[2,2,16,2048]{3,2,1,0:T(8,128)(2,1)S(1)} %get-tuple-element.66.refs_0_.refs_6_, bf16[2,2,16,2048]{3,2,1,0:T(8,128)(2,1)S(1)} %collective-permute-done.3.refs_1_.refs_7_, bf16[1,2,16,2048]{3,2,1,0:T(8,128)(2,1)S(1)} %collective-permute-done.4.refs_2_.refs_8_, ...), custom_call_target="tpu_custom_call" | custom-call | flops 1000 | bytes 1000 | tf_op jit(solution)/shard_map/last_gram/pallas_call | solution.py:245
  62.9 1.3 %collective-permute-start.16 = (f32[2,96,128]{2,1,0:T(8,128)S(1)}, f32[2,96,128]{2,1,0:T(8,128)S(1)}, u32[]{:S(2)}, u32[]{:S(2)}) collective-permute-start(f32[2,96,128]{2,1,0:T(8,128)S(1)} %last_gram.1.refs_0_), channel_id=1, source_target_pairs={{0,3},{1,2},{2,1},{3,0},{4,7},{5,6},{6,5},{7,4},{8,11},{9,10},{10,... | collective-permute-start | bytes 294920 | tf_op jit(solution)/shard_map/ppermute | solution.py:479
  64.2 0.2 collective-permute-start.15
  64.4 1.2 %collective-permute-start.14 = (f32[2,96,128]{2,1,0:T(8,128)S(1)}, f32[2,96,128]{2,1,0:T(8,128)S(1)}, u32[]{:S(2)}, u32[]{:S(2)}) collective-permute-start(f32[2,96,128]{2,1,0:T(8,128)S(1)} %last_gram.1.refs_0_), channel_id=1, source_target_pairs={{0,1},{1,0},{2,3},{3,2},{4,5},{5,4},{6,7},{7,6},{8,9},{9,8},{10,11... | collective-permute-start | bytes 294920 | tf_op jit(solution)/shard_map/ppermute | solution.py:479
  65.6 2.8 %collective-permute-done.16.refs_3_ = f32[2,96,128]{2,1,0:T(8,128)S(1)} collective-permute-done((f32[2,96,128]{2,1,0:T(8,128)S(1)}, f32[2,96,128]{2,1,0:T(8,128)S(1)}, u32[]{:S(2)}, u32[]{:S(2)}) %collective-permute-start.16) | collective-permute-done | bytes 98336 | tf_op jit(solution)/shard_map/ppermute | solution.py:479
  68.4 2.2 %collective-permute-done.15.refs_2_ = f32[2,96,128]{2,1,0:T(8,128)S(1)} collective-permute-done((f32[2,96,128]{2,1,0:T(8,128)S(1)}, f32[2,96,128]{2,1,0:T(8,128)S(1)}, u32[]{:S(2)}, u32[]{:S(2)}) %collective-permute-start.15) | collective-permute-done | bytes 98336 | tf_op jit(solution)/shard_map/ppermute | solution.py:479
  70.7 0.0 collective-permute-done.14.refs_1_
  70.7 6.7 %beams.1 = bf16[2,2,128,2048]{3,2,1,0:T(8,128)(2,1)} custom-call(f32[2,96,128]{2,1,0:T(8,128)S(1)} %last_gram.1.refs_0_, f32[2,96,128]{2,1,0:T(8,128)S(1)} %collective-permute-done.14.refs_1_, f32[2,96,128]{2,1,0:T(8,128)S(1)} %collective-permute-done.15.refs_2_, f32[2,96,128]{2,1,0:T(8,128)S(1)} %collective-permute-done.16.refs_3_, ...), custom_call_target="tpu_custom_call" | custom-call | flops 1000 | bytes 1000 | tf_op jit(solution)/shard_map/beams/pallas_call | solution.py:464
Async XLA Ops:
  0.0 11.8 %copy-start.1 = (s32[128]{0:T(128)S(1)}, s32[128]{0:T(128)}, u32[]{:S(2)}) copy-start(s32[128]{0:T(128)} %param.8) | copy-start | bytes 1540
  0.0 11.8 %copy-start = (f32[2,128]{1,0:T(2,128)S(1)}, f32[2,128]{1,0:T(2,128)}, u32[]{:S(2)}) copy-start(f32[2,128]{1,0:T(2,128)} %refs_4_.1) | copy-start | bytes 3076
  4.9 6.9 %collective-permute-start = (bf16[16,32,128]{2,1,0:T(8,128)(2,1)S(1)}, bf16[16,32,128]{2,1,0:T(8,128)(2,1)S(1)}, u32[]{:S(2)}, u32[]{:S(2)}) collective-permute-start(bf16[16,32,128]{2,1,0:T(8,128)(2,1)S(1)} %get-tuple-element.46), channel_id=1, source_target_pairs={{0,1},{1,2},{2,3},{4,5},{5,6},{6,7},{8,9},{9,10},{10,11},{12,13},{... | collective-permute-start | bytes 393224 | tf_op jit(solution)/shard_map/ppermute | solution.py:518
  8.2 11.1 %collective-permute-start.1 = (bf16[2,2,16,1024]{3,2,1,0:T(8,128)(2,1)S(1)}, bf16[2,2,16,1024]{3,2,1,0:T(8,128)(2,1)S(1)}, u32[]{:S(2)}, u32[]{:S(2)}) collective-permute-start(bf16[2,2,16,1024]{3,2,1,0:T(8,128)(2,1)S(1)} %get-tuple-element.64), channel_id=1, source_target_pairs={{0,16},{4,20},{8,24},{12,28},{16,0},{20,4},{24,8},{28,12},{1,17},{... | collective-permute-start | bytes 393224 | tf_op jit(solution)/shard_map/ppermute | solution.py:479
  10.6 11.5 %collective-permute-start.2 = (bf16[2,2,16,1024]{3,2,1,0:T(8,128)(2,1)S(1)}, bf16[2,2,16,1024]{3,2,1,0:T(8,128)(2,1)S(1)}, u32[]{:S(2)}, u32[]{:S(2)}) collective-permute-start(bf16[2,2,16,1024]{3,2,1,0:T(8,128)(2,1)S(1)} %get-tuple-element.65), channel_id=1, source_target_pairs={{0,20},{4,16},{8,28},{12,24},{16,4},{20,0},{24,12},{28,8},{1,21},{... | collective-permute-start | bytes 393224 | tf_op jit(solution)/shard_map/ppermute | solution.py:479
  22.1 17.6 %collective-permute-start.3 = (bf16[2,2,16,2048]{3,2,1,0:T(8,128)(2,1)S(1)}, bf16[2,2,16,2048]{3,2,1,0:T(8,128)(2,1)S(1)}, u32[]{:S(2)}, u32[]{:S(2)}) collective-permute-start(bf16[2,2,16,2048]{3,2,1,0:T(8,128)(2,1)S(1)} %get-tuple-element.67), channel_id=1, source_target_pairs={{0,4},{4,0},{8,12},{12,8},{16,20},{20,16},{24,28},{28,24},{1,5},{5... | collective-permute-start | bytes 786440 | tf_op jit(solution)/shard_map/ppermute | solution.py:479
  22.6 9.0 %collective-permute-start.5 = (bf16[2,2,16,1024]{3,2,1,0:T(8,128)(2,1)S(1)}, bf16[2,2,16,1024]{3,2,1,0:T(8,128)(2,1)S(1)}, u32[]{:S(2)}, u32[]{:S(2)}) collective-permute-start(bf16[2,2,16,1024]{3,2,1,0:T(8,128)(2,1)S(1)} %get-tuple-element.72), channel_id=1, source_target_pairs={{0,16},{4,20},{8,24},{12,28},{16,0},{20,4},{24,8},{28,12},{1,17},{... | collective-permute-start | bytes 393224 | tf_op jit(solution)/shard_map/ppermute | solution.py:479
  25.6 8.8 %collective-permute-start.6 = (bf16[2,2,16,1024]{3,2,1,0:T(8,128)(2,1)S(1)}, bf16[2,2,16,1024]{3,2,1,0:T(8,128)(2,1)S(1)}, u32[]{:S(2)}, u32[]{:S(2)}) collective-permute-start(bf16[2,2,16,1024]{3,2,1,0:T(8,128)(2,1)S(1)} %get-tuple-element.73), channel_id=1, source_target_pairs={{0,20},{4,16},{8,28},{12,24},{16,4},{20,0},{24,12},{28,8},{1,21},{... | collective-permute-start | bytes 393224 | tf_op jit(solution)/shard_map/ppermute | solution.py:479
  25.7 12.5 %collective-permute-start.4 = (bf16[1,2,16,2048]{3,2,1,0:T(8,128)(2,1)S(1)}, bf16[1,2,16,2048]{3,2,1,0:T(8,128)(2,1)S(1)}, u32[]{:S(2)}, u32[]{:S(2)}) collective-permute-start(bf16[1,2,16,2048]{3,2,1,0:T(8,128)(2,1)S(1)} %get-tuple-element.68), channel_id=1, source_target_pairs={{0,8},{4,12},{8,0},{12,4},{16,24},{20,28},{24,16},{28,20},{1,9},{5... | collective-permute-start | bytes 393224 | tf_op jit(solution)/shard_map/ppermute | solution.py:479
  26.0 13.7 %collective-permute-start.10 = (bf16[1,2,16,2048]{3,2,1,0:T(8,128)(2,1)S(1)}, bf16[1,2,16,2048]{3,2,1,0:T(8,128)(2,1)S(1)}, u32[]{:S(2)}, u32[]{:S(2)}) collective-permute-start(bf16[1,2,16,2048]{3,2,1,0:T(8,128)(2,1)S(1)} %get-tuple-element.81), channel_id=1, source_target_pairs={{0,8},{4,12},{8,0},{12,4},{16,24},{20,28},{24,16},{28,20},{1,9},{5... | collective-permute-start | bytes 393224 | tf_op jit(solution)/shard_map/ppermute | solution.py:479
  34.4 19.7 %collective-permute-start.7 = (bf16[2,2,16,2048]{3,2,1,0:T(8,128)(2,1)S(1)}, bf16[2,2,16,2048]{3,2,1,0:T(8,128)(2,1)S(1)}, u32[]{:S(2)}, u32[]{:S(2)}) collective-permute-start(bf16[2,2,16,2048]{3,2,1,0:T(8,128)(2,1)S(1)} %get-tuple-element.78), channel_id=1, source_target_pairs={{0,12},{4,8},{8,4},{12,0},{16,28},{20,24},{24,20},{28,16},{1,13},{... | collective-permute-start | bytes 786440 | tf_op jit(solution)/shard_map/ppermute | solution.py:479
  37.3 16.9 %collective-permute-start.8 = (bf16[2,2,16,2048]{3,2,1,0:T(8,128)(2,1)S(1)}, bf16[2,2,16,2048]{3,2,1,0:T(8,128)(2,1)S(1)}, u32[]{:S(2)}, u32[]{:S(2)}) collective-permute-start(bf16[2,2,16,2048]{3,2,1,0:T(8,128)(2,1)S(1)} %get-tuple-element.79), channel_id=1, source_target_pairs={{0,24},{4,28},{8,16},{12,20},{16,8},{20,12},{24,0},{28,4},{1,25},{... | collective-permute-start | bytes 786440 | tf_op jit(solution)/shard_map/ppermute | solution.py:479
  38.2 24.0 %collective-permute-start.9 = (bf16[2,2,16,2048]{3,2,1,0:T(8,128)(2,1)S(1)}, bf16[2,2,16,2048]{3,2,1,0:T(8,128)(2,1)S(1)}, u32[]{:S(2)}, u32[]{:S(2)}) collective-permute-start(bf16[2,2,16,2048]{3,2,1,0:T(8,128)(2,1)S(1)} %get-tuple-element.80), channel_id=1, source_target_pairs={{0,28},{4,24},{8,20},{12,16},{16,12},{20,8},{24,4},{28,0},{1,29},{... | collective-permute-start | bytes 786440 | tf_op jit(solution)/shard_map/ppermute | solution.py:479
  40.3 5.2 %collective-permute-start.13 = (f32[2,80,128]{2,1,0:T(8,128)S(1)}, f32[2,80,128]{2,1,0:T(8,128)S(1)}, u32[]{:S(2)}, u32[]{:S(2)}) collective-permute-start(f32[2,80,128]{2,1,0:T(8,128)S(1)} %first_gram.1.refs_0_), channel_id=1, source_target_pairs={{0,3},{1,2},{2,1},{3,0},{4,7},{5,6},{6,5},{7,4},{8,11},{9,10},{10,... | collective-permute-start | bytes 245768 | tf_op jit(solution)/shard_map/ppermute | solution.py:479
  41.6 5.8 %collective-permute-start.12 = (f32[2,80,128]{2,1,0:T(8,128)S(1)}, f32[2,80,128]{2,1,0:T(8,128)S(1)}, u32[]{:S(2)}, u32[]{:S(2)}) collective-permute-start(f32[2,80,128]{2,1,0:T(8,128)S(1)} %first_gram.1.refs_0_), channel_id=1, source_target_pairs={{0,2},{1,3},{2,0},{3,1},{4,6},{5,7},{6,4},{7,5},{8,10},{9,11},{10,... | collective-permute-start | bytes 245768 | tf_op jit(solution)/shard_map/ppermute | solution.py:479
  45.5 3.6 %collective-permute-start.11 = (f32[2,80,128]{2,1,0:T(8,128)S(1)}, f32[2,80,128]{2,1,0:T(8,128)S(1)}, u32[]{:S(2)}, u32[]{:S(2)}) collective-permute-start(f32[2,80,128]{2,1,0:T(8,128)S(1)} %first_gram.1.refs_0_), channel_id=1, source_target_pairs={{0,1},{1,0},{2,3},{3,2},{4,5},{5,4},{6,7},{7,6},{8,9},{9,8},{10,11... | collective-permute-start | bytes 245768 | tf_op jit(solution)/shard_map/ppermute | solution.py:479
  62.9 5.5 %collective-permute-start.16 = (f32[2,96,128]{2,1,0:T(8,128)S(1)}, f32[2,96,128]{2,1,0:T(8,128)S(1)}, u32[]{:S(2)}, u32[]{:S(2)}) collective-permute-start(f32[2,96,128]{2,1,0:T(8,128)S(1)} %last_gram.1.refs_0_), channel_id=1, source_target_pairs={{0,3},{1,2},{2,1},{3,0},{4,7},{5,6},{6,5},{7,4},{8,11},{9,10},{10,... | collective-permute-start | bytes 294920 | tf_op jit(solution)/shard_map/ppermute | solution.py:479
  64.2 6.5 %collective-permute-start.15 = (f32[2,96,128]{2,1,0:T(8,128)S(1)}, f32[2,96,128]{2,1,0:T(8,128)S(1)}, u32[]{:S(2)}, u32[]{:S(2)}) collective-permute-start(f32[2,96,128]{2,1,0:T(8,128)S(1)} %last_gram.1.refs_0_), channel_id=1, source_target_pairs={{0,2},{1,3},{2,0},{3,1},{4,6},{5,7},{6,4},{7,5},{8,10},{9,11},{10,... | collective-permute-start | bytes 294920 | tf_op jit(solution)/shard_map/ppermute | solution.py:479
  64.4 6.2 %collective-permute-start.14 = (f32[2,96,128]{2,1,0:T(8,128)S(1)}, f32[2,96,128]{2,1,0:T(8,128)S(1)}, u32[]{:S(2)}, u32[]{:S(2)}) collective-permute-start(f32[2,96,128]{2,1,0:T(8,128)S(1)} %last_gram.1.refs_0_), channel_id=1, source_target_pairs={{0,1},{1,0},{2,3},{3,2},{4,5},{5,4},{6,7},{7,6},{8,9},{9,8},{10,11... | collective-permute-start | bytes 294920 | tf_op jit(solution)/shard_map/ppermute | solution.py:479

commit v4 on v3

--- a/solution.py
+++ b/solution.py
@@ -133,9 +133,7 @@
         if (slot, d) in joined:
             at, inside = joined[slot, d]
             target[:, :, chunk:] = others[at][inside]
-    if not has_halo:
-        outs[-1][...] = held[:, :, chunk:]
-    else:
+    if has_halo:
         for slot in range(slots):
             channel = chans[me * slots + slot]
             outs[-1][slot] = steering(me, order, refs[4][...], refs[5][...], channel, owners * slots)
@@ -160,9 +158,7 @@
             places[key] = (number, entry)
         length = snaps if keys[0] in joined else chunk
         out_shape.append(jax.ShapeDtypeStruct((len(keys), 2, stations, length), bf16))
-    if halo is None:
-        out_shape.append(jax.ShapeDtypeStruct((stations, width, LANES), bf16))
-    else:
+    if halo is not None:
         out_shape.append(jax.ShapeDtypeStruct((slots, 2 * owners * stations, beam_dirs.shape[0]), f32))
     operands = [pltpu.with_memory_space_constraint(one, pltpu.HBM) for one in (chans, volts, taps)]
     operands += ([] if halo is None else [halo, positions, beam_dirs[None, :]]) + others
@@ -503,39 +499,38 @@
     half = owners * stations
     snap_total = snaps * segments
     near, far = list(range(1, owners // 2)), list(range(owners // 2, owners))
-    split, unsplit = far[: len(far) // 2], far[len(far) // 2 :]
-    late_ones = near[-1:] + unsplit if len(near) > 1 else unsplit
-    order = [d for d in range(owners) if d not in late_ones] + late_ones
+    order = list(range(owners))
+    late_ones = far[len(far) // 2 :]
     known = (owners - len(late_ones)) * stations
-    together = lambda d: [[(slot, d) for slot in range(slots)]]
-    apart = lambda d: [[(slot, d)] for slot in range(slots)]
-    middle = [d for d in near if d not in late_ones and d > 1]
-    sent = [keys for d in split for keys in together(d)] + [keys for d in middle for keys in apart(d)] + together(1)
-    outer = [keys for d in late_ones for keys in together(d)]
-    layout = sent + outer + together(0)
-    *second, last = channelize(slots, "second", order, layout, chan_table, voltages, filter_taps)
+    split = far[:1] + near[1:][: max(len(near) - 2, 1)]
+    rest = [d for d in order if d not in split]
+    layout = [[(slot, d) for slot in range(slots)] for d in split + rest]
+    halo = lax.ppermute(voltages[:, :, snaps - LANES :], "seg", [(i, i + 1) for i in range(segments - 1)])
+    second = channelize(slots, "second", order, layout, chan_table, voltages, filter_taps)
     late = [partners(one, "stn", d) for d, one in zip(split, second)]
-    halo = lax.ppermute(last, "seg", [(i, i + 1) for i in range(segments - 1)])
     joined = {key: (one, i) for keys, one in zip(layout[len(split) :], second[len(split) :]) for i, key in enumerate(keys)}
     *first, steer = channelize(
         slots, "first", order, layout, chan_table, voltages, filter_taps, halo, positions, beam_dirs, joined
     )
     first, steer, late = after(first, steer, late)
-    early = [partners(one, "stn", keys[0][1]) for one, keys in zip(first, sent)]
-    following, early[: len(split)] = after(first[len(sent) : -1], early[: len(split)])
-    following = [partners(one, "stn", keys[0][1]) for one, keys in zip(following, outer)]
-    held = {}
-    for keys, one in zip(layout, early + following + first[-1:]):
-        held.update({key: [(one, i)] for i, key in enumerate(keys)})
-    for keys, one in zip(layout, late):
-        for i, key in enumerate(keys):
-            held[key].append((one, i))
+    first = dict(zip(split + rest, first))
+    arrived = {d: partners(first[d], "stn", d) for d in split + rest[1:] if d not in late_ones}
+    following = {}
+    for i, d in enumerate(late_ones):
+        ahead = [far[i]] + [e for e in near if e in split][i :: len(late_ones)]
+        value, there = after(first[d], [arrived[e] for e in ahead])
+        arrived.update(zip(ahead, there))
+        following[d] = partners(value, "stn", d)
+    arrived.update({0: first[0], **following})
+    held = {(slot, d): [(one, slot)] for d, one in arrived.items() for slot in range(slots)}
+    for d, one in zip(split, late):
+        for slot in range(slots):
+            held[slot, d].append((one, slot))
     blocks = lambda ds: [[held[slot, d] for d in ds] for slot in range(slots)]
     grams = segment_sums(first_gram(blocks([d for d in order if d not in late_ones]), known, half))
     swept = first_solve(snap_total, grams, steer)
     following, swept = after(following, swept)
-    for keys, one in zip(outer, following):
-        held.update({key: [(one, i)] for i, key in enumerate(keys)})
+    held.update({(slot, d): [(one, slot)] for d, one in following.items() for slot in range(slots)})
     grams = segment_sums(last_gram(blocks(order), len(late_ones), half - known, half))
     return beams(snap_total, grams, swept, steer, blocks(order))
 

time: 77.6 us -> 74.7 us (0.963)
  starting transfers between devices: 21.6 us -> 18.8 us
  waiting for transfers between devices: 32.6 us -> 31.5 us
  local copies, waits for them, and re-layouts: 0.01 us -> 0.95 us
    ppermute x16 -> x15, starting transfers between devices: 18.3 us -> 15.7 us  [partners(): return lax.ppermute(value, axis, [(i, i ^ distance) for i in range(length)])]
    pallas_call x1, Pallas kernels: 5.01 us -> 6.19 us  [first_solve(): pl.pallas_call(functools.partial(first_solve_kernel, len(grams), snap_tot...]
    pallas_call x1, Pallas kernels: 6.72 us -> 5.61 us  [beams(): pl.pallas_call(functools.partial(beams_kernel, len(grams), snap_total, nu...]
    ppermute x16 -> x15, waiting for transfers between devices: 32.6 us -> 31.5 us  [partners(): return lax.ppermute(value, axis, [(i, i ^ distance) for i in range(length)])]
    slice x0 -> x1, local copies, waits for them, and re-layouts: none -> 0.94 us  [on_device(): voltages[:, :, snaps - LANES:]]
  transfers between devices with their start and end apart: 17 -> 16, of which waited for: 10 -> 8; matrix products, arithmetic and copies ran while one was open for 0% -> 0% of each run, Pallas kernels for 14% -> 23%
where the time goes in v4:
time: 74.7 us; the launch traced here: 74.5 us
  waiting for transfers between devices  31.5 us (42%)
  Pallas kernels  23.2 us (31%)
  starting transfers between devices  18.8 us (25%)
  local copies, waits for them, and re-layouts  0.95 us (1%)
    ppermute x15, waiting for transfers between devices, partners(): return lax.ppermute(value, axis, [(i, i ^ distance) for i in range(length)])  31.5 us
    ppermute x15, starting transfers between devices, partners(): return lax.ppermute(value, axis, [(i, i ^ distance) for i in range(length)])  15.7 us
    pallas_call x2, Pallas kernels, channelize(): pl.pallas_call(functools.partial(channelize_kernel, owners, slots, part,...  9.93 us
    pallas_call x1, Pallas kernels, first_solve(): pl.pallas_call(functools.partial(first_solve_kernel, len(grams), snap_tot...  6.19 us
    pallas_call x1, Pallas kernels, beams(): pl.pallas_call(functools.partial(beams_kernel, len(grams), snap_total, nu...  5.61 us
    ppermute x1, starting transfers between devices, on_device(): lax.ppermute(voltages[:, :, snaps - LANES:], 'seg', [(i, i + 1) for i in...  3.12 us
  transfers between devices with their start and end apart: 16, of which 8 were waited for; matrix products, arithmetic and copies ran while one was open for 0% of the time, Pallas kernels for 23%

profile of v4, /device:TPU:11, one launch (start us, length us, event | category | flops | bytes accessed | tf_op | source)
XLA Modules:
  0.0 74.5 jit_solution(13539578096705725831)
XLA Ops:
  0.0 0.0 copy-start.1
  0.0 0.0 copy-start
  0.0 0.9 %slice.3 = bf16[16,32,128]{2,1,0:T(8,128)(2,1)S(1)} slice(bf16[16,32,2048]{2,1,0:T(8,128)(2,1)} %refs_1_.3), slice={[0:16], [0:32], [1920:2048]} | slice | bytes 262144 | tf_op jit(solution)/shard_map/slice | solution.py:508
  0.9 3.1 %collective-permute-start = (bf16[16,32,128]{2,1,0:T(8,128)(2,1)S(1)}, bf16[16,32,128]{2,1,0:T(8,128)(2,1)S(1)}, u32[]{:S(2)}, u32[]{:S(2)}) collective-permute-start(bf16[16,32,128]{2,1,0:T(8,128)(2,1)S(1)} %slice.3), channel_id=1, source_target_pairs={{0,1},{1,2},{2,3},{4,5},{5,6},{6,7},{8,9},{9,10},{10,11},{12,13},{... | collective-permute-start | bytes 393224 | tf_op jit(solution)/shard_map/ppermute | solution.py:508
  4.1 4.8 %channelize_second.1 = (bf16[2,2,16,1024]{3,2,1,0:T(8,128)(2,1)S(1)}, bf16[2,2,16,1024]{3,2,1,0:T(8,128)(2,1)S(1)}, bf16[2,2,16,1024]{3,2,1,0:T(8,128)(2,1)S(1)}...) custom-call(s32[16]{0:T(128)} %refs_0_.3, ...), custom_call_target="tpu_custom_call" | custom-call | flops 1000 | bytes 1000 | tf_op jit(solution)/shard_map/channelize_second/pallas_call | solution.py:165
  8.9 2.4 %collective-permute-start.1 = (bf16[2,2,16,1024]{3,2,1,0:T(8,128)(2,1)S(1)}, bf16[2,2,16,1024]{3,2,1,0:T(8,128)(2,1)S(1)}, u32[]{:S(2)}, u32[]{:S(2)}) collective-permute-start(bf16[2,2,16,1024]{3,2,1,0:T(8,128)(2,1)S(1)} %get-tuple-element.56), channel_id=1, source_target_pairs={{0,16},{4,20},{8,24},{12,28},{16,0},{20,4},{24,8},{28,12},{1,17},{... | collective-permute-start | bytes 393224 | tf_op jit(solution)/shard_map/ppermute | solution.py:475
  11.3 0.2 collective-permute-start.2
  11.5 0.0 collective-permute-done.refs_3_
  11.5 0.0 copy-done.1
  11.5 0.0 copy-done
  11.5 5.1 %channelize_first.1 = (bf16[2,2,16,1024]{3,2,1,0:T(8,128)(2,1)S(1)}, bf16[2,2,16,1024]{3,2,1,0:T(8,128)(2,1)S(1)}, bf16[2,2,16,2048]{3,2,1,0:T(8,128)(2,1)S(1)},...) custom-call(s32[16]{0:T(128)} %refs_0_.3, ...), custom_call_target="tpu_custom_call" | custom-call | flops 1000 | bytes 1000 | tf_op jit(solution)/shard_map/channelize_first/pallas_call | solution.py:165
  16.6 0.6 collective-permute-done.1.refs_6_.refs_12_
  17.2 0.0 collective-permute-done.2.refs_3_.refs_9_
  17.2 3.5 %collective-permute-start.7 = (bf16[2,2,16,2048]{3,2,1,0:T(8,128)(2,1)S(1)}, bf16[2,2,16,2048]{3,2,1,0:T(8,128)(2,1)S(1)}, u32[]{:S(2)}, u32[]{:S(2)}) collective-permute-start(bf16[2,2,16,2048]{3,2,1,0:T(8,128)(2,1)S(1)} %get-tuple-element.69), channel_id=1, source_target_pairs={{0,20},{4,16},{8,28},{12,24},{16,4},{20,0},{24,12},{28,8},{1,21},{... | collective-permute-start | bytes 786440 | tf_op jit(solution)/shard_map/ppermute | solution.py:475
  20.7 0.3 collective-permute-start.4
  21.0 0.7 %collective-permute-start.5 = (bf16[2,2,16,1024]{3,2,1,0:T(8,128)(2,1)S(1)}, bf16[2,2,16,1024]{3,2,1,0:T(8,128)(2,1)S(1)}, u32[]{:S(2)}, u32[]{:S(2)}) collective-permute-start(bf16[2,2,16,1024]{3,2,1,0:T(8,128)(2,1)S(1)} %get-tuple-element.62), channel_id=1, source_target_pairs={{0,8},{4,12},{8,0},{12,4},{16,24},{20,28},{24,16},{28,20},{1,9},{5... | collective-permute-start | bytes 393224 | tf_op jit(solution)/shard_map/ppermute | solution.py:475
  21.7 0.0 collective-permute-start.3
  21.7 1.1 %collective-permute-start.6 = (bf16[2,2,16,2048]{3,2,1,0:T(8,128)(2,1)S(1)}, bf16[2,2,16,2048]{3,2,1,0:T(8,128)(2,1)S(1)}, u32[]{:S(2)}, u32[]{:S(2)}) collective-permute-start(bf16[2,2,16,2048]{3,2,1,0:T(8,128)(2,1)S(1)} %get-tuple-element.65), channel_id=1, source_target_pairs={{0,12},{4,8},{8,4},{12,0},{16,28},{20,24},{24,20},{28,16},{1,13},{... | collective-permute-start | bytes 786440 | tf_op jit(solution)/shard_map/ppermute | solution.py:475
  22.8 13.9 %collective-permute-done.4.refs_5_.refs_11_ = bf16[2,2,16,1024]{3,2,1,0:T(8,128)(2,1)S(1)} collective-permute-done((bf16[2,2,16,1024]{3,2,1,0:T(8,128)(2,1)S(1)}, bf16[2,2,16,1024]{3,2,1,0:T(8,128)(2,1)S(1)}, u32[]{:S(2)}, u32[]{:S(2)}) %collective-permute-start.4) | collective-permute-done | bytes 131104 | tf_op jit(solution)/shard_map/ppermute | solution.py:475
  36.8 0.0 collective-permute-done.5.refs_2_.refs_8_
  36.8 0.4 collective-permute-start.8
  37.1 0.0 collective-permute-done.7.refs_7_.refs_13_
  37.1 1.7 %collective-permute-start.9 = (bf16[2,2,16,2048]{3,2,1,0:T(8,128)(2,1)S(1)}, bf16[2,2,16,2048]{3,2,1,0:T(8,128)(2,1)S(1)}, u32[]{:S(2)}, u32[]{:S(2)}) collective-permute-start(bf16[2,2,16,2048]{3,2,1,0:T(8,128)(2,1)S(1)} %get-tuple-element.72), channel_id=1, source_target_pairs={{0,28},{4,24},{8,20},{12,16},{16,12},{20,8},{24,4},{28,0},{1,29},{... | collective-permute-start | bytes 786440 | tf_op jit(solution)/shard_map/ppermute | solution.py:475
  38.8 0.0 collective-permute-done.3.refs_1_.refs_7_
  38.8 0.0 collective-permute-done.6.refs_4_.refs_10_
  38.8 0.7 first_gram.1.refs_0_
  39.5 1.3 %collective-permute-start.12 = (f32[2,96,128]{2,1,0:T(8,128)S(1)}, f32[2,96,128]{2,1,0:T(8,128)S(1)}, u32[]{:S(2)}, u32[]{:S(2)}) collective-permute-start(f32[2,96,128]{2,1,0:T(8,128)S(1)} %first_gram.1.refs_0_), channel_id=1, source_target_pairs={{0,3},{1,2},{2,1},{3,0},{4,7},{5,6},{6,5},{7,4},{8,11},{9,10},{10,... | collective-permute-start | bytes 294920 | tf_op jit(solution)/shard_map/ppermute | solution.py:475
  40.8 0.2 collective-permute-start.11
  41.1 1.2 %collective-permute-start.10 = (f32[2,96,128]{2,1,0:T(8,128)S(1)}, f32[2,96,128]{2,1,0:T(8,128)S(1)}, u32[]{:S(2)}, u32[]{:S(2)}) collective-permute-start(f32[2,96,128]{2,1,0:T(8,128)S(1)} %first_gram.1.refs_0_), channel_id=1, source_target_pairs={{0,1},{1,0},{2,3},{3,2},{4,5},{5,4},{6,7},{7,6},{8,9},{9,8},{10,11... | collective-permute-start | bytes 294920 | tf_op jit(solution)/shard_map/ppermute | solution.py:475
  42.3 2.8 %collective-permute-done.12.refs_3_ = f32[2,96,128]{2,1,0:T(8,128)S(1)} collective-permute-done((f32[2,96,128]{2,1,0:T(8,128)S(1)}, f32[2,96,128]{2,1,0:T(8,128)S(1)}, u32[]{:S(2)}, u32[]{:S(2)}) %collective-permute-start.12) | collective-permute-done | bytes 98336 | tf_op jit(solution)/shard_map/ppermute | solution.py:475
  45.1 2.3 %collective-permute-done.11.refs_2_ = f32[2,96,128]{2,1,0:T(8,128)S(1)} collective-permute-done((f32[2,96,128]{2,1,0:T(8,128)S(1)}, f32[2,96,128]{2,1,0:T(8,128)S(1)}, u32[]{:S(2)}, u32[]{:S(2)}) %collective-permute-start.11) | collective-permute-done | bytes 98336 | tf_op jit(solution)/shard_map/ppermute | solution.py:475
  47.4 0.0 collective-permute-done.10.refs_1_
  47.4 6.2 %first_solve.1.refs_4_ = f32[2,2,128,384]{3,2,1,0:T(8,128)S(1)} custom-call(f32[2,96,128]{2,1,0:T(8,128)S(1)} %first_gram.1.refs_0_, f32[2,96,128]{2,1,0:T(8,128)S(1)} %collective-permute-done.10.refs_1_, f32[2,96,128]{2,1,0:T(8,128)S(1)} %collective-permute-done.11.refs_2_, f32[2,96,128]{2,1,0:T(8,128)S(1)} %collective-permute-done.12.refs_3_, ...), custom_call_target="tpu_custom_call" | custom-call | flops 1000 | bytes 1000 | tf_op jit(solution)/shard_map/first_solve/pallas_call | solution.py:375
  53.6 1.9 %collective-permute-done.8.refs_8_.refs_14_ = bf16[2,2,16,2048]{3,2,1,0:T(8,128)(2,1)S(1)} collective-permute-done((bf16[2,2,16,2048]{3,2,1,0:T(8,128)(2,1)S(1)}, bf16[2,2,16,2048]{3,2,1,0:T(8,128)(2,1)S(1)}, u32[]{:S(2)}, u32[]{:S(2)}) %collective-permute-start.8) | collective-permute-done | bytes 262176 | tf_op jit(solution)/shard_map/ppermute | solution.py:475
  55.5 6.2 %collective-permute-done.9.refs_9_.refs_15_ = bf16[2,2,16,2048]{3,2,1,0:T(8,128)(2,1)S(1)} collective-permute-done((bf16[2,2,16,2048]{3,2,1,0:T(8,128)(2,1)S(1)}, bf16[2,2,16,2048]{3,2,1,0:T(8,128)(2,1)S(1)}, u32[]{:S(2)}, u32[]{:S(2)}) %collective-permute-start.9) | collective-permute-done | bytes 262176 | tf_op jit(solution)/shard_map/ppermute | solution.py:475
  61.7 0.7 %last_gram.1.refs_0_ = f32[2,64,128]{2,1,0:T(8,128)S(1)} custom-call(bf16[2,2,16,2048]{3,2,1,0:T(8,128)(2,1)S(1)} %get-tuple-element.58.refs_0_.refs_6_, bf16[2,2,16,2048]{3,2,1,0:T(8,128)(2,1)S(1)} %collective-permute-done.3.refs_1_.refs_7_, bf16[2,2,16,1024]{3,2,1,0:T(8,128)(2,1)S(1)} %collective-permute-done.5.refs_2_.refs_8_, ...), custom_call_target="tpu_custom_call" | custom-call | flops 1000 | bytes 1000 | tf_op jit(solution)/shard_map/last_gram/pallas_call | solution.py:241
  62.4 1.3 %collective-permute-start.15 = (f32[2,64,128]{2,1,0:T(8,128)S(1)}, f32[2,64,128]{2,1,0:T(8,128)S(1)}, u32[]{:S(2)}, u32[]{:S(2)}) collective-permute-start(f32[2,64,128]{2,1,0:T(8,128)S(1)} %last_gram.1.refs_0_), channel_id=1, source_target_pairs={{0,3},{1,2},{2,1},{3,0},{4,7},{5,6},{6,5},{7,4},{8,11},{9,10},{10,... | collective-permute-start | bytes 196616 | tf_op jit(solution)/shard_map/ppermute | solution.py:475
  63.7 0.2 collective-permute-start.14
  63.9 1.2 %collective-permute-start.13 = (f32[2,64,128]{2,1,0:T(8,128)S(1)}, f32[2,64,128]{2,1,0:T(8,128)S(1)}, u32[]{:S(2)}, u32[]{:S(2)}) collective-permute-start(f32[2,64,128]{2,1,0:T(8,128)S(1)} %last_gram.1.refs_0_), channel_id=1, source_target_pairs={{0,1},{1,0},{2,3},{3,2},{4,5},{5,4},{6,7},{7,6},{8,9},{9,8},{10,11... | collective-permute-start | bytes 196616 | tf_op jit(solution)/shard_map/ppermute | solution.py:475
  65.1 2.1 %collective-permute-done.15.refs_3_ = f32[2,64,128]{2,1,0:T(8,128)S(1)} collective-permute-done((f32[2,64,128]{2,1,0:T(8,128)S(1)}, f32[2,64,128]{2,1,0:T(8,128)S(1)}, u32[]{:S(2)}, u32[]{:S(2)}) %collective-permute-start.15) | collective-permute-done | bytes 65568 | tf_op jit(solution)/shard_map/ppermute | solution.py:475
  67.2 1.6 %collective-permute-done.14.refs_2_ = f32[2,64,128]{2,1,0:T(8,128)S(1)} collective-permute-done((f32[2,64,128]{2,1,0:T(8,128)S(1)}, f32[2,64,128]{2,1,0:T(8,128)S(1)}, u32[]{:S(2)}, u32[]{:S(2)}) %collective-permute-start.14) | collective-permute-done | bytes 65568 | tf_op jit(solution)/shard_map/ppermute | solution.py:475
  68.8 0.0 collective-permute-done.13.refs_1_
  68.8 5.6 %beams.1 = bf16[2,2,128,2048]{3,2,1,0:T(8,128)(2,1)} custom-call(f32[2,64,128]{2,1,0:T(8,128)S(1)} %last_gram.1.refs_0_, f32[2,64,128]{2,1,0:T(8,128)S(1)} %collective-permute-done.13.refs_1_, f32[2,64,128]{2,1,0:T(8,128)S(1)} %collective-permute-done.14.refs_2_, f32[2,64,128]{2,1,0:T(8,128)S(1)} %collective-permute-done.15.refs_3_, ...), custom_call_target="tpu_custom_call" | custom-call | flops 1000 | bytes 1000 | tf_op jit(solution)/shard_map/beams/pallas_call | solution.py:460
Async XLA Ops:
  0.0 11.5 %copy-start.1 = (s32[128]{0:T(128)S(1)}, s32[128]{0:T(128)}, u32[]{:S(2)}) copy-start(s32[128]{0:T(128)} %param.8) | copy-start | bytes 1540
  0.0 11.5 %copy-start = (f32[2,128]{1,0:T(2,128)S(1)}, f32[2,128]{1,0:T(2,128)}, u32[]{:S(2)}) copy-start(f32[2,128]{1,0:T(2,128)} %refs_4_.1) | copy-start | bytes 3076
  0.9 10.5 %collective-permute-start = (bf16[16,32,128]{2,1,0:T(8,128)(2,1)S(1)}, bf16[16,32,128]{2,1,0:T(8,128)(2,1)S(1)}, u32[]{:S(2)}, u32[]{:S(2)}) collective-permute-start(bf16[16,32,128]{2,1,0:T(8,128)(2,1)S(1)} %slice.3), channel_id=1, source_target_pairs={{0,1},{1,2},{2,3},{4,5},{5,6},{6,7},{8,9},{9,10},{10,11},{12,13},{... | collective-permute-start | bytes 393224 | tf_op jit(solution)/shard_map/ppermute | solution.py:508
  8.9 8.3 %collective-permute-start.1 = (bf16[2,2,16,1024]{3,2,1,0:T(8,128)(2,1)S(1)}, bf16[2,2,16,1024]{3,2,1,0:T(8,128)(2,1)S(1)}, u32[]{:S(2)}, u32[]{:S(2)}) collective-permute-start(bf16[2,2,16,1024]{3,2,1,0:T(8,128)(2,1)S(1)} %get-tuple-element.56), channel_id=1, source_target_pairs={{0,16},{4,20},{8,24},{12,28},{16,0},{20,4},{24,8},{28,12},{1,17},{... | collective-permute-start | bytes 393224 | tf_op jit(solution)/shard_map/ppermute | solution.py:475
  11.3 5.9 %collective-permute-start.2 = (bf16[2,2,16,1024]{3,2,1,0:T(8,128)(2,1)S(1)}, bf16[2,2,16,1024]{3,2,1,0:T(8,128)(2,1)S(1)}, u32[]{:S(2)}, u32[]{:S(2)}) collective-permute-start(bf16[2,2,16,1024]{3,2,1,0:T(8,128)(2,1)S(1)} %get-tuple-element.57), channel_id=1, source_target_pairs={{0,8},{4,12},{8,0},{12,4},{16,24},{20,28},{24,16},{28,20},{1,9},{5... | collective-permute-start | bytes 393224 | tf_op jit(solution)/shard_map/ppermute | solution.py:475
  17.2 19.9 %collective-permute-start.7 = (bf16[2,2,16,2048]{3,2,1,0:T(8,128)(2,1)S(1)}, bf16[2,2,16,2048]{3,2,1,0:T(8,128)(2,1)S(1)}, u32[]{:S(2)}, u32[]{:S(2)}) collective-permute-start(bf16[2,2,16,2048]{3,2,1,0:T(8,128)(2,1)S(1)} %get-tuple-element.69), channel_id=1, source_target_pairs={{0,20},{4,16},{8,28},{12,24},{16,4},{20,0},{24,12},{28,8},{1,21},{... | collective-permute-start | bytes 786440 | tf_op jit(solution)/shard_map/ppermute | solution.py:475
  20.7 16.1 %collective-permute-start.4 = (bf16[2,2,16,1024]{3,2,1,0:T(8,128)(2,1)S(1)}, bf16[2,2,16,1024]{3,2,1,0:T(8,128)(2,1)S(1)}, u32[]{:S(2)}, u32[]{:S(2)}) collective-permute-start(bf16[2,2,16,1024]{3,2,1,0:T(8,128)(2,1)S(1)} %get-tuple-element.61), channel_id=1, source_target_pairs={{0,16},{4,20},{8,24},{12,28},{16,0},{20,4},{24,8},{28,12},{1,17},{... | collective-permute-start | bytes 393224 | tf_op jit(solution)/shard_map/ppermute | solution.py:475
  21.0 15.8 %collective-permute-start.5 = (bf16[2,2,16,1024]{3,2,1,0:T(8,128)(2,1)S(1)}, bf16[2,2,16,1024]{3,2,1,0:T(8,128)(2,1)S(1)}, u32[]{:S(2)}, u32[]{:S(2)}) collective-permute-start(bf16[2,2,16,1024]{3,2,1,0:T(8,128)(2,1)S(1)} %get-tuple-element.62), channel_id=1, source_target_pairs={{0,8},{4,12},{8,0},{12,4},{16,24},{20,28},{24,16},{28,20},{1,9},{5... | collective-permute-start | bytes 393224 | tf_op jit(solution)/shard_map/ppermute | solution.py:475
  21.7 17.1 %collective-permute-start.3 = (bf16[2,2,16,2048]{3,2,1,0:T(8,128)(2,1)S(1)}, bf16[2,2,16,2048]{3,2,1,0:T(8,128)(2,1)S(1)}, u32[]{:S(2)}, u32[]{:S(2)}) collective-permute-start(bf16[2,2,16,2048]{3,2,1,0:T(8,128)(2,1)S(1)} %get-tuple-element.59), channel_id=1, source_target_pairs={{0,4},{4,0},{8,12},{12,8},{16,20},{20,16},{24,28},{28,24},{1,5},{5... | collective-permute-start | bytes 786440 | tf_op jit(solution)/shard_map/ppermute | solution.py:475
  21.7 17.1 %collective-permute-start.6 = (bf16[2,2,16,2048]{3,2,1,0:T(8,128)(2,1)S(1)}, bf16[2,2,16,2048]{3,2,1,0:T(8,128)(2,1)S(1)}, u32[]{:S(2)}, u32[]{:S(2)}) collective-permute-start(bf16[2,2,16,2048]{3,2,1,0:T(8,128)(2,1)S(1)} %get-tuple-element.65), channel_id=1, source_target_pairs={{0,12},{4,8},{8,4},{12,0},{16,28},{20,24},{24,20},{28,16},{1,13},{... | collective-permute-start | bytes 786440 | tf_op jit(solution)/shard_map/ppermute | solution.py:475
  36.8 18.7 %collective-permute-start.8 = (bf16[2,2,16,2048]{3,2,1,0:T(8,128)(2,1)S(1)}, bf16[2,2,16,2048]{3,2,1,0:T(8,128)(2,1)S(1)}, u32[]{:S(2)}, u32[]{:S(2)}) collective-permute-start(bf16[2,2,16,2048]{3,2,1,0:T(8,128)(2,1)S(1)} %get-tuple-element.71), channel_id=1, source_target_pairs={{0,24},{4,28},{8,16},{12,20},{16,8},{20,12},{24,0},{28,4},{1,25},{... | collective-permute-start | bytes 786440 | tf_op jit(solution)/shard_map/ppermute | solution.py:475
  37.1 24.5 %collective-permute-start.9 = (bf16[2,2,16,2048]{3,2,1,0:T(8,128)(2,1)S(1)}, bf16[2,2,16,2048]{3,2,1,0:T(8,128)(2,1)S(1)}, u32[]{:S(2)}, u32[]{:S(2)}) collective-permute-start(bf16[2,2,16,2048]{3,2,1,0:T(8,128)(2,1)S(1)} %get-tuple-element.72), channel_id=1, source_target_pairs={{0,28},{4,24},{8,20},{12,16},{16,12},{20,8},{24,4},{28,0},{1,29},{... | collective-permute-start | bytes 786440 | tf_op jit(solution)/shard_map/ppermute | solution.py:475
  39.5 5.5 %collective-permute-start.12 = (f32[2,96,128]{2,1,0:T(8,128)S(1)}, f32[2,96,128]{2,1,0:T(8,128)S(1)}, u32[]{:S(2)}, u32[]{:S(2)}) collective-permute-start(f32[2,96,128]{2,1,0:T(8,128)S(1)} %first_gram.1.refs_0_), channel_id=1, source_target_pairs={{0,3},{1,2},{2,1},{3,0},{4,7},{5,6},{6,5},{7,4},{8,11},{9,10},{10,... | collective-permute-start | bytes 294920 | tf_op jit(solution)/shard_map/ppermute | solution.py:475
  40.8 6.6 %collective-permute-start.11 = (f32[2,96,128]{2,1,0:T(8,128)S(1)}, f32[2,96,128]{2,1,0:T(8,128)S(1)}, u32[]{:S(2)}, u32[]{:S(2)}) collective-permute-start(f32[2,96,128]{2,1,0:T(8,128)S(1)} %first_gram.1.refs_0_), channel_id=1, source_target_pairs={{0,2},{1,3},{2,0},{3,1},{4,6},{5,7},{6,4},{7,5},{8,10},{9,11},{10,... | collective-permute-start | bytes 294920 | tf_op jit(solution)/shard_map/ppermute | solution.py:475
  41.1 6.3 %collective-permute-start.10 = (f32[2,96,128]{2,1,0:T(8,128)S(1)}, f32[2,96,128]{2,1,0:T(8,128)S(1)}, u32[]{:S(2)}, u32[]{:S(2)}) collective-permute-start(f32[2,96,128]{2,1,0:T(8,128)S(1)} %first_gram.1.refs_0_), channel_id=1, source_target_pairs={{0,1},{1,0},{2,3},{3,2},{4,5},{5,4},{6,7},{7,6},{8,9},{9,8},{10,11... | collective-permute-start | bytes 294920 | tf_op jit(solution)/shard_map/ppermute | solution.py:475
  62.4 4.8 %collective-permute-start.15 = (f32[2,64,128]{2,1,0:T(8,128)S(1)}, f32[2,64,128]{2,1,0:T(8,128)S(1)}, u32[]{:S(2)}, u32[]{:S(2)}) collective-permute-start(f32[2,64,128]{2,1,0:T(8,128)S(1)} %last_gram.1.refs_0_), channel_id=1, source_target_pairs={{0,3},{1,2},{2,1},{3,0},{4,7},{5,6},{6,5},{7,4},{8,11},{9,10},{10,... | collective-permute-start | bytes 196616 | tf_op jit(solution)/shard_map/ppermute | solution.py:475
  63.7 5.2 %collective-permute-start.14 = (f32[2,64,128]{2,1,0:T(8,128)S(1)}, f32[2,64,128]{2,1,0:T(8,128)S(1)}, u32[]{:S(2)}, u32[]{:S(2)}) collective-permute-start(f32[2,64,128]{2,1,0:T(8,128)S(1)} %last_gram.1.refs_0_), channel_id=1, source_target_pairs={{0,2},{1,3},{2,0},{3,1},{4,6},{5,7},{6,4},{7,5},{8,10},{9,11},{10,... | collective-permute-start | bytes 196616 | tf_op jit(solution)/shard_map/ppermute | solution.py:475
  63.9 4.9 %collective-permute-start.13 = (f32[2,64,128]{2,1,0:T(8,128)S(1)}, f32[2,64,128]{2,1,0:T(8,128)S(1)}, u32[]{:S(2)}, u32[]{:S(2)}) collective-permute-start(f32[2,64,128]{2,1,0:T(8,128)S(1)} %last_gram.1.refs_0_), channel_id=1, source_target_pairs={{0,1},{1,0},{2,3},{3,2},{4,5},{5,4},{6,7},{7,6},{8,9},{9,8},{10,11... | collective-permute-start | bytes 196616 | tf_op jit(solution)/shard_map/ppermute | solution.py:475

commit v5 on v4

--- a/solution.py
+++ b/solution.py
@@ -502,7 +502,7 @@
     order = list(range(owners))
     late_ones = far[len(far) // 2 :]
     known = (owners - len(late_ones)) * stations
-    split = far[:1] + near[1:][: max(len(near) - 2, 1)]
+    split = far[:1] + near[1:] + far[1:2]
     rest = [d for d in order if d not in split]
     layout = [[(slot, d) for slot in range(slots)] for d in split + rest]
     halo = lax.ppermute(voltages[:, :, snaps - LANES :], "seg", [(i, i + 1) for i in range(segments - 1)])
@@ -512,12 +512,14 @@
     *first, steer = channelize(
         slots, "first", order, layout, chan_table, voltages, filter_taps, halo, positions, beam_dirs, joined
     )
-    first, steer, late = after(first, steer, late)
+    at = len(split) - 1
+    first, steer, late[:at] = after(first, steer, late[:at])
+    first[at], late[at] = after(first[at], late[at])
     first = dict(zip(split + rest, first))
     arrived = {d: partners(first[d], "stn", d) for d in split + rest[1:] if d not in late_ones}
     following = {}
     for i, d in enumerate(late_ones):
-        ahead = [far[i]] + [e for e in near if e in split][i :: len(late_ones)]
+        ahead = [far[i]] + (near[1:] if d == far[-1] else [])
         value, there = after(first[d], [arrived[e] for e in ahead])
         arrived.update(zip(ahead, there))
         following[d] = partners(value, "stn", d)

time: 74.7 us -> 73.8 us (0.988)
  waiting for transfers between devices: 31.5 us -> 27.4 us
  starting transfers between devices: 18.8 us -> 21.9 us
    ppermute x15 -> x17, waiting for transfers between devices: 31.5 us -> 27.4 us  [partners(): return lax.ppermute(value, axis, [(i, i ^ distance) for i in range(length)])]
    ppermute x15 -> x17, starting transfers between devices: 15.7 us -> 18.8 us  [partners(): return lax.ppermute(value, axis, [(i, i ^ distance) for i in range(length)])]
  transfers between devices with their start and end apart: 16 -> 18, of which waited for: 8 -> 9; matrix products, arithmetic and copies ran while one was open for 0% -> 0% of each run, Pallas kernels for 23% -> 23%
where the time goes in v5:
time: 73.8 us; the launch traced here: 73.6 us
  waiting for transfers between devices  27.4 us (37%)
  Pallas kernels  23.2 us (31%)
  starting transfers between devices  21.9 us (30%)
  local copies, waits for them, and re-layouts  0.95 us (1%)
    ppermute x17, waiting for transfers between devices, partners(): return lax.ppermute(value, axis, [(i, i ^ distance) for i in range(length)])  27.4 us
    ppermute x17, starting transfers between devices, partners(): return lax.ppermute(value, axis, [(i, i ^ distance) for i in range(length)])  18.8 us
    pallas_call x2, Pallas kernels, channelize(): pl.pallas_call(functools.partial(channelize_kernel, owners, slots, part,...  9.91 us
    pallas_call x1, Pallas kernels, first_solve(): pl.pallas_call(functools.partial(first_solve_kernel, len(grams), snap_tot...  6.19 us
    pallas_call x1, Pallas kernels, beams(): pl.pallas_call(functools.partial(beams_kernel, len(grams), snap_total, nu...  5.62 us
    ppermute x1, starting transfers between devices, on_device(): lax.ppermute(voltages[:, :, snaps - LANES:], 'seg', [(i, i + 1) for i in...  3.12 us
  transfers between devices with their start and end apart: 18, of which 9 were waited for; matrix products, arithmetic and copies ran while one was open for 0% of the time, Pallas kernels for 23%

profile of v5, /device:TPU:11, one launch (start us, length us, event | category | flops | bytes accessed | tf_op | source)
XLA Modules:
  0.0 73.6 jit_solution(58560410926062705)
XLA Ops:
  0.0 0.0 copy-start.1
  0.0 0.0 copy-start
  0.0 0.9 %slice.3 = bf16[16,32,128]{2,1,0:T(8,128)(2,1)S(1)} slice(bf16[16,32,2048]{2,1,0:T(8,128)(2,1)} %refs_1_.3), slice={[0:16], [0:32], [1920:2048]} | slice | bytes 262144 | tf_op jit(solution)/shard_map/slice | solution.py:508
  0.9 3.1 %collective-permute-start = (bf16[16,32,128]{2,1,0:T(8,128)(2,1)S(1)}, bf16[16,32,128]{2,1,0:T(8,128)(2,1)S(1)}, u32[]{:S(2)}, u32[]{:S(2)}) collective-permute-start(bf16[16,32,128]{2,1,0:T(8,128)(2,1)S(1)} %slice.3), channel_id=1, source_target_pairs={{0,1},{1,2},{2,3},{4,5},{5,6},{6,7},{8,9},{9,10},{10,11},{12,13},{... | collective-permute-start | bytes 393224 | tf_op jit(solution)/shard_map/ppermute | solution.py:508
  4.1 4.8 %channelize_second.1 = (bf16[2,2,16,1024]{3,2,1,0:T(8,128)(2,1)S(1)}, bf16[2,2,16,1024]{3,2,1,0:T(8,128)(2,1)S(1)}, bf16[2,2,16,1024]{3,2,1,0:T(8,128)(2,1)S(1)}...) custom-call(s32[16]{0:T(128)} %refs_0_.3, ...), custom_call_target="tpu_custom_call" | custom-call | flops 1000 | bytes 1000 | tf_op jit(solution)/shard_map/channelize_second/pallas_call | solution.py:165
  8.9 2.4 %collective-permute-start.1 = (bf16[2,2,16,1024]{3,2,1,0:T(8,128)(2,1)S(1)}, bf16[2,2,16,1024]{3,2,1,0:T(8,128)(2,1)S(1)}, u32[]{:S(2)}, u32[]{:S(2)}) collective-permute-start(bf16[2,2,16,1024]{3,2,1,0:T(8,128)(2,1)S(1)} %get-tuple-element.58), channel_id=1, source_target_pairs={{0,16},{4,20},{8,24},{12,28},{16,0},{20,4},{24,8},{28,12},{1,17},{... | collective-permute-start | bytes 393224 | tf_op jit(solution)/shard_map/ppermute | solution.py:475
  11.3 0.2 collective-permute-start.2
  11.5 2.7 %collective-permute-start.3 = (bf16[2,2,16,1024]{3,2,1,0:T(8,128)(2,1)S(1)}, bf16[2,2,16,1024]{3,2,1,0:T(8,128)(2,1)S(1)}, u32[]{:S(2)}, u32[]{:S(2)}) collective-permute-start(bf16[2,2,16,1024]{3,2,1,0:T(8,128)(2,1)S(1)} %get-tuple-element.60), channel_id=1, source_target_pairs={{0,12},{4,8},{8,4},{12,0},{16,28},{20,24},{24,20},{28,16},{1,13},{... | collective-permute-start | bytes 393224 | tf_op jit(solution)/shard_map/ppermute | solution.py:475
  14.2 0.0 collective-permute-start.5
  14.2 0.0 collective-permute-done.refs_3_
  14.2 0.0 copy-done.1
  14.2 0.0 copy-done
  14.2 5.1 %channelize_first.1 = (bf16[2,2,16,1024]{3,2,1,0:T(8,128)(2,1)S(1)}, bf16[2,2,16,1024]{3,2,1,0:T(8,128)(2,1)S(1)}, bf16[2,2,16,1024]{3,2,1,0:T(8,128)(2,1)S(1)},...) custom-call(s32[16]{0:T(128)} %refs_0_.3, ...), custom_call_target="tpu_custom_call" | custom-call | flops 1000 | bytes 1000 | tf_op jit(solution)/shard_map/channelize_first/pallas_call | solution.py:165
  19.3 0.0 collective-permute-done.1.refs_7_.refs_13_
  19.3 0.0 collective-permute-done.2.refs_3_.refs_9_
  19.3 3.2 %collective-permute-done.3.refs_5_.refs_11_ = bf16[2,2,16,1024]{3,2,1,0:T(8,128)(2,1)S(1)} collective-permute-done((bf16[2,2,16,1024]{3,2,1,0:T(8,128)(2,1)S(1)}, bf16[2,2,16,1024]{3,2,1,0:T(8,128)(2,1)S(1)}, u32[]{:S(2)}, u32[]{:S(2)}) %collective-permute-start.3) | collective-permute-done | bytes 131104 | tf_op jit(solution)/shard_map/ppermute | solution.py:475
  22.5 1.1 %collective-permute-done.5.refs_9_.refs_15_ = bf16[2,2,16,1024]{3,2,1,0:T(8,128)(2,1)S(1)} collective-permute-done((bf16[2,2,16,1024]{3,2,1,0:T(8,128)(2,1)S(1)}, bf16[2,2,16,1024]{3,2,1,0:T(8,128)(2,1)S(1)}, u32[]{:S(2)}, u32[]{:S(2)}) %collective-permute-start.5) | collective-permute-done | bytes 131104 | tf_op jit(solution)/shard_map/ppermute | solution.py:475
  23.6 1.3 %collective-permute-start.6 = (bf16[2,2,16,1024]{3,2,1,0:T(8,128)(2,1)S(1)}, bf16[2,2,16,1024]{3,2,1,0:T(8,128)(2,1)S(1)}, u32[]{:S(2)}, u32[]{:S(2)}) collective-permute-start(bf16[2,2,16,1024]{3,2,1,0:T(8,128)(2,1)S(1)} %get-tuple-element.66), channel_id=1, source_target_pairs={{0,20},{4,16},{8,28},{12,24},{16,4},{20,0},{24,12},{28,8},{1,21},{... | collective-permute-start | bytes 393224 | tf_op jit(solution)/shard_map/ppermute | solution.py:475
  24.9 0.3 collective-permute-start.7
  25.1 2.0 %collective-permute-start.8 = (bf16[2,2,16,1024]{3,2,1,0:T(8,128)(2,1)S(1)}, bf16[2,2,16,1024]{3,2,1,0:T(8,128)(2,1)S(1)}, u32[]{:S(2)}, u32[]{:S(2)}) collective-permute-start(bf16[2,2,16,1024]{3,2,1,0:T(8,128)(2,1)S(1)} %get-tuple-element.68), channel_id=1, source_target_pairs={{0,12},{4,8},{8,4},{12,0},{16,28},{20,24},{24,20},{28,16},{1,13},{... | collective-permute-start | bytes 393224 | tf_op jit(solution)/shard_map/ppermute | solution.py:475
  27.1 0.8 %collective-permute-start.9 = (bf16[2,2,16,1024]{3,2,1,0:T(8,128)(2,1)S(1)}, bf16[2,2,16,1024]{3,2,1,0:T(8,128)(2,1)S(1)}, u32[]{:S(2)}, u32[]{:S(2)}) collective-permute-start(bf16[2,2,16,1024]{3,2,1,0:T(8,128)(2,1)S(1)} %get-tuple-element.74), channel_id=1, source_target_pairs={{0,16},{4,20},{8,24},{12,28},{16,0},{20,4},{24,8},{28,12},{1,17},{... | collective-permute-start | bytes 393224 | tf_op jit(solution)/shard_map/ppermute | solution.py:475
  28.0 0.0 collective-permute-start.4
  28.0 2.9 %collective-permute-done.6.refs_8_.refs_14_ = bf16[2,2,16,1024]{3,2,1,0:T(8,128)(2,1)S(1)} collective-permute-done((bf16[2,2,16,1024]{3,2,1,0:T(8,128)(2,1)S(1)}, bf16[2,2,16,1024]{3,2,1,0:T(8,128)(2,1)S(1)}, u32[]{:S(2)}, u32[]{:S(2)}) %collective-permute-start.6) | collective-permute-done | bytes 131104 | tf_op jit(solution)/shard_map/ppermute | solution.py:475
  30.9 0.0 collective-permute-done.7.refs_2_.refs_8_
  30.9 5.0 %collective-permute-done.8.refs_4_.refs_10_ = bf16[2,2,16,1024]{3,2,1,0:T(8,128)(2,1)S(1)} collective-permute-done((bf16[2,2,16,1024]{3,2,1,0:T(8,128)(2,1)S(1)}, bf16[2,2,16,1024]{3,2,1,0:T(8,128)(2,1)S(1)}, u32[]{:S(2)}, u32[]{:S(2)}) %collective-permute-start.8) | collective-permute-done | bytes 131104 | tf_op jit(solution)/shard_map/ppermute | solution.py:475
  35.9 0.0 collective-permute-done.9.refs_6_.refs_12_
  35.9 1.0 %collective-permute-start.10 = (bf16[2,2,16,2048]{3,2,1,0:T(8,128)(2,1)S(1)}, bf16[2,2,16,2048]{3,2,1,0:T(8,128)(2,1)S(1)}, u32[]{:S(2)}, u32[]{:S(2)}) collective-permute-start(bf16[2,2,16,2048]{3,2,1,0:T(8,128)(2,1)S(1)} %get-tuple-element.79), channel_id=1, source_target_pairs={{0,24},{4,28},{8,16},{12,20},{16,8},{20,12},{24,0},{28,4},{1,25},{... | collective-permute-start | bytes 786440 | tf_op jit(solution)/shard_map/ppermute | solution.py:475
  36.9 2.7 %collective-permute-start.11 = (bf16[2,2,16,2048]{3,2,1,0:T(8,128)(2,1)S(1)}, bf16[2,2,16,2048]{3,2,1,0:T(8,128)(2,1)S(1)}, u32[]{:S(2)}, u32[]{:S(2)}) collective-permute-start(bf16[2,2,16,2048]{3,2,1,0:T(8,128)(2,1)S(1)} %get-tuple-element.80), channel_id=1, source_target_pairs={{0,28},{4,24},{8,20},{12,16},{16,12},{20,8},{24,4},{28,0},{1,29},{... | collective-permute-start | bytes 786440 | tf_op jit(solution)/shard_map/ppermute | solution.py:475
  39.7 0.0 collective-permute-done.4.refs_1_.refs_7_
  39.7 0.7 first_gram.1.refs_0_
  40.4 1.3 %collective-permute-start.14 = (f32[2,96,128]{2,1,0:T(8,128)S(1)}, f32[2,96,128]{2,1,0:T(8,128)S(1)}, u32[]{:S(2)}, u32[]{:S(2)}) collective-permute-start(f32[2,96,128]{2,1,0:T(8,128)S(1)} %first_gram.1.refs_0_), channel_id=1, source_target_pairs={{0,3},{1,2},{2,1},{3,0},{4,7},{5,6},{6,5},{7,4},{8,11},{9,10},{10,... | collective-permute-start | bytes 294920 | tf_op jit(solution)/shard_map/ppermute | solution.py:475
  41.6 0.3 collective-permute-start.13
  41.9 1.2 %collective-permute-start.12 = (f32[2,96,128]{2,1,0:T(8,128)S(1)}, f32[2,96,128]{2,1,0:T(8,128)S(1)}, u32[]{:S(2)}, u32[]{:S(2)}) collective-permute-start(f32[2,96,128]{2,1,0:T(8,128)S(1)} %first_gram.1.refs_0_), channel_id=1, source_target_pairs={{0,1},{1,0},{2,3},{3,2},{4,5},{5,4},{6,7},{7,6},{8,9},{9,8},{10,11... | collective-permute-start | bytes 294920 | tf_op jit(solution)/shard_map/ppermute | solution.py:475
  43.1 2.8 %collective-permute-done.14.refs_3_ = f32[2,96,128]{2,1,0:T(8,128)S(1)} collective-permute-done((f32[2,96,128]{2,1,0:T(8,128)S(1)}, f32[2,96,128]{2,1,0:T(8,128)S(1)}, u32[]{:S(2)}, u32[]{:S(2)}) %collective-permute-start.14) | collective-permute-done | bytes 98336 | tf_op jit(solution)/shard_map/ppermute | solution.py:475
  45.9 2.3 %collective-permute-done.13.refs_2_ = f32[2,96,128]{2,1,0:T(8,128)S(1)} collective-permute-done((f32[2,96,128]{2,1,0:T(8,128)S(1)}, f32[2,96,128]{2,1,0:T(8,128)S(1)}, u32[]{:S(2)}, u32[]{:S(2)}) %collective-permute-start.13) | collective-permute-done | bytes 98336 | tf_op jit(solution)/shard_map/ppermute | solution.py:475
  48.2 0.0 collective-permute-done.12.refs_1_
  48.2 6.2 %first_solve.1.refs_4_ = f32[2,2,128,384]{3,2,1,0:T(8,128)S(1)} custom-call(f32[2,96,128]{2,1,0:T(8,128)S(1)} %first_gram.1.refs_0_, f32[2,96,128]{2,1,0:T(8,128)S(1)} %collective-permute-done.12.refs_1_, f32[2,96,128]{2,1,0:T(8,128)S(1)} %collective-permute-done.13.refs_2_, f32[2,96,128]{2,1,0:T(8,128)S(1)} %collective-permute-done.14.refs_3_, ...), custom_call_target="tpu_custom_call" | custom-call | flops 1000 | bytes 1000 | tf_op jit(solution)/shard_map/first_solve/pallas_call | solution.py:375
  54.4 0.0 collective-permute-done.10.refs_10_.refs_16_
  54.4 6.4 %collective-permute-done.11.refs_11_.refs_17_ = bf16[2,2,16,2048]{3,2,1,0:T(8,128)(2,1)S(1)} collective-permute-done((bf16[2,2,16,2048]{3,2,1,0:T(8,128)(2,1)S(1)}, bf16[2,2,16,2048]{3,2,1,0:T(8,128)(2,1)S(1)}, u32[]{:S(2)}, u32[]{:S(2)}) %collective-permute-start.11) | collective-permute-done | bytes 262176 | tf_op jit(solution)/shard_map/ppermute | solution.py:475
  60.8 0.8 %last_gram.1.refs_0_ = f32[2,64,128]{2,1,0:T(8,128)S(1)} custom-call(bf16[2,2,16,2048]{3,2,1,0:T(8,128)(2,1)S(1)} %get-tuple-element.61.refs_0_.refs_6_, bf16[2,2,16,2048]{3,2,1,0:T(8,128)(2,1)S(1)} %collective-permute-done.4.refs_1_.refs_7_, bf16[2,2,16,1024]{3,2,1,0:T(8,128)(2,1)S(1)} %collective-permute-done.7.refs_2_.refs_8_, ...), custom_call_target="tpu_custom_call" | custom-call | flops 1000 | bytes 1000 | tf_op jit(solution)/shard_map/last_gram/pallas_call | solution.py:241
  61.6 1.3 %collective-permute-start.17 = (f32[2,64,128]{2,1,0:T(8,128)S(1)}, f32[2,64,128]{2,1,0:T(8,128)S(1)}, u32[]{:S(2)}, u32[]{:S(2)}) collective-permute-start(f32[2,64,128]{2,1,0:T(8,128)S(1)} %last_gram.1.refs_0_), channel_id=1, source_target_pairs={{0,3},{1,2},{2,1},{3,0},{4,7},{5,6},{6,5},{7,4},{8,11},{9,10},{10,... | collective-permute-start | bytes 196616 | tf_op jit(solution)/shard_map/ppermute | solution.py:475
  62.8 0.2 collective-permute-start.16
  63.1 1.2 %collective-permute-start.15 = (f32[2,64,128]{2,1,0:T(8,128)S(1)}, f32[2,64,128]{2,1,0:T(8,128)S(1)}, u32[]{:S(2)}, u32[]{:S(2)}) collective-permute-start(f32[2,64,128]{2,1,0:T(8,128)S(1)} %last_gram.1.refs_0_), channel_id=1, source_target_pairs={{0,1},{1,0},{2,3},{3,2},{4,5},{5,4},{6,7},{7,6},{8,9},{9,8},{10,11... | collective-permute-start | bytes 196616 | tf_op jit(solution)/shard_map/ppermute | solution.py:475
  64.3 2.3 %collective-permute-done.17.refs_3_ = f32[2,64,128]{2,1,0:T(8,128)S(1)} collective-permute-done((f32[2,64,128]{2,1,0:T(8,128)S(1)}, f32[2,64,128]{2,1,0:T(8,128)S(1)}, u32[]{:S(2)}, u32[]{:S(2)}) %collective-permute-start.17) | collective-permute-done | bytes 65568 | tf_op jit(solution)/shard_map/ppermute | solution.py:475
  66.5 1.4 %collective-permute-done.16.refs_2_ = f32[2,64,128]{2,1,0:T(8,128)S(1)} collective-permute-done((f32[2,64,128]{2,1,0:T(8,128)S(1)}, f32[2,64,128]{2,1,0:T(8,128)S(1)}, u32[]{:S(2)}, u32[]{:S(2)}) %collective-permute-start.16) | collective-permute-done | bytes 65568 | tf_op jit(solution)/shard_map/ppermute | solution.py:475
  68.0 0.0 collective-permute-done.15.refs_1_
  68.0 5.6 %beams.1 = bf16[2,2,128,2048]{3,2,1,0:T(8,128)(2,1)} custom-call(f32[2,64,128]{2,1,0:T(8,128)S(1)} %last_gram.1.refs_0_, f32[2,64,128]{2,1,0:T(8,128)S(1)} %collective-permute-done.15.refs_1_, f32[2,64,128]{2,1,0:T(8,128)S(1)} %collective-permute-done.16.refs_2_, f32[2,64,128]{2,1,0:T(8,128)S(1)} %collective-permute-done.17.refs_3_, ...), custom_call_target="tpu_custom_call" | custom-call | flops 1000 | bytes 1000 | tf_op jit(solution)/shard_map/beams/pallas_call | solution.py:460
Async XLA Ops:
  0.0 14.2 %copy-start.1 = (s32[128]{0:T(128)S(1)}, s32[128]{0:T(128)}, u32[]{:S(2)}) copy-start(s32[128]{0:T(128)} %param.8) | copy-start | bytes 1540
  0.0 14.2 %copy-start = (f32[2,128]{1,0:T(2,128)S(1)}, f32[2,128]{1,0:T(2,128)}, u32[]{:S(2)}) copy-start(f32[2,128]{1,0:T(2,128)} %refs_4_.1) | copy-start | bytes 3076
  0.9 13.2 %collective-permute-start = (bf16[16,32,128]{2,1,0:T(8,128)(2,1)S(1)}, bf16[16,32,128]{2,1,0:T(8,128)(2,1)S(1)}, u32[]{:S(2)}, u32[]{:S(2)}) collective-permute-start(bf16[16,32,128]{2,1,0:T(8,128)(2,1)S(1)} %slice.3), channel_id=1, source_target_pairs={{0,1},{1,2},{2,3},{4,5},{5,6},{6,7},{8,9},{9,10},{10,11},{12,13},{... | collective-permute-start | bytes 393224 | tf_op jit(solution)/shard_map/ppermute | solution.py:508
  8.9 10.3 %collective-permute-start.1 = (bf16[2,2,16,1024]{3,2,1,0:T(8,128)(2,1)S(1)}, bf16[2,2,16,1024]{3,2,1,0:T(8,128)(2,1)S(1)}, u32[]{:S(2)}, u32[]{:S(2)}) collective-permute-start(bf16[2,2,16,1024]{3,2,1,0:T(8,128)(2,1)S(1)} %get-tuple-element.58), channel_id=1, source_target_pairs={{0,16},{4,20},{8,24},{12,28},{16,0},{20,4},{24,8},{28,12},{1,17},{... | collective-permute-start | bytes 393224 | tf_op jit(solution)/shard_map/ppermute | solution.py:475
  11.3 8.0 %collective-permute-start.2 = (bf16[2,2,16,1024]{3,2,1,0:T(8,128)(2,1)S(1)}, bf16[2,2,16,1024]{3,2,1,0:T(8,128)(2,1)S(1)}, u32[]{:S(2)}, u32[]{:S(2)}) collective-permute-start(bf16[2,2,16,1024]{3,2,1,0:T(8,128)(2,1)S(1)} %get-tuple-element.59), channel_id=1, source_target_pairs={{0,8},{4,12},{8,0},{12,4},{16,24},{20,28},{24,16},{28,20},{1,9},{5... | collective-permute-start | bytes 393224 | tf_op jit(solution)/shard_map/ppermute | solution.py:475
  11.5 11.0 %collective-permute-start.3 = (bf16[2,2,16,1024]{3,2,1,0:T(8,128)(2,1)S(1)}, bf16[2,2,16,1024]{3,2,1,0:T(8,128)(2,1)S(1)}, u32[]{:S(2)}, u32[]{:S(2)}) collective-permute-start(bf16[2,2,16,1024]{3,2,1,0:T(8,128)(2,1)S(1)} %get-tuple-element.60), channel_id=1, source_target_pairs={{0,12},{4,8},{8,4},{12,0},{16,28},{20,24},{24,20},{28,16},{1,13},{... | collective-permute-start | bytes 393224 | tf_op jit(solution)/shard_map/ppermute | solution.py:475
  14.2 9.4 %collective-permute-start.5 = (bf16[2,2,16,1024]{3,2,1,0:T(8,128)(2,1)S(1)}, bf16[2,2,16,1024]{3,2,1,0:T(8,128)(2,1)S(1)}, u32[]{:S(2)}, u32[]{:S(2)}) collective-permute-start(bf16[2,2,16,1024]{3,2,1,0:T(8,128)(2,1)S(1)} %get-tuple-element.65), channel_id=1, source_target_pairs={{0,20},{4,16},{8,28},{12,24},{16,4},{20,0},{24,12},{28,8},{1,21},{... | collective-permute-start | bytes 393224 | tf_op jit(solution)/shard_map/ppermute | solution.py:475
  23.6 7.3 %collective-permute-start.6 = (bf16[2,2,16,1024]{3,2,1,0:T(8,128)(2,1)S(1)}, bf16[2,2,16,1024]{3,2,1,0:T(8,128)(2,1)S(1)}, u32[]{:S(2)}, u32[]{:S(2)}) collective-permute-start(bf16[2,2,16,1024]{3,2,1,0:T(8,128)(2,1)S(1)} %get-tuple-element.66), channel_id=1, source_target_pairs={{0,20},{4,16},{8,28},{12,24},{16,4},{20,0},{24,12},{28,8},{1,21},{... | collective-permute-start | bytes 393224 | tf_op jit(solution)/shard_map/ppermute | solution.py:475
  24.9 6.0 %collective-permute-start.7 = (bf16[2,2,16,1024]{3,2,1,0:T(8,128)(2,1)S(1)}, bf16[2,2,16,1024]{3,2,1,0:T(8,128)(2,1)S(1)}, u32[]{:S(2)}, u32[]{:S(2)}) collective-permute-start(bf16[2,2,16,1024]{3,2,1,0:T(8,128)(2,1)S(1)} %get-tuple-element.67), channel_id=1, source_target_pairs={{0,8},{4,12},{8,0},{12,4},{16,24},{20,28},{24,16},{28,20},{1,9},{5... | collective-permute-start | bytes 393224 | tf_op jit(solution)/shard_map/ppermute | solution.py:475
  25.1 10.8 %collective-permute-start.8 = (bf16[2,2,16,1024]{3,2,1,0:T(8,128)(2,1)S(1)}, bf16[2,2,16,1024]{3,2,1,0:T(8,128)(2,1)S(1)}, u32[]{:S(2)}, u32[]{:S(2)}) collective-permute-start(bf16[2,2,16,1024]{3,2,1,0:T(8,128)(2,1)S(1)} %get-tuple-element.68), channel_id=1, source_target_pairs={{0,12},{4,8},{8,4},{12,0},{16,28},{20,24},{24,20},{28,16},{1,13},{... | collective-permute-start | bytes 393224 | tf_op jit(solution)/shard_map/ppermute | solution.py:475
  27.1 8.8 %collective-permute-start.9 = (bf16[2,2,16,1024]{3,2,1,0:T(8,128)(2,1)S(1)}, bf16[2,2,16,1024]{3,2,1,0:T(8,128)(2,1)S(1)}, u32[]{:S(2)}, u32[]{:S(2)}) collective-permute-start(bf16[2,2,16,1024]{3,2,1,0:T(8,128)(2,1)S(1)} %get-tuple-element.74), channel_id=1, source_target_pairs={{0,16},{4,20},{8,24},{12,28},{16,0},{20,4},{24,8},{28,12},{1,17},{... | collective-permute-start | bytes 393224 | tf_op jit(solution)/shard_map/ppermute | solution.py:475
  28.0 11.7 %collective-permute-start.4 = (bf16[2,2,16,2048]{3,2,1,0:T(8,128)(2,1)S(1)}, bf16[2,2,16,2048]{3,2,1,0:T(8,128)(2,1)S(1)}, u32[]{:S(2)}, u32[]{:S(2)}) collective-permute-start(bf16[2,2,16,2048]{3,2,1,0:T(8,128)(2,1)S(1)} %get-tuple-element.62), channel_id=1, source_target_pairs={{0,4},{4,0},{8,12},{12,8},{16,20},{20,16},{24,28},{28,24},{1,5},{5... | collective-permute-start | bytes 786440 | tf_op jit(solution)/shard_map/ppermute | solution.py:475
  35.9 18.5 %collective-permute-start.10 = (bf16[2,2,16,2048]{3,2,1,0:T(8,128)(2,1)S(1)}, bf16[2,2,16,2048]{3,2,1,0:T(8,128)(2,1)S(1)}, u32[]{:S(2)}, u32[]{:S(2)}) collective-permute-start(bf16[2,2,16,2048]{3,2,1,0:T(8,128)(2,1)S(1)} %get-tuple-element.79), channel_id=1, source_target_pairs={{0,24},{4,28},{8,16},{12,20},{16,8},{20,12},{24,0},{28,4},{1,25},{... | collective-permute-start | bytes 786440 | tf_op jit(solution)/shard_map/ppermute | solution.py:475
  36.9 23.9 %collective-permute-start.11 = (bf16[2,2,16,2048]{3,2,1,0:T(8,128)(2,1)S(1)}, bf16[2,2,16,2048]{3,2,1,0:T(8,128)(2,1)S(1)}, u32[]{:S(2)}, u32[]{:S(2)}) collective-permute-start(bf16[2,2,16,2048]{3,2,1,0:T(8,128)(2,1)S(1)} %get-tuple-element.80), channel_id=1, source_target_pairs={{0,28},{4,24},{8,20},{12,16},{16,12},{20,8},{24,4},{28,0},{1,29},{... | collective-permute-start | bytes 786440 | tf_op jit(solution)/shard_map/ppermute | solution.py:475
  40.4 5.5 %collective-permute-start.14 = (f32[2,96,128]{2,1,0:T(8,128)S(1)}, f32[2,96,128]{2,1,0:T(8,128)S(1)}, u32[]{:S(2)}, u32[]{:S(2)}) collective-permute-start(f32[2,96,128]{2,1,0:T(8,128)S(1)} %first_gram.1.refs_0_), channel_id=1, source_target_pairs={{0,3},{1,2},{2,1},{3,0},{4,7},{5,6},{6,5},{7,4},{8,11},{9,10},{10,... | collective-permute-start | bytes 294920 | tf_op jit(solution)/shard_map/ppermute | solution.py:475
  41.6 6.6 %collective-permute-start.13 = (f32[2,96,128]{2,1,0:T(8,128)S(1)}, f32[2,96,128]{2,1,0:T(8,128)S(1)}, u32[]{:S(2)}, u32[]{:S(2)}) collective-permute-start(f32[2,96,128]{2,1,0:T(8,128)S(1)} %first_gram.1.refs_0_), channel_id=1, source_target_pairs={{0,2},{1,3},{2,0},{3,1},{4,6},{5,7},{6,4},{7,5},{8,10},{9,11},{10,... | collective-permute-start | bytes 294920 | tf_op jit(solution)/shard_map/ppermute | solution.py:475
  41.9 6.3 %collective-permute-start.12 = (f32[2,96,128]{2,1,0:T(8,128)S(1)}, f32[2,96,128]{2,1,0:T(8,128)S(1)}, u32[]{:S(2)}, u32[]{:S(2)}) collective-permute-start(f32[2,96,128]{2,1,0:T(8,128)S(1)} %first_gram.1.refs_0_), channel_id=1, source_target_pairs={{0,1},{1,0},{2,3},{3,2},{4,5},{5,4},{6,7},{7,6},{8,9},{9,8},{10,11... | collective-permute-start | bytes 294920 | tf_op jit(solution)/shard_map/ppermute | solution.py:475
  61.6 5.0 %collective-permute-start.17 = (f32[2,64,128]{2,1,0:T(8,128)S(1)}, f32[2,64,128]{2,1,0:T(8,128)S(1)}, u32[]{:S(2)}, u32[]{:S(2)}) collective-permute-start(f32[2,64,128]{2,1,0:T(8,128)S(1)} %last_gram.1.refs_0_), channel_id=1, source_target_pairs={{0,3},{1,2},{2,1},{3,0},{4,7},{5,6},{6,5},{7,4},{8,11},{9,10},{10,... | collective-permute-start | bytes 196616 | tf_op jit(solution)/shard_map/ppermute | solution.py:475
  62.8 5.1 %collective-permute-start.16 = (f32[2,64,128]{2,1,0:T(8,128)S(1)}, f32[2,64,128]{2,1,0:T(8,128)S(1)}, u32[]{:S(2)}, u32[]{:S(2)}) collective-permute-start(f32[2,64,128]{2,1,0:T(8,128)S(1)} %last_gram.1.refs_0_), channel_id=1, source_target_pairs={{0,2},{1,3},{2,0},{3,1},{4,6},{5,7},{6,4},{7,5},{8,10},{9,11},{10,... | collective-permute-start | bytes 196616 | tf_op jit(solution)/shard_map/ppermute | solution.py:475
  63.1 4.9 %collective-permute-start.15 = (f32[2,64,128]{2,1,0:T(8,128)S(1)}, f32[2,64,128]{2,1,0:T(8,128)S(1)}, u32[]{:S(2)}, u32[]{:S(2)}) collective-permute-start(f32[2,64,128]{2,1,0:T(8,128)S(1)} %last_gram.1.refs_0_), channel_id=1, source_target_pairs={{0,1},{1,0},{2,3},{3,2},{4,5},{5,4},{6,7},{7,6},{8,9},{9,8},{10,11... | collective-permute-start | bytes 196616 | tf_op jit(solution)/shard_map/ppermute | solution.py:475

commit v6 on v5

--- a/solution.py
+++ b/solution.py
@@ -417,37 +417,38 @@
 
 def beams_kernel(segments, snap_total, blocks, *refs):
     grams, swept, steer = refs[:segments], refs[segments], refs[segments + 1]
-    arrays, out, mix = refs[segments + 2 : -2], refs[-2], refs[-1]
+    arrays, (out, mix, mixed_beams, sems) = refs[segments + 2 : -4], refs[-4:]
     slots, double, half = grams[0].shape
     known = half - double // 2
     count = steer.shape[2]
 
-    @pl.when(pl.program_id(0) == 0)
-    def _():
-        systems = []
-        shape = (double // 2, half)
-        diagonal = lax.broadcasted_iota(jnp.int32, shape, 0) + known == lax.broadcasted_iota(jnp.int32, shape, 1)
-        for slot in range(slots):
-            rows = sum(one[slot] for one in grams) * (1.0 / snap_total)
-            rows_r, rows_i = rows[: double // 2], rows[double // 2 :]
-            rows_r = jnp.where(diagonal, rows_r + loading_level, rows_r)
-            steer_r, steer_i = steer[slot, :half], steer[slot, half:]
-            systems.append(joined_system(swept[slot, 0], swept[slot, 1], rows_r, rows_i, steer_r, steer_i, known))
-        for slot, (real, imag) in enumerate(eliminate(systems, known, half, math.gcd(known, PIVOTS), AT_ONCE)):
-            solved_r, solved_i = real[:, half:], imag[:, half:]
-            power = jnp.sum(steer[slot, :half] * solved_r + steer[slot, half:] * solved_i, axis=0, keepdims=True)
-            scale = 1.0 / jnp.sqrt(power)
-            weight_r, weight_i = (solved_r * scale).T, (solved_i * scale).T
-            mix[slot, :count] = jnp.concatenate([weight_r, weight_i], axis=1).astype(bf16)
-            mix[slot, count:] = jnp.concatenate([-weight_i, weight_r], axis=1).astype(bf16)
-
+    systems = []
+    shape = (double // 2, half)
+    diagonal = lax.broadcasted_iota(jnp.int32, shape, 0) + known == lax.broadcasted_iota(jnp.int32, shape, 1)
     for slot in range(slots):
-
-        @pl.when(pl.program_id(0) == slot)
-        def _():
-            mixed = jnp.dot(mix[slot], stacked_rows(blocks[slot], arrays), preferred_element_type=f32).astype(bf16)
-            out[0, 0] = mixed[:count]
-            out[0, 1] = mixed[count:]
+        rows = sum(one[slot] for one in grams) * (1.0 / snap_total)
+        rows_r, rows_i = rows[: double // 2], rows[double // 2 :]
+        rows_r = jnp.where(diagonal, rows_r + loading_level, rows_r)
+        steer_r, steer_i = steer[slot, :half], steer[slot, half:]
+        systems.append(joined_system(swept[slot, 0], swept[slot, 1], rows_r, rows_i, steer_r, steer_i, known))
+    for slot, (real, imag) in enumerate(eliminate(systems, known, half, math.gcd(known, PIVOTS), AT_ONCE)):
+        solved_r, solved_i = real[:, half:], imag[:, half:]
+        power = jnp.sum(steer[slot, :half] * solved_r + steer[slot, half:] * solved_i, axis=0, keepdims=True)
+        scale = 1.0 / jnp.sqrt(power)
+        weight_r, weight_i = (solved_r * scale).T, (solved_i * scale).T
+        mix[slot, :count] = jnp.concatenate([weight_r, weight_i], axis=1).astype(bf16)
+        mix[slot, count:] = jnp.concatenate([-weight_i, weight_r], axis=1).astype(bf16)
+
+    copies = []
+    for slot in range(slots):
+        stacked = stacked_rows(blocks[slot], arrays)
+        for part in range(2):
+            rows = mix[slot, part * count : (part + 1) * count]
+            mixed_beams[slot, part] = jnp.dot(rows, stacked, preferred_element_type=f32).astype(bf16)
+            copies.append(pltpu.make_async_copy(mixed_beams.at[slot, part], out.at[slot, part], sems.at[slot, part]))
+            copies[-1].start()
+    for copy in copies:
+        copy.wait()
 
 
 def beams(snap_total, grams, swept, steer, blocks):
@@ -459,11 +460,14 @@
     operands = [*grams, swept, steer, *arrays]
     return pl.pallas_call(
         functools.partial(beams_kernel, len(grams), snap_total, numbered),
-        grid=(slots,),
         in_specs=[pl.BlockSpec(memory_space=pltpu.VMEM)] * len(operands),
-        out_specs=pl.BlockSpec((1, 2, count, snaps), lambda i: (i, 0, 0, 0)),
+        out_specs=pl.BlockSpec(memory_space=pltpu.HBM),
         out_shape=jax.ShapeDtypeStruct((slots, 2, count, snaps), bf16),
-        scratch_shapes=[pltpu.VMEM((slots, 2 * count, double), bf16)],
+        scratch_shapes=[
+            pltpu.VMEM((slots, 2 * count, double), bf16),
+            pltpu.VMEM((slots, 2, count, snaps), bf16),
+            pltpu.SemaphoreType.DMA((slots, 2)),
+        ],
         compiler_params=pltpu.CompilerParams(vmem_limit_bytes=BEAMS_VMEM),
         cost_estimate=QUICK,
         name="beams",

time: 73.8 us -> 73.7 us (level)
  no operation moved by 1% of the time
where the time goes in v6:
time: 73.7 us; the launch traced here: 73.5 us
  waiting for transfers between devices  27.4 us (37%)
  Pallas kernels  22.9 us (31%)
  starting transfers between devices  21.9 us (30%)
  local copies, waits for them, and re-layouts  0.95 us (1%)
    ppermute x17, waiting for transfers between devices, partners(): return lax.ppermute(value, axis, [(i, i ^ distance) for i in range(length)])  27.4 us
    ppermute x17, starting transfers between devices, partners(): return lax.ppermute(value, axis, [(i, i ^ distance) for i in range(length)])  18.8 us
    pallas_call x2, Pallas kernels, channelize(): pl.pallas_call(functools.partial(channelize_kernel, owners, slots, part,...  9.91 us
    pallas_call x1, Pallas kernels, first_solve(): pl.pallas_call(functools.partial(first_solve_kernel, len(grams), snap_tot...  6.19 us
    pallas_call x1, Pallas kernels, beams(): pl.pallas_call(functools.partial(beams_kernel, len(grams), snap_total, nu...  5.39 us
    ppermute x1, starting transfers between devices, on_device(): lax.ppermute(voltages[:, :, snaps - LANES:], 'seg', [(i, i + 1) for i in...  3.12 us
  transfers between devices with their start and end apart: 18, of which 9 were waited for; matrix products, arithmetic and copies ran while one was open for 0% of the time, Pallas kernels for 23%

profile of v6, /device:TPU:11, one launch (start us, length us, event | category | flops | bytes accessed | tf_op | source)
XLA Modules:
  0.0 73.5 jit_solution(14678901918361236869)
XLA Ops:
  0.0 0.0 copy-start.1
  0.0 0.0 copy-start
  0.0 0.9 %slice.3 = bf16[16,32,128]{2,1,0:T(8,128)(2,1)S(1)} slice(bf16[16,32,2048]{2,1,0:T(8,128)(2,1)} %refs_1_.3), slice={[0:16], [0:32], [1920:2048]} | slice | bytes 262144 | tf_op jit(solution)/shard_map/slice | solution.py:512
  0.9 3.1 %collective-permute-start = (bf16[16,32,128]{2,1,0:T(8,128)(2,1)S(1)}, bf16[16,32,128]{2,1,0:T(8,128)(2,1)S(1)}, u32[]{:S(2)}, u32[]{:S(2)}) collective-permute-start(bf16[16,32,128]{2,1,0:T(8,128)(2,1)S(1)} %slice.3), channel_id=1, source_target_pairs={{0,1},{1,2},{2,3},{4,5},{5,6},{6,7},{8,9},{9,10},{10,11},{12,13},{... | collective-permute-start | bytes 393224 | tf_op jit(solution)/shard_map/ppermute | solution.py:512
  4.1 4.8 %channelize_second.1 = (bf16[2,2,16,1024]{3,2,1,0:T(8,128)(2,1)S(1)}, bf16[2,2,16,1024]{3,2,1,0:T(8,128)(2,1)S(1)}, bf16[2,2,16,1024]{3,2,1,0:T(8,128)(2,1)S(1)}...) custom-call(s32[16]{0:T(128)} %refs_0_.3, ...), custom_call_target="tpu_custom_call" | custom-call | flops 1000 | bytes 1000 | tf_op jit(solution)/shard_map/channelize_second/pallas_call | solution.py:165
  8.9 2.4 %collective-permute-start.1 = (bf16[2,2,16,1024]{3,2,1,0:T(8,128)(2,1)S(1)}, bf16[2,2,16,1024]{3,2,1,0:T(8,128)(2,1)S(1)}, u32[]{:S(2)}, u32[]{:S(2)}) collective-permute-start(bf16[2,2,16,1024]{3,2,1,0:T(8,128)(2,1)S(1)} %get-tuple-element.58), channel_id=1, source_target_pairs={{0,16},{4,20},{8,24},{12,28},{16,0},{20,4},{24,8},{28,12},{1,17},{... | collective-permute-start | bytes 393224 | tf_op jit(solution)/shard_map/ppermute | solution.py:479
  11.3 0.2 collective-permute-start.2
  11.5 2.7 %collective-permute-start.3 = (bf16[2,2,16,1024]{3,2,1,0:T(8,128)(2,1)S(1)}, bf16[2,2,16,1024]{3,2,1,0:T(8,128)(2,1)S(1)}, u32[]{:S(2)}, u32[]{:S(2)}) collective-permute-start(bf16[2,2,16,1024]{3,2,1,0:T(8,128)(2,1)S(1)} %get-tuple-element.60), channel_id=1, source_target_pairs={{0,12},{4,8},{8,4},{12,0},{16,28},{20,24},{24,20},{28,16},{1,13},{... | collective-permute-start | bytes 393224 | tf_op jit(solution)/shard_map/ppermute | solution.py:479
  14.2 0.0 collective-permute-start.5
  14.2 0.0 collective-permute-done.refs_3_
  14.2 0.0 copy-done.1
  14.2 0.0 copy-done
  14.2 5.1 %channelize_first.1 = (bf16[2,2,16,1024]{3,2,1,0:T(8,128)(2,1)S(1)}, bf16[2,2,16,1024]{3,2,1,0:T(8,128)(2,1)S(1)}, bf16[2,2,16,1024]{3,2,1,0:T(8,128)(2,1)S(1)},...) custom-call(s32[16]{0:T(128)} %refs_0_.3, ...), custom_call_target="tpu_custom_call" | custom-call | flops 1000 | bytes 1000 | tf_op jit(solution)/shard_map/channelize_first/pallas_call | solution.py:165
  19.3 0.0 collective-permute-done.1.refs_7_.refs_13_
  19.3 0.0 collective-permute-done.2.refs_3_.refs_9_
  19.3 3.2 %collective-permute-done.3.refs_5_.refs_11_ = bf16[2,2,16,1024]{3,2,1,0:T(8,128)(2,1)S(1)} collective-permute-done((bf16[2,2,16,1024]{3,2,1,0:T(8,128)(2,1)S(1)}, bf16[2,2,16,1024]{3,2,1,0:T(8,128)(2,1)S(1)}, u32[]{:S(2)}, u32[]{:S(2)}) %collective-permute-start.3) | collective-permute-done | bytes 131104 | tf_op jit(solution)/shard_map/ppermute | solution.py:479
  22.5 1.1 %collective-permute-done.5.refs_9_.refs_15_ = bf16[2,2,16,1024]{3,2,1,0:T(8,128)(2,1)S(1)} collective-permute-done((bf16[2,2,16,1024]{3,2,1,0:T(8,128)(2,1)S(1)}, bf16[2,2,16,1024]{3,2,1,0:T(8,128)(2,1)S(1)}, u32[]{:S(2)}, u32[]{:S(2)}) %collective-permute-start.5) | collective-permute-done | bytes 131104 | tf_op jit(solution)/shard_map/ppermute | solution.py:479
  23.6 1.3 %collective-permute-start.6 = (bf16[2,2,16,1024]{3,2,1,0:T(8,128)(2,1)S(1)}, bf16[2,2,16,1024]{3,2,1,0:T(8,128)(2,1)S(1)}, u32[]{:S(2)}, u32[]{:S(2)}) collective-permute-start(bf16[2,2,16,1024]{3,2,1,0:T(8,128)(2,1)S(1)} %get-tuple-element.66), channel_id=1, source_target_pairs={{0,20},{4,16},{8,28},{12,24},{16,4},{20,0},{24,12},{28,8},{1,21},{... | collective-permute-start | bytes 393224 | tf_op jit(solution)/shard_map/ppermute | solution.py:479
  24.9 0.3 collective-permute-start.7
  25.1 2.0 %collective-permute-start.8 = (bf16[2,2,16,1024]{3,2,1,0:T(8,128)(2,1)S(1)}, bf16[2,2,16,1024]{3,2,1,0:T(8,128)(2,1)S(1)}, u32[]{:S(2)}, u32[]{:S(2)}) collective-permute-start(bf16[2,2,16,1024]{3,2,1,0:T(8,128)(2,1)S(1)} %get-tuple-element.68), channel_id=1, source_target_pairs={{0,12},{4,8},{8,4},{12,0},{16,28},{20,24},{24,20},{28,16},{1,13},{... | collective-permute-start | bytes 393224 | tf_op jit(solution)/shard_map/ppermute | solution.py:479
  27.1 0.8 %collective-permute-start.9 = (bf16[2,2,16,1024]{3,2,1,0:T(8,128)(2,1)S(1)}, bf16[2,2,16,1024]{3,2,1,0:T(8,128)(2,1)S(1)}, u32[]{:S(2)}, u32[]{:S(2)}) collective-permute-start(bf16[2,2,16,1024]{3,2,1,0:T(8,128)(2,1)S(1)} %get-tuple-element.74), channel_id=1, source_target_pairs={{0,16},{4,20},{8,24},{12,28},{16,0},{20,4},{24,8},{28,12},{1,17},{... | collective-permute-start | bytes 393224 | tf_op jit(solution)/shard_map/ppermute | solution.py:479
  28.0 0.0 collective-permute-start.4
  28.0 2.9 %collective-permute-done.6.refs_8_.refs_14_ = bf16[2,2,16,1024]{3,2,1,0:T(8,128)(2,1)S(1)} collective-permute-done((bf16[2,2,16,1024]{3,2,1,0:T(8,128)(2,1)S(1)}, bf16[2,2,16,1024]{3,2,1,0:T(8,128)(2,1)S(1)}, u32[]{:S(2)}, u32[]{:S(2)}) %collective-permute-start.6) | collective-permute-done | bytes 131104 | tf_op jit(solution)/shard_map/ppermute | solution.py:479
  30.9 0.0 collective-permute-done.7.refs_2_.refs_8_
  30.9 5.0 %collective-permute-done.8.refs_4_.refs_10_ = bf16[2,2,16,1024]{3,2,1,0:T(8,128)(2,1)S(1)} collective-permute-done((bf16[2,2,16,1024]{3,2,1,0:T(8,128)(2,1)S(1)}, bf16[2,2,16,1024]{3,2,1,0:T(8,128)(2,1)S(1)}, u32[]{:S(2)}, u32[]{:S(2)}) %collective-permute-start.8) | collective-permute-done | bytes 131104 | tf_op jit(solution)/shard_map/ppermute | solution.py:479
  35.9 0.0 collective-permute-done.9.refs_6_.refs_12_
  35.9 1.0 %collective-permute-start.10 = (bf16[2,2,16,2048]{3,2,1,0:T(8,128)(2,1)S(1)}, bf16[2,2,16,2048]{3,2,1,0:T(8,128)(2,1)S(1)}, u32[]{:S(2)}, u32[]{:S(2)}) collective-permute-start(bf16[2,2,16,2048]{3,2,1,0:T(8,128)(2,1)S(1)} %get-tuple-element.79), channel_id=1, source_target_pairs={{0,24},{4,28},{8,16},{12,20},{16,8},{20,12},{24,0},{28,4},{1,25},{... | collective-permute-start | bytes 786440 | tf_op jit(solution)/shard_map/ppermute | solution.py:479
  36.9 2.7 %collective-permute-start.11 = (bf16[2,2,16,2048]{3,2,1,0:T(8,128)(2,1)S(1)}, bf16[2,2,16,2048]{3,2,1,0:T(8,128)(2,1)S(1)}, u32[]{:S(2)}, u32[]{:S(2)}) collective-permute-start(bf16[2,2,16,2048]{3,2,1,0:T(8,128)(2,1)S(1)} %get-tuple-element.80), channel_id=1, source_target_pairs={{0,28},{4,24},{8,20},{12,16},{16,12},{20,8},{24,4},{28,0},{1,29},{... | collective-permute-start | bytes 786440 | tf_op jit(solution)/shard_map/ppermute | solution.py:479
  39.7 0.0 collective-permute-done.4.refs_1_.refs_7_
  39.7 0.7 first_gram.1.refs_0_
  40.4 1.3 %collective-permute-start.14 = (f32[2,96,128]{2,1,0:T(8,128)S(1)}, f32[2,96,128]{2,1,0:T(8,128)S(1)}, u32[]{:S(2)}, u32[]{:S(2)}) collective-permute-start(f32[2,96,128]{2,1,0:T(8,128)S(1)} %first_gram.1.refs_0_), channel_id=1, source_target_pairs={{0,3},{1,2},{2,1},{3,0},{4,7},{5,6},{6,5},{7,4},{8,11},{9,10},{10,... | collective-permute-start | bytes 294920 | tf_op jit(solution)/shard_map/ppermute | solution.py:479
  41.6 0.3 collective-permute-start.13
  41.9 1.2 %collective-permute-start.12 = (f32[2,96,128]{2,1,0:T(8,128)S(1)}, f32[2,96,128]{2,1,0:T(8,128)S(1)}, u32[]{:S(2)}, u32[]{:S(2)}) collective-permute-start(f32[2,96,128]{2,1,0:T(8,128)S(1)} %first_gram.1.refs_0_), channel_id=1, source_target_pairs={{0,1},{1,0},{2,3},{3,2},{4,5},{5,4},{6,7},{7,6},{8,9},{9,8},{10,11... | collective-permute-start | bytes 294920 | tf_op jit(solution)/shard_map/ppermute | solution.py:479
  43.1 2.8 %collective-permute-done.14.refs_3_ = f32[2,96,128]{2,1,0:T(8,128)S(1)} collective-permute-done((f32[2,96,128]{2,1,0:T(8,128)S(1)}, f32[2,96,128]{2,1,0:T(8,128)S(1)}, u32[]{:S(2)}, u32[]{:S(2)}) %collective-permute-start.14) | collective-permute-done | bytes 98336 | tf_op jit(solution)/shard_map/ppermute | solution.py:479
  45.9 2.3 %collective-permute-done.13.refs_2_ = f32[2,96,128]{2,1,0:T(8,128)S(1)} collective-permute-done((f32[2,96,128]{2,1,0:T(8,128)S(1)}, f32[2,96,128]{2,1,0:T(8,128)S(1)}, u32[]{:S(2)}, u32[]{:S(2)}) %collective-permute-start.13) | collective-permute-done | bytes 98336 | tf_op jit(solution)/shard_map/ppermute | solution.py:479
  48.2 0.0 collective-permute-done.12.refs_1_
  48.2 6.2 %first_solve.1.refs_4_ = f32[2,2,128,384]{3,2,1,0:T(8,128)S(1)} custom-call(f32[2,96,128]{2,1,0:T(8,128)S(1)} %first_gram.1.refs_0_, f32[2,96,128]{2,1,0:T(8,128)S(1)} %collective-permute-done.12.refs_1_, f32[2,96,128]{2,1,0:T(8,128)S(1)} %collective-permute-done.13.refs_2_, f32[2,96,128]{2,1,0:T(8,128)S(1)} %collective-permute-done.14.refs_3_, ...), custom_call_target="tpu_custom_call" | custom-call | flops 1000 | bytes 1000 | tf_op jit(solution)/shard_map/first_solve/pallas_call | solution.py:375
  54.4 0.0 collective-permute-done.10.refs_10_.refs_16_
  54.4 6.4 %collective-permute-done.11.refs_11_.refs_17_ = bf16[2,2,16,2048]{3,2,1,0:T(8,128)(2,1)S(1)} collective-permute-done((bf16[2,2,16,2048]{3,2,1,0:T(8,128)(2,1)S(1)}, bf16[2,2,16,2048]{3,2,1,0:T(8,128)(2,1)S(1)}, u32[]{:S(2)}, u32[]{:S(2)}) %collective-permute-start.11) | collective-permute-done | bytes 262176 | tf_op jit(solution)/shard_map/ppermute | solution.py:479
  60.8 0.8 %last_gram.1.refs_0_ = f32[2,64,128]{2,1,0:T(8,128)S(1)} custom-call(bf16[2,2,16,2048]{3,2,1,0:T(8,128)(2,1)S(1)} %get-tuple-element.61.refs_0_.refs_6_, bf16[2,2,16,2048]{3,2,1,0:T(8,128)(2,1)S(1)} %collective-permute-done.4.refs_1_.refs_7_, bf16[2,2,16,1024]{3,2,1,0:T(8,128)(2,1)S(1)} %collective-permute-done.7.refs_2_.refs_8_, ...), custom_call_target="tpu_custom_call" | custom-call | flops 1000 | bytes 1000 | tf_op jit(solution)/shard_map/last_gram/pallas_call | solution.py:241
  61.6 1.3 %collective-permute-start.17 = (f32[2,64,128]{2,1,0:T(8,128)S(1)}, f32[2,64,128]{2,1,0:T(8,128)S(1)}, u32[]{:S(2)}, u32[]{:S(2)}) collective-permute-start(f32[2,64,128]{2,1,0:T(8,128)S(1)} %last_gram.1.refs_0_), channel_id=1, source_target_pairs={{0,3},{1,2},{2,1},{3,0},{4,7},{5,6},{6,5},{7,4},{8,11},{9,10},{10,... | collective-permute-start | bytes 196616 | tf_op jit(solution)/shard_map/ppermute | solution.py:479
  62.8 0.2 collective-permute-start.16
  63.1 1.2 %collective-permute-start.15 = (f32[2,64,128]{2,1,0:T(8,128)S(1)}, f32[2,64,128]{2,1,0:T(8,128)S(1)}, u32[]{:S(2)}, u32[]{:S(2)}) collective-permute-start(f32[2,64,128]{2,1,0:T(8,128)S(1)} %last_gram.1.refs_0_), channel_id=1, source_target_pairs={{0,1},{1,0},{2,3},{3,2},{4,5},{5,4},{6,7},{7,6},{8,9},{9,8},{10,11... | collective-permute-start | bytes 196616 | tf_op jit(solution)/shard_map/ppermute | solution.py:479
  64.3 2.3 %collective-permute-done.17.refs_3_ = f32[2,64,128]{2,1,0:T(8,128)S(1)} collective-permute-done((f32[2,64,128]{2,1,0:T(8,128)S(1)}, f32[2,64,128]{2,1,0:T(8,128)S(1)}, u32[]{:S(2)}, u32[]{:S(2)}) %collective-permute-start.17) | collective-permute-done | bytes 65568 | tf_op jit(solution)/shard_map/ppermute | solution.py:479
  66.5 1.4 %collective-permute-done.16.refs_2_ = f32[2,64,128]{2,1,0:T(8,128)S(1)} collective-permute-done((f32[2,64,128]{2,1,0:T(8,128)S(1)}, f32[2,64,128]{2,1,0:T(8,128)S(1)}, u32[]{:S(2)}, u32[]{:S(2)}) %collective-permute-start.16) | collective-permute-done | bytes 65568 | tf_op jit(solution)/shard_map/ppermute | solution.py:479
  68.0 0.0 collective-permute-done.15.refs_1_
  68.0 5.4 %beams.1 = bf16[2,2,128,2048]{3,2,1,0:T(8,128)(2,1)} custom-call(f32[2,64,128]{2,1,0:T(8,128)S(1)} %last_gram.1.refs_0_, f32[2,64,128]{2,1,0:T(8,128)S(1)} %collective-permute-done.15.refs_1_, f32[2,64,128]{2,1,0:T(8,128)S(1)} %collective-permute-done.16.refs_2_, f32[2,64,128]{2,1,0:T(8,128)S(1)} %collective-permute-done.17.refs_3_, ...), custom_call_target="tpu_custom_call" | custom-call | flops 1000 | bytes 1000 | tf_op jit(solution)/shard_map/beams/pallas_call | solution.py:461
Async XLA Ops:
  0.0 14.2 %copy-start.1 = (s32[128]{0:T(128)S(1)}, s32[128]{0:T(128)}, u32[]{:S(2)}) copy-start(s32[128]{0:T(128)} %param.8) | copy-start | bytes 1540
  0.0 14.2 %copy-start = (f32[2,128]{1,0:T(2,128)S(1)}, f32[2,128]{1,0:T(2,128)}, u32[]{:S(2)}) copy-start(f32[2,128]{1,0:T(2,128)} %refs_4_.1) | copy-start | bytes 3076
  0.9 13.2 %collective-permute-start = (bf16[16,32,128]{2,1,0:T(8,128)(2,1)S(1)}, bf16[16,32,128]{2,1,0:T(8,128)(2,1)S(1)}, u32[]{:S(2)}, u32[]{:S(2)}) collective-permute-start(bf16[16,32,128]{2,1,0:T(8,128)(2,1)S(1)} %slice.3), channel_id=1, source_target_pairs={{0,1},{1,2},{2,3},{4,5},{5,6},{6,7},{8,9},{9,10},{10,11},{12,13},{... | collective-permute-start | bytes 393224 | tf_op jit(solution)/shard_map/ppermute | solution.py:512
  8.9 10.3 %collective-permute-start.1 = (bf16[2,2,16,1024]{3,2,1,0:T(8,128)(2,1)S(1)}, bf16[2,2,16,1024]{3,2,1,0:T(8,128)(2,1)S(1)}, u32[]{:S(2)}, u32[]{:S(2)}) collective-permute-start(bf16[2,2,16,1024]{3,2,1,0:T(8,128)(2,1)S(1)} %get-tuple-element.58), channel_id=1, source_target_pairs={{0,16},{4,20},{8,24},{12,28},{16,0},{20,4},{24,8},{28,12},{1,17},{... | collective-permute-start | bytes 393224 | tf_op jit(solution)/shard_map/ppermute | solution.py:479
  11.3 8.0 %collective-permute-start.2 = (bf16[2,2,16,1024]{3,2,1,0:T(8,128)(2,1)S(1)}, bf16[2,2,16,1024]{3,2,1,0:T(8,128)(2,1)S(1)}, u32[]{:S(2)}, u32[]{:S(2)}) collective-permute-start(bf16[2,2,16,1024]{3,2,1,0:T(8,128)(2,1)S(1)} %get-tuple-element.59), channel_id=1, source_target_pairs={{0,8},{4,12},{8,0},{12,4},{16,24},{20,28},{24,16},{28,20},{1,9},{5... | collective-permute-start | bytes 393224 | tf_op jit(solution)/shard_map/ppermute | solution.py:479
  11.5 11.0 %collective-permute-start.3 = (bf16[2,2,16,1024]{3,2,1,0:T(8,128)(2,1)S(1)}, bf16[2,2,16,1024]{3,2,1,0:T(8,128)(2,1)S(1)}, u32[]{:S(2)}, u32[]{:S(2)}) collective-permute-start(bf16[2,2,16,1024]{3,2,1,0:T(8,128)(2,1)S(1)} %get-tuple-element.60), channel_id=1, source_target_pairs={{0,12},{4,8},{8,4},{12,0},{16,28},{20,24},{24,20},{28,16},{1,13},{... | collective-permute-start | bytes 393224 | tf_op jit(solution)/shard_map/ppermute | solution.py:479
  14.2 9.4 %collective-permute-start.5 = (bf16[2,2,16,1024]{3,2,1,0:T(8,128)(2,1)S(1)}, bf16[2,2,16,1024]{3,2,1,0:T(8,128)(2,1)S(1)}, u32[]{:S(2)}, u32[]{:S(2)}) collective-permute-start(bf16[2,2,16,1024]{3,2,1,0:T(8,128)(2,1)S(1)} %get-tuple-element.65), channel_id=1, source_target_pairs={{0,20},{4,16},{8,28},{12,24},{16,4},{20,0},{24,12},{28,8},{1,21},{... | collective-permute-start | bytes 393224 | tf_op jit(solution)/shard_map/ppermute | solution.py:479
  23.6 7.3 %collective-permute-start.6 = (bf16[2,2,16,1024]{3,2,1,0:T(8,128)(2,1)S(1)}, bf16[2,2,16,1024]{3,2,1,0:T(8,128)(2,1)S(1)}, u32[]{:S(2)}, u32[]{:S(2)}) collective-permute-start(bf16[2,2,16,1024]{3,2,1,0:T(8,128)(2,1)S(1)} %get-tuple-element.66), channel_id=1, source_target_pairs={{0,20},{4,16},{8,28},{12,24},{16,4},{20,0},{24,12},{28,8},{1,21},{... | collective-permute-start | bytes 393224 | tf_op jit(solution)/shard_map/ppermute | solution.py:479
  24.9 6.0 %collective-permute-start.7 = (bf16[2,2,16,1024]{3,2,1,0:T(8,128)(2,1)S(1)}, bf16[2,2,16,1024]{3,2,1,0:T(8,128)(2,1)S(1)}, u32[]{:S(2)}, u32[]{:S(2)}) collective-permute-start(bf16[2,2,16,1024]{3,2,1,0:T(8,128)(2,1)S(1)} %get-tuple-element.67), channel_id=1, source_target_pairs={{0,8},{4,12},{8,0},{12,4},{16,24},{20,28},{24,16},{28,20},{1,9},{5... | collective-permute-start | bytes 393224 | tf_op jit(solution)/shard_map/ppermute | solution.py:479
  25.1 10.8 %collective-permute-start.8 = (bf16[2,2,16,1024]{3,2,1,0:T(8,128)(2,1)S(1)}, bf16[2,2,16,1024]{3,2,1,0:T(8,128)(2,1)S(1)}, u32[]{:S(2)}, u32[]{:S(2)}) collective-permute-start(bf16[2,2,16,1024]{3,2,1,0:T(8,128)(2,1)S(1)} %get-tuple-element.68), channel_id=1, source_target_pairs={{0,12},{4,8},{8,4},{12,0},{16,28},{20,24},{24,20},{28,16},{1,13},{... | collective-permute-start | bytes 393224 | tf_op jit(solution)/shard_map/ppermute | solution.py:479
  27.1 8.8 %collective-permute-start.9 = (bf16[2,2,16,1024]{3,2,1,0:T(8,128)(2,1)S(1)}, bf16[2,2,16,1024]{3,2,1,0:T(8,128)(2,1)S(1)}, u32[]{:S(2)}, u32[]{:S(2)}) collective-permute-start(bf16[2,2,16,1024]{3,2,1,0:T(8,128)(2,1)S(1)} %get-tuple-element.74), channel_id=1, source_target_pairs={{0,16},{4,20},{8,24},{12,28},{16,0},{20,4},{24,8},{28,12},{1,17},{... | collective-permute-start | bytes 393224 | tf_op jit(solution)/shard_map/ppermute | solution.py:479
  28.0 11.7 %collective-permute-start.4 = (bf16[2,2,16,2048]{3,2,1,0:T(8,128)(2,1)S(1)}, bf16[2,2,16,2048]{3,2,1,0:T(8,128)(2,1)S(1)}, u32[]{:S(2)}, u32[]{:S(2)}) collective-permute-start(bf16[2,2,16,2048]{3,2,1,0:T(8,128)(2,1)S(1)} %get-tuple-element.62), channel_id=1, source_target_pairs={{0,4},{4,0},{8,12},{12,8},{16,20},{20,16},{24,28},{28,24},{1,5},{5... | collective-permute-start | bytes 786440 | tf_op jit(solution)/shard_map/ppermute | solution.py:479
  35.9 18.5 %collective-permute-start.10 = (bf16[2,2,16,2048]{3,2,1,0:T(8,128)(2,1)S(1)}, bf16[2,2,16,2048]{3,2,1,0:T(8,128)(2,1)S(1)}, u32[]{:S(2)}, u32[]{:S(2)}) collective-permute-start(bf16[2,2,16,2048]{3,2,1,0:T(8,128)(2,1)S(1)} %get-tuple-element.79), channel_id=1, source_target_pairs={{0,24},{4,28},{8,16},{12,20},{16,8},{20,12},{24,0},{28,4},{1,25},{... | collective-permute-start | bytes 786440 | tf_op jit(solution)/shard_map/ppermute | solution.py:479
  36.9 23.9 %collective-permute-start.11 = (bf16[2,2,16,2048]{3,2,1,0:T(8,128)(2,1)S(1)}, bf16[2,2,16,2048]{3,2,1,0:T(8,128)(2,1)S(1)}, u32[]{:S(2)}, u32[]{:S(2)}) collective-permute-start(bf16[2,2,16,2048]{3,2,1,0:T(8,128)(2,1)S(1)} %get-tuple-element.80), channel_id=1, source_target_pairs={{0,28},{4,24},{8,20},{12,16},{16,12},{20,8},{24,4},{28,0},{1,29},{... | collective-permute-start | bytes 786440 | tf_op jit(solution)/shard_map/ppermute | solution.py:479
  40.4 5.5 %collective-permute-start.14 = (f32[2,96,128]{2,1,0:T(8,128)S(1)}, f32[2,96,128]{2,1,0:T(8,128)S(1)}, u32[]{:S(2)}, u32[]{:S(2)}) collective-permute-start(f32[2,96,128]{2,1,0:T(8,128)S(1)} %first_gram.1.refs_0_), channel_id=1, source_target_pairs={{0,3},{1,2},{2,1},{3,0},{4,7},{5,6},{6,5},{7,4},{8,11},{9,10},{10,... | collective-permute-start | bytes 294920 | tf_op jit(solution)/shard_map/ppermute | solution.py:479
  41.6 6.6 %collective-permute-start.13 = (f32[2,96,128]{2,1,0:T(8,128)S(1)}, f32[2,96,128]{2,1,0:T(8,128)S(1)}, u32[]{:S(2)}, u32[]{:S(2)}) collective-permute-start(f32[2,96,128]{2,1,0:T(8,128)S(1)} %first_gram.1.refs_0_), channel_id=1, source_target_pairs={{0,2},{1,3},{2,0},{3,1},{4,6},{5,7},{6,4},{7,5},{8,10},{9,11},{10,... | collective-permute-start | bytes 294920 | tf_op jit(solution)/shard_map/ppermute | solution.py:479
  41.9 6.3 %collective-permute-start.12 = (f32[2,96,128]{2,1,0:T(8,128)S(1)}, f32[2,96,128]{2,1,0:T(8,128)S(1)}, u32[]{:S(2)}, u32[]{:S(2)}) collective-permute-start(f32[2,96,128]{2,1,0:T(8,128)S(1)} %first_gram.1.refs_0_), channel_id=1, source_target_pairs={{0,1},{1,0},{2,3},{3,2},{4,5},{5,4},{6,7},{7,6},{8,9},{9,8},{10,11... | collective-permute-start | bytes 294920 | tf_op jit(solution)/shard_map/ppermute | solution.py:479
  61.6 5.0 %collective-permute-start.17 = (f32[2,64,128]{2,1,0:T(8,128)S(1)}, f32[2,64,128]{2,1,0:T(8,128)S(1)}, u32[]{:S(2)}, u32[]{:S(2)}) collective-permute-start(f32[2,64,128]{2,1,0:T(8,128)S(1)} %last_gram.1.refs_0_), channel_id=1, source_target_pairs={{0,3},{1,2},{2,1},{3,0},{4,7},{5,6},{6,5},{7,4},{8,11},{9,10},{10,... | collective-permute-start | bytes 196616 | tf_op jit(solution)/shard_map/ppermute | solution.py:479
  62.8 5.1 %collective-permute-start.16 = (f32[2,64,128]{2,1,0:T(8,128)S(1)}, f32[2,64,128]{2,1,0:T(8,128)S(1)}, u32[]{:S(2)}, u32[]{:S(2)}) collective-permute-start(f32[2,64,128]{2,1,0:T(8,128)S(1)} %last_gram.1.refs_0_), channel_id=1, source_target_pairs={{0,2},{1,3},{2,0},{3,1},{4,6},{5,7},{6,4},{7,5},{8,10},{9,11},{10,... | collective-permute-start | bytes 196616 | tf_op jit(solution)/shard_map/ppermute | solution.py:479
  63.1 4.9 %collective-permute-start.15 = (f32[2,64,128]{2,1,0:T(8,128)S(1)}, f32[2,64,128]{2,1,0:T(8,128)S(1)}, u32[]{:S(2)}, u32[]{:S(2)}) collective-permute-start(f32[2,64,128]{2,1,0:T(8,128)S(1)} %last_gram.1.refs_0_), channel_id=1, source_target_pairs={{0,1},{1,0},{2,3},{3,2},{4,5},{5,4},{6,7},{7,6},{8,9},{9,8},{10,11... | collective-permute-start | bytes 196616 | tf_op jit(solution)/shard_map/ppermute | solution.py:479

commit v7 on v6

--- a/solution.py
+++ b/solution.py
@@ -516,9 +516,7 @@
     *first, steer = channelize(
         slots, "first", order, layout, chan_table, voltages, filter_taps, halo, positions, beam_dirs, joined
     )
-    at = len(split) - 1
-    first, steer, late[:at] = after(first, steer, late[:at])
-    first[at], late[at] = after(first[at], late[at])
+    first, steer, late = after(first, steer, late)
     first = dict(zip(split + rest, first))
     arrived = {d: partners(first[d], "stn", d) for d in split + rest[1:] if d not in late_ones}
     following = {}

time: 73.7 us -> 73.7 us (level)
  no operation moved by 1% of the time
where the time goes in v7:
time: 73.7 us; the launch traced here: 73.5 us
  waiting for transfers between devices  27.4 us (37%)
  Pallas kernels  22.9 us (31%)
  starting transfers between devices  21.9 us (30%)
  local copies, waits for them, and re-layouts  0.95 us (1%)
    ppermute x17, waiting for transfers between devices, partners(): return lax.ppermute(value, axis, [(i, i ^ distance) for i in range(length)])  27.4 us
    ppermute x17, starting transfers between devices, partners(): return lax.ppermute(value, axis, [(i, i ^ distance) for i in range(length)])  18.8 us
    pallas_call x2, Pallas kernels, channelize(): pl.pallas_call(functools.partial(channelize_kernel, owners, slots, part,...  9.91 us
    pallas_call x1, Pallas kernels, first_solve(): pl.pallas_call(functools.partial(first_solve_kernel, len(grams), snap_tot...  6.19 us
    pallas_call x1, Pallas kernels, beams(): pl.pallas_call(functools.partial(beams_kernel, len(grams), snap_total, nu...  5.39 us
    ppermute x1, starting transfers between devices, on_device(): lax.ppermute(voltages[:, :, snaps - LANES:], 'seg', [(i, i + 1) for i in...  3.12 us
  transfers between devices with their start and end apart: 18, of which 9 were waited for; matrix products, arithmetic and copies ran while one was open for 0% of the time, Pallas kernels for 23%

profile of v7, /device:TPU:11, one launch (start us, length us, event | category | flops | bytes accessed | tf_op | source)
XLA Modules:
  0.0 73.5 jit_solution(14678901918361236869)
XLA Ops:
  0.0 0.0 copy-start.1
  0.0 0.0 copy-start
  0.0 0.9 %slice.3 = bf16[16,32,128]{2,1,0:T(8,128)(2,1)S(1)} slice(bf16[16,32,2048]{2,1,0:T(8,128)(2,1)} %refs_1_.3), slice={[0:16], [0:32], [1920:2048]} | slice | bytes 262144 | tf_op jit(solution)/shard_map/slice | solution.py:512
  0.9 3.1 %collective-permute-start = (bf16[16,32,128]{2,1,0:T(8,128)(2,1)S(1)}, bf16[16,32,128]{2,1,0:T(8,128)(2,1)S(1)}, u32[]{:S(2)}, u32[]{:S(2)}) collective-permute-start(bf16[16,32,128]{2,1,0:T(8,128)(2,1)S(1)} %slice.3), channel_id=1, source_target_pairs={{0,1},{1,2},{2,3},{4,5},{5,6},{6,7},{8,9},{9,10},{10,11},{12,13},{... | collective-permute-start | bytes 393224 | tf_op jit(solution)/shard_map/ppermute | solution.py:512
  4.1 4.8 %channelize_second.1 = (bf16[2,2,16,1024]{3,2,1,0:T(8,128)(2,1)S(1)}, bf16[2,2,16,1024]{3,2,1,0:T(8,128)(2,1)S(1)}, bf16[2,2,16,1024]{3,2,1,0:T(8,128)(2,1)S(1)}...) custom-call(s32[16]{0:T(128)} %refs_0_.3, ...), custom_call_target="tpu_custom_call" | custom-call | flops 1000 | bytes 1000 | tf_op jit(solution)/shard_map/channelize_second/pallas_call | solution.py:165
  8.9 2.4 %collective-permute-start.1 = (bf16[2,2,16,1024]{3,2,1,0:T(8,128)(2,1)S(1)}, bf16[2,2,16,1024]{3,2,1,0:T(8,128)(2,1)S(1)}, u32[]{:S(2)}, u32[]{:S(2)}) collective-permute-start(bf16[2,2,16,1024]{3,2,1,0:T(8,128)(2,1)S(1)} %get-tuple-element.57), channel_id=1, source_target_pairs={{0,16},{4,20},{8,24},{12,28},{16,0},{20,4},{24,8},{28,12},{1,17},{... | collective-permute-start | bytes 393224 | tf_op jit(solution)/shard_map/ppermute | solution.py:479
  11.3 0.2 collective-permute-start.2
  11.5 2.7 %collective-permute-start.3 = (bf16[2,2,16,1024]{3,2,1,0:T(8,128)(2,1)S(1)}, bf16[2,2,16,1024]{3,2,1,0:T(8,128)(2,1)S(1)}, u32[]{:S(2)}, u32[]{:S(2)}) collective-permute-start(bf16[2,2,16,1024]{3,2,1,0:T(8,128)(2,1)S(1)} %get-tuple-element.59), channel_id=1, source_target_pairs={{0,12},{4,8},{8,4},{12,0},{16,28},{20,24},{24,20},{28,16},{1,13},{... | collective-permute-start | bytes 393224 | tf_op jit(solution)/shard_map/ppermute | solution.py:479
  14.2 0.0 collective-permute-start.4
  14.2 0.0 collective-permute-done.refs_3_
  14.2 0.0 copy-done.1
  14.2 0.0 copy-done
  14.2 5.1 %channelize_first.1 = (bf16[2,2,16,1024]{3,2,1,0:T(8,128)(2,1)S(1)}, bf16[2,2,16,1024]{3,2,1,0:T(8,128)(2,1)S(1)}, bf16[2,2,16,1024]{3,2,1,0:T(8,128)(2,1)S(1)},...) custom-call(s32[16]{0:T(128)} %refs_0_.3, ...), custom_call_target="tpu_custom_call" | custom-call | flops 1000 | bytes 1000 | tf_op jit(solution)/shard_map/channelize_first/pallas_call | solution.py:165
  19.3 0.0 collective-permute-done.1.refs_7_.refs_13_
  19.3 0.0 collective-permute-done.2.refs_3_.refs_9_
  19.3 3.2 %collective-permute-done.3.refs_5_.refs_11_ = bf16[2,2,16,1024]{3,2,1,0:T(8,128)(2,1)S(1)} collective-permute-done((bf16[2,2,16,1024]{3,2,1,0:T(8,128)(2,1)S(1)}, bf16[2,2,16,1024]{3,2,1,0:T(8,128)(2,1)S(1)}, u32[]{:S(2)}, u32[]{:S(2)}) %collective-permute-start.3) | collective-permute-done | bytes 131104 | tf_op jit(solution)/shard_map/ppermute | solution.py:479
  22.5 1.1 %collective-permute-done.4.refs_9_.refs_15_ = bf16[2,2,16,1024]{3,2,1,0:T(8,128)(2,1)S(1)} collective-permute-done((bf16[2,2,16,1024]{3,2,1,0:T(8,128)(2,1)S(1)}, bf16[2,2,16,1024]{3,2,1,0:T(8,128)(2,1)S(1)}, u32[]{:S(2)}, u32[]{:S(2)}) %collective-permute-start.4) | collective-permute-done | bytes 131104 | tf_op jit(solution)/shard_map/ppermute | solution.py:479
  23.6 1.3 %collective-permute-start.6 = (bf16[2,2,16,1024]{3,2,1,0:T(8,128)(2,1)S(1)}, bf16[2,2,16,1024]{3,2,1,0:T(8,128)(2,1)S(1)}, u32[]{:S(2)}, u32[]{:S(2)}) collective-permute-start(bf16[2,2,16,1024]{3,2,1,0:T(8,128)(2,1)S(1)} %get-tuple-element.64), channel_id=1, source_target_pairs={{0,20},{4,16},{8,28},{12,24},{16,4},{20,0},{24,12},{28,8},{1,21},{... | collective-permute-start | bytes 393224 | tf_op jit(solution)/shard_map/ppermute | solution.py:479
  24.9 0.3 collective-permute-start.7
  25.1 2.0 %collective-permute-start.8 = (bf16[2,2,16,1024]{3,2,1,0:T(8,128)(2,1)S(1)}, bf16[2,2,16,1024]{3,2,1,0:T(8,128)(2,1)S(1)}, u32[]{:S(2)}, u32[]{:S(2)}) collective-permute-start(bf16[2,2,16,1024]{3,2,1,0:T(8,128)(2,1)S(1)} %get-tuple-element.66), channel_id=1, source_target_pairs={{0,12},{4,8},{8,4},{12,0},{16,28},{20,24},{24,20},{28,16},{1,13},{... | collective-permute-start | bytes 393224 | tf_op jit(solution)/shard_map/ppermute | solution.py:479
  27.1 0.8 %collective-permute-start.9 = (bf16[2,2,16,1024]{3,2,1,0:T(8,128)(2,1)S(1)}, bf16[2,2,16,1024]{3,2,1,0:T(8,128)(2,1)S(1)}, u32[]{:S(2)}, u32[]{:S(2)}) collective-permute-start(bf16[2,2,16,1024]{3,2,1,0:T(8,128)(2,1)S(1)} %get-tuple-element.72), channel_id=1, source_target_pairs={{0,16},{4,20},{8,24},{12,28},{16,0},{20,4},{24,8},{28,12},{1,17},{... | collective-permute-start | bytes 393224 | tf_op jit(solution)/shard_map/ppermute | solution.py:479
  28.0 0.0 collective-permute-start.5
  28.0 2.9 %collective-permute-done.6.refs_8_.refs_14_ = bf16[2,2,16,1024]{3,2,1,0:T(8,128)(2,1)S(1)} collective-permute-done((bf16[2,2,16,1024]{3,2,1,0:T(8,128)(2,1)S(1)}, bf16[2,2,16,1024]{3,2,1,0:T(8,128)(2,1)S(1)}, u32[]{:S(2)}, u32[]{:S(2)}) %collective-permute-start.6) | collective-permute-done | bytes 131104 | tf_op jit(solution)/shard_map/ppermute | solution.py:479
  30.9 0.0 collective-permute-done.7.refs_2_.refs_8_
  30.9 5.0 %collective-permute-done.8.refs_4_.refs_10_ = bf16[2,2,16,1024]{3,2,1,0:T(8,128)(2,1)S(1)} collective-permute-done((bf16[2,2,16,1024]{3,2,1,0:T(8,128)(2,1)S(1)}, bf16[2,2,16,1024]{3,2,1,0:T(8,128)(2,1)S(1)}, u32[]{:S(2)}, u32[]{:S(2)}) %collective-permute-start.8) | collective-permute-done | bytes 131104 | tf_op jit(solution)/shard_map/ppermute | solution.py:479
  35.9 0.0 collective-permute-done.9.refs_6_.refs_12_
  35.9 1.0 %collective-permute-start.10 = (bf16[2,2,16,2048]{3,2,1,0:T(8,128)(2,1)S(1)}, bf16[2,2,16,2048]{3,2,1,0:T(8,128)(2,1)S(1)}, u32[]{:S(2)}, u32[]{:S(2)}) collective-permute-start(bf16[2,2,16,2048]{3,2,1,0:T(8,128)(2,1)S(1)} %get-tuple-element.77), channel_id=1, source_target_pairs={{0,24},{4,28},{8,16},{12,20},{16,8},{20,12},{24,0},{28,4},{1,25},{... | collective-permute-start | bytes 786440 | tf_op jit(solution)/shard_map/ppermute | solution.py:479
  36.9 2.7 %collective-permute-start.11 = (bf16[2,2,16,2048]{3,2,1,0:T(8,128)(2,1)S(1)}, bf16[2,2,16,2048]{3,2,1,0:T(8,128)(2,1)S(1)}, u32[]{:S(2)}, u32[]{:S(2)}) collective-permute-start(bf16[2,2,16,2048]{3,2,1,0:T(8,128)(2,1)S(1)} %get-tuple-element.78), channel_id=1, source_target_pairs={{0,28},{4,24},{8,20},{12,16},{16,12},{20,8},{24,4},{28,0},{1,29},{... | collective-permute-start | bytes 786440 | tf_op jit(solution)/shard_map/ppermute | solution.py:479
  39.7 0.0 collective-permute-done.5.refs_1_.refs_7_
  39.7 0.7 first_gram.1.refs_0_
  40.4 1.3 %collective-permute-start.14 = (f32[2,96,128]{2,1,0:T(8,128)S(1)}, f32[2,96,128]{2,1,0:T(8,128)S(1)}, u32[]{:S(2)}, u32[]{:S(2)}) collective-permute-start(f32[2,96,128]{2,1,0:T(8,128)S(1)} %first_gram.1.refs_0_), channel_id=1, source_target_pairs={{0,3},{1,2},{2,1},{3,0},{4,7},{5,6},{6,5},{7,4},{8,11},{9,10},{10,... | collective-permute-start | bytes 294920 | tf_op jit(solution)/shard_map/ppermute | solution.py:479
  41.6 0.3 collective-permute-start.13
  41.9 1.2 %collective-permute-start.12 = (f32[2,96,128]{2,1,0:T(8,128)S(1)}, f32[2,96,128]{2,1,0:T(8,128)S(1)}, u32[]{:S(2)}, u32[]{:S(2)}) collective-permute-start(f32[2,96,128]{2,1,0:T(8,128)S(1)} %first_gram.1.refs_0_), channel_id=1, source_target_pairs={{0,1},{1,0},{2,3},{3,2},{4,5},{5,4},{6,7},{7,6},{8,9},{9,8},{10,11... | collective-permute-start | bytes 294920 | tf_op jit(solution)/shard_map/ppermute | solution.py:479
  43.1 2.8 %collective-permute-done.14.refs_3_ = f32[2,96,128]{2,1,0:T(8,128)S(1)} collective-permute-done((f32[2,96,128]{2,1,0:T(8,128)S(1)}, f32[2,96,128]{2,1,0:T(8,128)S(1)}, u32[]{:S(2)}, u32[]{:S(2)}) %collective-permute-start.14) | collective-permute-done | bytes 98336 | tf_op jit(solution)/shard_map/ppermute | solution.py:479
  45.9 2.3 %collective-permute-done.13.refs_2_ = f32[2,96,128]{2,1,0:T(8,128)S(1)} collective-permute-done((f32[2,96,128]{2,1,0:T(8,128)S(1)}, f32[2,96,128]{2,1,0:T(8,128)S(1)}, u32[]{:S(2)}, u32[]{:S(2)}) %collective-permute-start.13) | collective-permute-done | bytes 98336 | tf_op jit(solution)/shard_map/ppermute | solution.py:479
  48.2 0.0 collective-permute-done.12.refs_1_
  48.2 6.2 %first_solve.1.refs_4_ = f32[2,2,128,384]{3,2,1,0:T(8,128)S(1)} custom-call(f32[2,96,128]{2,1,0:T(8,128)S(1)} %first_gram.1.refs_0_, f32[2,96,128]{2,1,0:T(8,128)S(1)} %collective-permute-done.12.refs_1_, f32[2,96,128]{2,1,0:T(8,128)S(1)} %collective-permute-done.13.refs_2_, f32[2,96,128]{2,1,0:T(8,128)S(1)} %collective-permute-done.14.refs_3_, ...), custom_call_target="tpu_custom_call" | custom-call | flops 1000 | bytes 1000 | tf_op jit(solution)/shard_map/first_solve/pallas_call | solution.py:375
  54.4 0.0 collective-permute-done.10.refs_10_.refs_16_
  54.4 6.4 %collective-permute-done.11.refs_11_.refs_17_ = bf16[2,2,16,2048]{3,2,1,0:T(8,128)(2,1)S(1)} collective-permute-done((bf16[2,2,16,2048]{3,2,1,0:T(8,128)(2,1)S(1)}, bf16[2,2,16,2048]{3,2,1,0:T(8,128)(2,1)S(1)}, u32[]{:S(2)}, u32[]{:S(2)}) %collective-permute-start.11) | collective-permute-done | bytes 262176 | tf_op jit(solution)/shard_map/ppermute | solution.py:479
  60.8 0.8 %last_gram.1.refs_0_ = f32[2,64,128]{2,1,0:T(8,128)S(1)} custom-call(bf16[2,2,16,2048]{3,2,1,0:T(8,128)(2,1)S(1)} %get-tuple-element.61.refs_0_.refs_6_, bf16[2,2,16,2048]{3,2,1,0:T(8,128)(2,1)S(1)} %collective-permute-done.5.refs_1_.refs_7_, bf16[2,2,16,1024]{3,2,1,0:T(8,128)(2,1)S(1)} %collective-permute-done.7.refs_2_.refs_8_, ...), custom_call_target="tpu_custom_call" | custom-call | flops 1000 | bytes 1000 | tf_op jit(solution)/shard_map/last_gram/pallas_call | solution.py:241
  61.6 1.3 %collective-permute-start.17 = (f32[2,64,128]{2,1,0:T(8,128)S(1)}, f32[2,64,128]{2,1,0:T(8,128)S(1)}, u32[]{:S(2)}, u32[]{:S(2)}) collective-permute-start(f32[2,64,128]{2,1,0:T(8,128)S(1)} %last_gram.1.refs_0_), channel_id=1, source_target_pairs={{0,3},{1,2},{2,1},{3,0},{4,7},{5,6},{6,5},{7,4},{8,11},{9,10},{10,... | collective-permute-start | bytes 196616 | tf_op jit(solution)/shard_map/ppermute | solution.py:479
  62.8 0.2 collective-permute-start.16
  63.1 1.2 %collective-permute-start.15 = (f32[2,64,128]{2,1,0:T(8,128)S(1)}, f32[2,64,128]{2,1,0:T(8,128)S(1)}, u32[]{:S(2)}, u32[]{:S(2)}) collective-permute-start(f32[2,64,128]{2,1,0:T(8,128)S(1)} %last_gram.1.refs_0_), channel_id=1, source_target_pairs={{0,1},{1,0},{2,3},{3,2},{4,5},{5,4},{6,7},{7,6},{8,9},{9,8},{10,11... | collective-permute-start | bytes 196616 | tf_op jit(solution)/shard_map/ppermute | solution.py:479
  64.3 2.3 %collective-permute-done.17.refs_3_ = f32[2,64,128]{2,1,0:T(8,128)S(1)} collective-permute-done((f32[2,64,128]{2,1,0:T(8,128)S(1)}, f32[2,64,128]{2,1,0:T(8,128)S(1)}, u32[]{:S(2)}, u32[]{:S(2)}) %collective-permute-start.17) | collective-permute-done | bytes 65568 | tf_op jit(solution)/shard_map/ppermute | solution.py:479
  66.5 1.4 %collective-permute-done.16.refs_2_ = f32[2,64,128]{2,1,0:T(8,128)S(1)} collective-permute-done((f32[2,64,128]{2,1,0:T(8,128)S(1)}, f32[2,64,128]{2,1,0:T(8,128)S(1)}, u32[]{:S(2)}, u32[]{:S(2)}) %collective-permute-start.16) | collective-permute-done | bytes 65568 | tf_op jit(solution)/shard_map/ppermute | solution.py:479
  68.0 0.0 collective-permute-done.15.refs_1_
  68.0 5.4 %beams.1 = bf16[2,2,128,2048]{3,2,1,0:T(8,128)(2,1)} custom-call(f32[2,64,128]{2,1,0:T(8,128)S(1)} %last_gram.1.refs_0_, f32[2,64,128]{2,1,0:T(8,128)S(1)} %collective-permute-done.15.refs_1_, f32[2,64,128]{2,1,0:T(8,128)S(1)} %collective-permute-done.16.refs_2_, f32[2,64,128]{2,1,0:T(8,128)S(1)} %collective-permute-done.17.refs_3_, ...), custom_call_target="tpu_custom_call" | custom-call | flops 1000 | bytes 1000 | tf_op jit(solution)/shard_map/beams/pallas_call | solution.py:461
Async XLA Ops:
  0.0 14.2 %copy-start.1 = (s32[128]{0:T(128)S(1)}, s32[128]{0:T(128)}, u32[]{:S(2)}) copy-start(s32[128]{0:T(128)} %param.8) | copy-start | bytes 1540
  0.0 14.2 %copy-start = (f32[2,128]{1,0:T(2,128)S(1)}, f32[2,128]{1,0:T(2,128)}, u32[]{:S(2)}) copy-start(f32[2,128]{1,0:T(2,128)} %refs_4_.1) | copy-start | bytes 3076
  0.9 13.2 %collective-permute-start = (bf16[16,32,128]{2,1,0:T(8,128)(2,1)S(1)}, bf16[16,32,128]{2,1,0:T(8,128)(2,1)S(1)}, u32[]{:S(2)}, u32[]{:S(2)}) collective-permute-start(bf16[16,32,128]{2,1,0:T(8,128)(2,1)S(1)} %slice.3), channel_id=1, source_target_pairs={{0,1},{1,2},{2,3},{4,5},{5,6},{6,7},{8,9},{9,10},{10,11},{12,13},{... | collective-permute-start | bytes 393224 | tf_op jit(solution)/shard_map/ppermute | solution.py:512
  8.9 10.3 %collective-permute-start.1 = (bf16[2,2,16,1024]{3,2,1,0:T(8,128)(2,1)S(1)}, bf16[2,2,16,1024]{3,2,1,0:T(8,128)(2,1)S(1)}, u32[]{:S(2)}, u32[]{:S(2)}) collective-permute-start(bf16[2,2,16,1024]{3,2,1,0:T(8,128)(2,1)S(1)} %get-tuple-element.57), channel_id=1, source_target_pairs={{0,16},{4,20},{8,24},{12,28},{16,0},{20,4},{24,8},{28,12},{1,17},{... | collective-permute-start | bytes 393224 | tf_op jit(solution)/shard_map/ppermute | solution.py:479
  11.3 8.0 %collective-permute-start.2 = (bf16[2,2,16,1024]{3,2,1,0:T(8,128)(2,1)S(1)}, bf16[2,2,16,1024]{3,2,1,0:T(8,128)(2,1)S(1)}, u32[]{:S(2)}, u32[]{:S(2)}) collective-permute-start(bf16[2,2,16,1024]{3,2,1,0:T(8,128)(2,1)S(1)} %get-tuple-element.58), channel_id=1, source_target_pairs={{0,8},{4,12},{8,0},{12,4},{16,24},{20,28},{24,16},{28,20},{1,9},{5... | collective-permute-start | bytes 393224 | tf_op jit(solution)/shard_map/ppermute | solution.py:479
  11.5 11.0 %collective-permute-start.3 = (bf16[2,2,16,1024]{3,2,1,0:T(8,128)(2,1)S(1)}, bf16[2,2,16,1024]{3,2,1,0:T(8,128)(2,1)S(1)}, u32[]{:S(2)}, u32[]{:S(2)}) collective-permute-start(bf16[2,2,16,1024]{3,2,1,0:T(8,128)(2,1)S(1)} %get-tuple-element.59), channel_id=1, source_target_pairs={{0,12},{4,8},{8,4},{12,0},{16,28},{20,24},{24,20},{28,16},{1,13},{... | collective-permute-start | bytes 393224 | tf_op jit(solution)/shard_map/ppermute | solution.py:479
  14.2 9.4 %collective-permute-start.4 = (bf16[2,2,16,1024]{3,2,1,0:T(8,128)(2,1)S(1)}, bf16[2,2,16,1024]{3,2,1,0:T(8,128)(2,1)S(1)}, u32[]{:S(2)}, u32[]{:S(2)}) collective-permute-start(bf16[2,2,16,1024]{3,2,1,0:T(8,128)(2,1)S(1)} %get-tuple-element.60), channel_id=1, source_target_pairs={{0,20},{4,16},{8,28},{12,24},{16,4},{20,0},{24,12},{28,8},{1,21},{... | collective-permute-start | bytes 393224 | tf_op jit(solution)/shard_map/ppermute | solution.py:479
  23.6 7.3 %collective-permute-start.6 = (bf16[2,2,16,1024]{3,2,1,0:T(8,128)(2,1)S(1)}, bf16[2,2,16,1024]{3,2,1,0:T(8,128)(2,1)S(1)}, u32[]{:S(2)}, u32[]{:S(2)}) collective-permute-start(bf16[2,2,16,1024]{3,2,1,0:T(8,128)(2,1)S(1)} %get-tuple-element.64), channel_id=1, source_target_pairs={{0,20},{4,16},{8,28},{12,24},{16,4},{20,0},{24,12},{28,8},{1,21},{... | collective-permute-start | bytes 393224 | tf_op jit(solution)/shard_map/ppermute | solution.py:479
  24.9 6.0 %collective-permute-start.7 = (bf16[2,2,16,1024]{3,2,1,0:T(8,128)(2,1)S(1)}, bf16[2,2,16,1024]{3,2,1,0:T(8,128)(2,1)S(1)}, u32[]{:S(2)}, u32[]{:S(2)}) collective-permute-start(bf16[2,2,16,1024]{3,2,1,0:T(8,128)(2,1)S(1)} %get-tuple-element.65), channel_id=1, source_target_pairs={{0,8},{4,12},{8,0},{12,4},{16,24},{20,28},{24,16},{28,20},{1,9},{5... | collective-permute-start | bytes 393224 | tf_op jit(solution)/shard_map/ppermute | solution.py:479
  25.1 10.8 %collective-permute-start.8 = (bf16[2,2,16,1024]{3,2,1,0:T(8,128)(2,1)S(1)}, bf16[2,2,16,1024]{3,2,1,0:T(8,128)(2,1)S(1)}, u32[]{:S(2)}, u32[]{:S(2)}) collective-permute-start(bf16[2,2,16,1024]{3,2,1,0:T(8,128)(2,1)S(1)} %get-tuple-element.66), channel_id=1, source_target_pairs={{0,12},{4,8},{8,4},{12,0},{16,28},{20,24},{24,20},{28,16},{1,13},{... | collective-permute-start | bytes 393224 | tf_op jit(solution)/shard_map/ppermute | solution.py:479
  27.1 8.8 %collective-permute-start.9 = (bf16[2,2,16,1024]{3,2,1,0:T(8,128)(2,1)S(1)}, bf16[2,2,16,1024]{3,2,1,0:T(8,128)(2,1)S(1)}, u32[]{:S(2)}, u32[]{:S(2)}) collective-permute-start(bf16[2,2,16,1024]{3,2,1,0:T(8,128)(2,1)S(1)} %get-tuple-element.72), channel_id=1, source_target_pairs={{0,16},{4,20},{8,24},{12,28},{16,0},{20,4},{24,8},{28,12},{1,17},{... | collective-permute-start | bytes 393224 | tf_op jit(solution)/shard_map/ppermute | solution.py:479
  28.0 11.7 %collective-permute-start.5 = (bf16[2,2,16,2048]{3,2,1,0:T(8,128)(2,1)S(1)}, bf16[2,2,16,2048]{3,2,1,0:T(8,128)(2,1)S(1)}, u32[]{:S(2)}, u32[]{:S(2)}) collective-permute-start(bf16[2,2,16,2048]{3,2,1,0:T(8,128)(2,1)S(1)} %get-tuple-element.62), channel_id=1, source_target_pairs={{0,4},{4,0},{8,12},{12,8},{16,20},{20,16},{24,28},{28,24},{1,5},{5... | collective-permute-start | bytes 786440 | tf_op jit(solution)/shard_map/ppermute | solution.py:479
  35.9 18.5 %collective-permute-start.10 = (bf16[2,2,16,2048]{3,2,1,0:T(8,128)(2,1)S(1)}, bf16[2,2,16,2048]{3,2,1,0:T(8,128)(2,1)S(1)}, u32[]{:S(2)}, u32[]{:S(2)}) collective-permute-start(bf16[2,2,16,2048]{3,2,1,0:T(8,128)(2,1)S(1)} %get-tuple-element.77), channel_id=1, source_target_pairs={{0,24},{4,28},{8,16},{12,20},{16,8},{20,12},{24,0},{28,4},{1,25},{... | collective-permute-start | bytes 786440 | tf_op jit(solution)/shard_map/ppermute | solution.py:479
  36.9 23.9 %collective-permute-start.11 = (bf16[2,2,16,2048]{3,2,1,0:T(8,128)(2,1)S(1)}, bf16[2,2,16,2048]{3,2,1,0:T(8,128)(2,1)S(1)}, u32[]{:S(2)}, u32[]{:S(2)}) collective-permute-start(bf16[2,2,16,2048]{3,2,1,0:T(8,128)(2,1)S(1)} %get-tuple-element.78), channel_id=1, source_target_pairs={{0,28},{4,24},{8,20},{12,16},{16,12},{20,8},{24,4},{28,0},{1,29},{... | collective-permute-start | bytes 786440 | tf_op jit(solution)/shard_map/ppermute | solution.py:479
  40.4 5.5 %collective-permute-start.14 = (f32[2,96,128]{2,1,0:T(8,128)S(1)}, f32[2,96,128]{2,1,0:T(8,128)S(1)}, u32[]{:S(2)}, u32[]{:S(2)}) collective-permute-start(f32[2,96,128]{2,1,0:T(8,128)S(1)} %first_gram.1.refs_0_), channel_id=1, source_target_pairs={{0,3},{1,2},{2,1},{3,0},{4,7},{5,6},{6,5},{7,4},{8,11},{9,10},{10,... | collective-permute-start | bytes 294920 | tf_op jit(solution)/shard_map/ppermute | solution.py:479
  41.6 6.6 %collective-permute-start.13 = (f32[2,96,128]{2,1,0:T(8,128)S(1)}, f32[2,96,128]{2,1,0:T(8,128)S(1)}, u32[]{:S(2)}, u32[]{:S(2)}) collective-permute-start(f32[2,96,128]{2,1,0:T(8,128)S(1)} %first_gram.1.refs_0_), channel_id=1, source_target_pairs={{0,2},{1,3},{2,0},{3,1},{4,6},{5,7},{6,4},{7,5},{8,10},{9,11},{10,... | collective-permute-start | bytes 294920 | tf_op jit(solution)/shard_map/ppermute | solution.py:479
  41.9 6.3 %collective-permute-start.12 = (f32[2,96,128]{2,1,0:T(8,128)S(1)}, f32[2,96,128]{2,1,0:T(8,128)S(1)}, u32[]{:S(2)}, u32[]{:S(2)}) collective-permute-start(f32[2,96,128]{2,1,0:T(8,128)S(1)} %first_gram.1.refs_0_), channel_id=1, source_target_pairs={{0,1},{1,0},{2,3},{3,2},{4,5},{5,4},{6,7},{7,6},{8,9},{9,8},{10,11... | collective-permute-start | bytes 294920 | tf_op jit(solution)/shard_map/ppermute | solution.py:479
  61.6 5.0 %collective-permute-start.17 = (f32[2,64,128]{2,1,0:T(8,128)S(1)}, f32[2,64,128]{2,1,0:T(8,128)S(1)}, u32[]{:S(2)}, u32[]{:S(2)}) collective-permute-start(f32[2,64,128]{2,1,0:T(8,128)S(1)} %last_gram.1.refs_0_), channel_id=1, source_target_pairs={{0,3},{1,2},{2,1},{3,0},{4,7},{5,6},{6,5},{7,4},{8,11},{9,10},{10,... | collective-permute-start | bytes 196616 | tf_op jit(solution)/shard_map/ppermute | solution.py:479
  62.8 5.1 %collective-permute-start.16 = (f32[2,64,128]{2,1,0:T(8,128)S(1)}, f32[2,64,128]{2,1,0:T(8,128)S(1)}, u32[]{:S(2)}, u32[]{:S(2)}) collective-permute-start(f32[2,64,128]{2,1,0:T(8,128)S(1)} %last_gram.1.refs_0_), channel_id=1, source_target_pairs={{0,2},{1,3},{2,0},{3,1},{4,6},{5,7},{6,4},{7,5},{8,10},{9,11},{10,... | collective-permute-start | bytes 196616 | tf_op jit(solution)/shard_map/ppermute | solution.py:479
  63.1 4.9 %collective-permute-start.15 = (f32[2,64,128]{2,1,0:T(8,128)S(1)}, f32[2,64,128]{2,1,0:T(8,128)S(1)}, u32[]{:S(2)}, u32[]{:S(2)}) collective-permute-start(f32[2,64,128]{2,1,0:T(8,128)S(1)} %last_gram.1.refs_0_), channel_id=1, source_target_pairs={{0,1},{1,0},{2,3},{3,2},{4,5},{5,4},{6,7},{7,6},{8,9},{9,8},{10,11... | collective-permute-start | bytes 196616 | tf_op jit(solution)/shard_map/ppermute | solution.py:479
